TPU v7x, 512 devices: a whole 4x4x16 slice. The times are simulated.
512 devices in a mesh: dp: 16 (over x, z_hi, core), expert: 32 (over z_lo, y).
Axes of the slice: x: 4, y: 4, z: 16 (z_hi: 2, z_lo: 8; z = z_hi * 8 + z_lo), core: 2. Of those that a mesh axis runs over, the one named last changes fastest.
Arguments:
- stash: bfloat16 [512, 5120], P('dp', 'expert'), may hold values from -6 to 6
- scale_exp: int32 [512, 160], P('dp', 'expert'), may hold values from -2 to 1
- grad_out: bfloat16 [512, 5120], P('dp', 'expert'), may hold values from -6 to 6
- route_ids: int32 [512, 6], P('dp'), may hold values from 0 to 15, all different within a row; in each aligned block of 16 rows (0 to 15, 16 to 31, ...) at most 8 rows name the same one
- route_probs: bfloat16 [512, 6], P('dp'), may hold values from 0.049804688 to 0.5
- w_gate: bfloat16 [16, 7864320], P(None, ('dp', 'expert')), may hold values from -0.078125 to 0.078125
- w_up: bfloat16 [16, 7864320], P(None, ('dp', 'expert')), may hold values from -0.078125 to 0.078125
- w_down: bfloat16 [16, 7864320], P(None, ('dp', 'expert')), may hold values from -0.15625 to 0.15625
Outputs:
- grad_in: bfloat16 [512, 5120], P('dp', 'expert')
- grad_probs: float32 [512, 6], P('dp')
- grad_gate: bfloat16 [16, 7864320], P(None, ('dp', 'expert'))
- grad_up: bfloat16 [16, 7864320], P(None, ('dp', 'expert'))
- grad_down: bfloat16 [16, 7864320], P(None, ('dp', 'expert'))
Inputs may be any that keep to these rules, and one draw needn't show every extreme that they name: `route_ids`: each row names 6 different experts; within each aligned block of 16 rows (the blocks of one shard in order) no expert is named by more than 8 rows, a bound that some block reaches.
All inputs are finite; a program needn't handle non-finite values.
Results may differ from a plain program's by a relative error of at most 0.022.
Values may be sent and summed in bfloat16 or wider, within the bound.
No kernel may reach another device: no remote copies, remote signals or barrier semaphores. Data moves between devices by JAX's collectives and lax.ppermute only.
A program may use at most 64 MiB of HBM per device.

v0:
```python
import jax
import jax.numpy as jnp
from jax import lax
from jax.sharding import PartitionSpec as P

D = 5120


scale_cols = 32


def route_tables(route_ids, route_probs, repl, experts, cap):
    tok_dp, top = route_ids.shape
    blk = tok_dp // repl
    ids_blocks = route_ids.reshape(repl, blk, top)
    probs_blocks = route_probs.astype(jnp.float32).reshape(repl, blk, top)
    expert_ids = lax.iota(jnp.int32, experts)
    match = ids_blocks[:, None, :, :] == expert_ids[None, :, None, None]
    hit = jnp.any(match, axis=3)
    position = jnp.cumsum(hit.astype(jnp.int32), axis=2) - 1
    slot_ids = lax.iota(jnp.int32, cap)
    onehot = hit[:, :, None, :] & (position[:, :, None, :] == slot_ids[None, None, :, None])
    weight = jnp.sum(jnp.where(match, probs_blocks[:, None, :, :], 0.0), axis=3)
    return (onehot.astype(jnp.bfloat16), match, weight)


def pick_own(table, part, expert_id):
    inner = lax.dynamic_index_in_dim(table, part, 0, False)
    return lax.dynamic_index_in_dim(inner, expert_id, 0, False)


def local(stash, scale_exp, grad_out, route_ids, route_probs, w_gate, w_up, w_down):
    n_exp = lax.axis_size("expert")
    experts = w_gate.shape[0]
    tile_len = w_gate.shape[1]
    repl = n_exp // experts
    tok_dp, top = route_ids.shape
    blk = tok_dp // repl
    cap = blk * top * 4 // (experts * 3)
    hid_cols = tile_len * n_exp // D
    column = lax.axis_index("expert")
    expert_id = column % experts
    part = column // experts
    factors = jnp.repeat(jnp.exp2(scale_exp.astype(jnp.float32)), scale_cols, axis=1)
    x_local = (stash.astype(jnp.float32) * factors).astype(jnp.bfloat16)
    onehot, match, weight = route_tables(route_ids, route_probs, repl, experts, cap)
    own_onehot = pick_own(onehot, part, expert_id)
    own_match = pick_own(match, part, expert_id)
    own_weight = pick_own(weight, part, expert_id)
    own_float = own_onehot.astype(jnp.float32)
    slot_gate = jnp.dot(own_float, own_weight, precision=lax.Precision.HIGHEST).astype(jnp.bfloat16)
    full_x, full_dy = (
        lax.all_gather(x_local, "expert", axis=1, tiled=True),
        lax.all_gather(grad_out, "expert", axis=1, tiled=True),
    )
    block_x = lax.dynamic_slice_in_dim(full_x, part * blk, blk, 0)
    block_dy = lax.dynamic_slice_in_dim(full_dy, part * blk, blk, 0)
    sel_x = jnp.dot(own_onehot, block_x, preferred_element_type=jnp.float32).astype(jnp.bfloat16)
    sel_dy = jnp.dot(own_onehot, block_dy, preferred_element_type=jnp.float32).astype(jnp.bfloat16)
    gate_w, up_w, down_w = (
        lax.all_to_all(
            jnp.tile(w_gate, (repl, 1)), "expert", split_axis=0, concat_axis=1, tiled=True
        ),
        lax.all_to_all(
            jnp.tile(w_up, (repl, 1)), "expert", split_axis=0, concat_axis=1, tiled=True
        ),
        lax.all_to_all(
            jnp.tile(w_down, (repl, 1)), "expert", split_axis=0, concat_axis=1, tiled=True
        ),
    )
    gate_w = gate_w.reshape(D, hid_cols)
    up_w = up_w.reshape(D, hid_cols)
    down_w = down_w.reshape(D, hid_cols)
    rows_x, rows_dy, rows_gate = (
        lax.all_gather(sel_x, "dp", axis=0, tiled=True),
        lax.all_gather(sel_dy, "dp", axis=0, tiled=True),
        lax.all_gather(slot_gate, "dp", axis=0, tiled=True),
    )
    pre_a = jnp.dot(rows_x, gate_w, preferred_element_type=jnp.float32)
    pre_b = jnp.dot(rows_x, up_w, preferred_element_type=jnp.float32)
    back = jnp.dot(rows_dy, down_w, preferred_element_type=jnp.float32)
    sig = jax.nn.sigmoid(pre_a)
    act = pre_a * sig
    hidden = act * pre_b
    gate = rows_gate.astype(jnp.float32)[:, None]
    dh = gate * back
    d_gate = (dh * pre_b * sig * (1.0 + pre_a * (1.0 - sig))).astype(jnp.bfloat16)
    d_up = (dh * act).astype(jnp.bfloat16)
    gated = (gate * hidden).astype(jnp.bfloat16)
    prob_part = jnp.sum(hidden * back, axis=1)
    right = (((1,), (1,)), ((), ()))
    dx_part = lax.dot_general(d_gate, gate_w, right, preferred_element_type=jnp.float32)
    dx_part = dx_part + lax.dot_general(d_up, up_w, right, preferred_element_type=jnp.float32)
    over_rows = (((0,), (0,)), ((), ()))
    grad_g = lax.dot_general(rows_x, d_gate, over_rows, preferred_element_type=jnp.float32)
    grad_u = lax.dot_general(rows_x, d_up, over_rows, preferred_element_type=jnp.float32)
    grad_d = lax.dot_general(rows_dy, gated, over_rows, preferred_element_type=jnp.float32)
    back_x, back_p = (
        lax.psum_scatter(
            dx_part.astype(jnp.bfloat16), "dp", scatter_dimension=0, tiled=True
        ).astype(jnp.float32),
        lax.psum_scatter(
            prob_part.astype(jnp.bfloat16), "dp", scatter_dimension=0, tiled=True
        ).astype(jnp.float32),
    )
    width = back_x.shape[1]
    token_x = jnp.dot(own_float.T, back_x, precision=lax.Precision.HIGHEST)
    token_p = jnp.dot(own_float.T, back_p, precision=lax.Precision.HIGHEST)
    slot_p = jnp.where(own_match, token_p[:, None], 0.0)
    full_buf = lax.dynamic_update_slice_in_dim(
        jnp.zeros((tok_dp, width), jnp.float32), token_x, part * blk, 0
    )
    prob_buf = lax.dynamic_update_slice_in_dim(
        jnp.zeros((tok_dp, top), jnp.float32), slot_p, part * blk, 0
    )
    grad_in = lax.psum_scatter(
        full_buf.astype(jnp.bfloat16), "expert", scatter_dimension=1, tiled=True
    )
    grad_probs = lax.psum(prob_buf, "expert")
    flat_len = D * hid_cols
    ret_g, ret_u, ret_d = (
        lax.all_to_all(
            grad_g.astype(jnp.bfloat16).reshape(1, flat_len),
            "expert",
            split_axis=1,
            concat_axis=0,
            tiled=True,
        ),
        lax.all_to_all(
            grad_u.astype(jnp.bfloat16).reshape(1, flat_len),
            "expert",
            split_axis=1,
            concat_axis=0,
            tiled=True,
        ),
        lax.all_to_all(
            grad_d.astype(jnp.bfloat16).reshape(1, flat_len),
            "expert",
            split_axis=1,
            concat_axis=0,
            tiled=True,
        ),
    )

    def fold_parts(piece):
        return jnp.sum(piece.astype(jnp.float32).reshape(repl, experts, tile_len), axis=0).astype(
            jnp.bfloat16
        )

    return (grad_in, grad_probs, fold_parts(ret_g), fold_parts(ret_u), fold_parts(ret_d))


def solution(mesh):
    in_specs = (
        P("dp", "expert"),
        P("dp", "expert"),
        P("dp", "expert"),
        P("dp", None),
        P("dp", None),
        P(None, ("dp", "expert")),
        P(None, ("dp", "expert")),
        P(None, ("dp", "expert")),
    )
    out_specs = (
        P("dp", "expert"),
        P("dp", None),
        P(None, ("dp", "expert")),
        P(None, ("dp", "expert")),
        P(None, ("dp", "expert")),
    )
    return jax.shard_map(local, mesh=mesh, in_specs=in_specs, out_specs=out_specs, check_vma=False)
```

profile of v0, /device:TPU:2, one launch (start us, length us, event | category | flops | bytes accessed | tf_op | source)
XLA Modules:
  0.0 1011.9 jit_solution(7265799141665734204)
XLA Ops:
  7.2 1.1 tile.7
  8.8 1.4 reduce.6
  10.2 1.7 reshape.134
  11.9 15.7 %all-to-all-start.1 = ((bf16[32,2,7680]{2,1,0:T(2,128)(2,1)}), bf16[32,2,7680]{2,1,0:T(2,128)(2,1)S(1)}, u32[]{:S(2)}, u32[]{:S(2)}) async-start(bf16[32,2,7680]{2,1,0:T(2,128)(2,1)} %reshape.134), calls=%async_computation.1 | async-start | bytes 1966080 | tf_op jit(solution)/shard_map/all_to_all | solution.py:64
  27.7 1.4 reduce.7
  29.0 1.7 reshape.132
  30.7 46.0 %all-to-all-done.1 = bf16[32,2,7680]{2,1,0:T(2,128)(2,1)S(1)} async-done(((bf16[32,2,7680]{2,1,0:T(2,128)(2,1)}), bf16[32,2,7680]{2,1,0:T(2,128)(2,1)S(1)}, u32[]{:S(2)}, u32[]{:S(2)}) %all-to-all-start.1) | async-done | bytes 983072 | tf_op jit(solution)/shard_map/all_to_all | solution.py:64
  76.8 6.2 all-to-all-start.2
  83.8 129.9 %all-gather.1 = bf16[32,160,32]{1,2,0:T(8,128)(2,1)S(1)} all-gather(bf16[1,160,32]{1,2,0:T(8,128)(2,1)S(1)} %copy.41), channel_id=1, replica_groups=mesh['dp'=16,'expert'=32] {'expert'}, dimensions={0}, use_global_device_ids=true | all-gather | bytes 337920 | tf_op jit(solution)/shard_map/all_gather | solution.py:53
  214.0 0.7 reshape.119
  214.8 0.8 convolution_convert_fusion.3
  215.6 2.1 tile.6
  217.7 2.6 reduce.8
  220.3 1.7 reshape.136
  222.0 4.8 all-to-all-start
  226.8 132.6 %all-gather = bf16[32,160,32]{1,2,0:T(8,128)(2,1)S(1)} all-gather(bf16[1,160,32]{1,2,0:T(8,128)(2,1)S(1)} %bitcast.91), channel_id=1, replica_groups=mesh['dp'=16,'expert'=32] {'expert'}, dimensions={0}, use_global_device_ids=true | all-gather | bytes 337920 | tf_op jit(solution)/shard_map/all_gather | solution.py:54
  359.7 0.7 reshape.117
  360.5 0.8 convolution_convert_fusion.4
  363.1 0.8 reshape.135
  363.9 6.0 reduce.4
  369.9 1.3 reshape.110
  371.2 4.4 reshape.133
  375.6 6.9 reduce.5
  382.5 3.2 reshape.111
  385.7 4.6 reshape.137
  390.3 6.9 reduce.3
  397.2 3.2 reshape.108
  400.4 2.1 fusion.33
  403.2 31.4 %all-gather.5.cloned.1.call-done = bf16[128,5120]{1,0:T(8,128)(2,1)} async-done(((bf16[8,5120]{1,0:T(8,128)(2,1)}), bf16[128,5120]{1,0:T(8,128)(2,1)}) %all-gather.5.cloned.1.call-update) | async-done | bytes 1310736 | tf_op jit(solution)/shard_map/all_gather | solution.py:76
  434.6 2.4 multiply_reduce_fusion
  437.0 57.6 %all-reduce.2 = (bf16[128]{0:T(256)(128)(2,1)S(1)}, bf16[128]{0:T(256)(128)(2,1)S(1)}) all-reduce(bf16[128]{0:T(256)(128)(2,1)S(1)} %dynamic-update-slice, bf16[128]{0:T(256)(128)(2,1)S(1)} %get-tuple-element.13), channel_id=1, replica_groups=mesh['dp'=16,'expert'=32] {'dp'}, use_global_device_ids=true, to_apply=%add | all-reduce | flops 256 | bytes 1024
  494.6 2.7 convolution_convert_fusion
  497.3 2.4 copy.49
  499.7 6.3 all_to_all.83
  506.0 8.6 reduce.11
  514.6 3.7 reshape.142
  518.3 11.7 %all-to-all-start.5 = ((bf16[32,2,7680]{2,1,0:T(2,128)(2,1)}), bf16[32,2,7680]{2,1,0:T(2,128)(2,1)}, u32[]{:S(2)}, u32[]{:S(2)}) async-start(bf16[32,2,7680]{2,1,0:T(2,128)(2,1)} %reshape.142), calls=%async_computation.6 | async-start | bytes 1966080 | tf_op jit(solution)/shard_map/all_to_all | solution.py:136
  530.0 1.4 convolution_convert_fusion.2
  531.4 2.4 copy.45
  533.8 6.3 all_to_all.81
  540.1 8.6 reduce.9
  548.7 3.7 reshape.138
  552.4 20.3 %all-to-all-done.5 = bf16[32,2,7680]{2,1,0:T(2,128)(2,1)} async-done(((bf16[32,2,7680]{2,1,0:T(2,128)(2,1)}), bf16[32,2,7680]{2,1,0:T(2,128)(2,1)}, u32[]{:S(2)}, u32[]{:S(2)}) %all-to-all-start.5) | async-done | bytes 983072 | tf_op jit(solution)/shard_map/all_to_all | solution.py:136
  572.7 6.5 all-to-all-start.3
  579.2 1.4 convolution_convert_fusion.1
  580.6 2.4 copy.47
  583.0 5.0 all_to_all.82
  588.0 7.6 reduce.10
  595.5 3.7 reshape.140
  599.2 27.8 %all-to-all-done.3 = bf16[32,2,7680]{2,1,0:T(2,128)(2,1)} async-done(((bf16[32,2,7680]{2,1,0:T(2,128)(2,1)}), bf16[32,2,7680]{2,1,0:T(2,128)(2,1)}, u32[]{:S(2)}, u32[]{:S(2)}) %all-to-all-start.3) | async-done | bytes 983072 | tf_op jit(solution)/shard_map/all_to_all | solution.py:122
  627.0 6.3 all-to-all-start.4
  633.9 1.6 fusion
  635.6 116.2 %reduce-scatter.5.cloned.1.call-done = bf16[8,5120]{1,0:T(8,128)(2,1)} async-done(((bf16[128,5120]{1,0:T(8,128)(2,1)}), bf16[8,5120]{1,0:T(8,128)(2,1)}) %reduce-scatter.5.cloned.1.call-update) | async-done | bytes 81936 | tf_op jit(solution)/shard_map/reduce_scatter | solution.py:99
  751.8 1.1 convolution_dynamic-update-slice_fusion
  752.9 1.4 copy.51
  755.3 115.2 %psum.7 = f32[32,6]{0,1:T(8,128)} all-reduce(f32[32,6]{0,1:T(8,128)S(1)} %dynamic_update_slice.7), channel_id=1, replica_groups=mesh['dp'=16,'expert'=32] {'expert'}, use_global_device_ids=true, to_apply=%region_7.8 | all-reduce | flops 192 | bytes 1536 | tf_op jit(solution)/shard_map/psum | solution.py:119
  870.5 116.2 %reduce-scatter.7.cloned.1.call-done = bf16[160,32]{1,0:T(8,128)(2,1)} async-done(((bf16[5120,32]{1,0:T(8,128)(2,1)}), bf16[160,32]{1,0:T(8,128)(2,1)}) %reduce-scatter.7.cloned.1.call-update) | async-done | bytes 10256
  986.7 1.5 copy.52
  988.2 4.1 reshape.143
  992.7 1.1 reduce_sum.58
  993.7 4.1 reshape.139
  998.2 1.1 reduce_sum.56
  999.3 4.1 reshape.141
  1003.8 1.1 reduce_sum.57
  (69 shorter events, 5.9 us)
Async XLA Ops:
  11.9 15.7 %copy-start.4 = (bf16[16,15360]{1,0:T(8,128)(2,1)S(1)}, bf16[16,15360]{1,0:T(8,128)(2,1)}, u32[]{:S(2)}) copy-start(bf16[16,15360]{1,0:T(8,128)(2,1)} %param.13) | copy-start | bytes 1474564
  11.9 64.9 %all-to-all-start.1 = ((bf16[32,2,7680]{2,1,0:T(2,128)(2,1)}), bf16[32,2,7680]{2,1,0:T(2,128)(2,1)S(1)}, u32[]{:S(2)}, u32[]{:S(2)}) async-start(bf16[32,2,7680]{2,1,0:T(2,128)(2,1)} %reshape.134), calls=%async_computation.1 | async-start | bytes 1966080 | tf_op jit(solution)/shard_map/all_to_all | solution.py:64
  30.7 52.3 %copy-start.7 = (s32[32,6]{0,1:T(8,128)S(1)}, s32[32,6]{0,1:T(8,128)}, u32[]{:S(2)}) copy-start(s32[32,6]{0,1:T(8,128)} %param.11) | copy-start | bytes 2308
  30.7 52.8 %copy-start.5 = (bf16[32,160]{1,0:T(8,128)(2,1)S(1)}, bf16[32,160]{1,0:T(8,128)(2,1)}, u32[]{:S(2)}) copy-start(bf16[32,160]{1,0:T(8,128)(2,1)} %param.8) | copy-start | bytes 30724
  30.7 53.0 %copy-start.8 = (s32[32,5]{0,1:T(8,128)S(1)}, s32[32,5]{0,1:T(8,128)}, u32[]{:S(2)}) copy-start(s32[32,5]{0,1:T(8,128)} %param.9) | copy-start | bytes 1924
  76.8 145.2 %all-to-all-start.2 = ((bf16[32,2,7680]{2,1,0:T(2,128)(2,1)}), bf16[32,2,7680]{2,1,0:T(2,128)(2,1)S(1)}, u32[]{:S(2)}, u32[]{:S(2)}) async-start(bf16[32,2,7680]{2,1,0:T(2,128)(2,1)} %reshape.132), calls=%async_computation.2 | async-start | bytes 1966080 | tf_op jit(solution)/shard_map/all_to_all | solution.py:61
  83.0 317.5 %all-gather.7.cloned.1.call-start = ((), (), s32[]{:S(2)}) async-start(), calls=%async_computation.9 | async-start | bytes 1392640 | tf_op jit(solution)/shard_map/all_gather | solution.py:75
  221.9 4.8 copy-start.6
  222.0 137.8 %copy-start.3 = (bf16[32,2,7680]{2,1,0:T(2,128)(2,1)}, bf16[32,2,7680]{2,1,0:T(2,128)(2,1)S(1)}, u32[]{:S(2)}) copy-start(bf16[32,2,7680]{2,1,0:T(2,128)(2,1)S(1)} %all-to-all-done.2) | copy-start | bytes 2949124
  222.0 163.7 %all-to-all-start = ((bf16[32,2,7680]{2,1,0:T(2,128)(2,1)}), bf16[32,2,7680]{2,1,0:T(2,128)(2,1)}, u32[]{:S(2)}, u32[]{:S(2)}) async-start(bf16[32,2,7680]{2,1,0:T(2,128)(2,1)} %reshape.136), calls=%async_computation | async-start | bytes 1966080 | tf_op jit(solution)/shard_map/all_to_all | solution.py:67
  226.7 207.9 %all-gather.5.cloned.1.call-start = ((), (), s32[]{:S(2)}) async-start(), calls=%async_computation.8 | async-start | bytes 1392640 | tf_op jit(solution)/shard_map/all_gather | solution.py:76
  226.8 134.5 %copy-start.9 = (bf16[32,6]{0,1:T(8,128)(2,1)S(1)}, bf16[32,6]{0,1:T(8,128)(2,1)}, u32[]{:S(2)}) copy-start(bf16[32,6]{0,1:T(8,128)(2,1)} %param.12) | copy-start | bytes 1156
  226.8 134.6 %copy-start.10 = (u32[512]{0:T(512)S(1)}, u32[512]{0:T(512)}, u32[]{:S(2)}) copy-start(u32[512]{0:T(512)} %constant.136) | copy-start | bytes 6148
  400.4 2.1 copy-start
  400.4 2.1 copy-start.1
  518.3 54.4 %all-to-all-start.5 = ((bf16[32,2,7680]{2,1,0:T(2,128)(2,1)}), bf16[32,2,7680]{2,1,0:T(2,128)(2,1)}, u32[]{:S(2)}, u32[]{:S(2)}) async-start(bf16[32,2,7680]{2,1,0:T(2,128)(2,1)} %reshape.142), calls=%async_computation.6 | async-start | bytes 1966080 | tf_op jit(solution)/shard_map/all_to_all | solution.py:136
  572.7 54.3 %all-to-all-start.3 = ((bf16[32,2,7680]{2,1,0:T(2,128)(2,1)}), bf16[32,2,7680]{2,1,0:T(2,128)(2,1)}, u32[]{:S(2)}, u32[]{:S(2)}) async-start(bf16[32,2,7680]{2,1,0:T(2,128)(2,1)} %reshape.138), calls=%async_computation.4 | async-start | bytes 1966080 | tf_op jit(solution)/shard_map/all_to_all | solution.py:122
  599.2 34.1 %copy-start.2 = (bf16[5120,96]{1,0:T(8,128)(2,1)S(1)}, bf16[5120,96]{1,0:T(8,128)(2,1)}, u32[]{:S(2)}) copy-start(bf16[5120,96]{1,0:T(8,128)(2,1)} %reshape.111) | copy-start | bytes 2949124
  627.0 372.3 %all-to-all-start.4 = ((bf16[32,2,7680]{2,1,0:T(2,128)(2,1)}), bf16[32,2,7680]{2,1,0:T(2,128)(2,1)}, u32[]{:S(2)}, u32[]{:S(2)}) async-start(bf16[32,2,7680]{2,1,0:T(2,128)(2,1)} %reshape.140), calls=%async_computation.5 | async-start | bytes 1966080 | tf_op jit(solution)/shard_map/all_to_all | solution.py:129
  633.3 118.5 %reduce-scatter.5.cloned.1.call-start = ((), (), s32[]{:S(2)}) async-start(), calls=%async_computation.10 | async-start | bytes 1392640 | tf_op jit(solution)/shard_map/reduce_scatter | solution.py:99
  635.5 351.2 %reduce-scatter.7.cloned.1.call-start = ((), (), s32[]{:S(2)}) async-start(), calls=%async_computation.11 | async-start | bytes 1351680
Sparse Core Ops, SparseCore 0:
  215.7 83.8 all-gather.6
  361.4 73.1 all-gather.4
  638.8 112.8 reduce-scatter.4
  754.5 232.2 reduce-scatter.6
where the time goes:
time: 1020 us; the launch traced here: 1010 us
  blocking collectives  435 us (43%)
  waiting for transfers between devices  358 us (35%)
  local copies, waits for them, and re-layouts  81.8 us (8%)
  other arithmetic  53.8 us (5%)
  starting transfers between devices  51.4 us (5%)
  between operations  16 us (2%)
  matrix products  15.8 us (2%)
    all_gather x1, blocking collectives, local(): lax.all_gather(grad_out, 'expert', axis=1, tiled=True)  133 us
    all_gather x1, blocking collectives, local(): lax.all_gather(x_local, 'expert', axis=1, tiled=True)  130 us
    unnamed x5, waiting for transfers between devices  116 us
    reduce_scatter x1, waiting for transfers between devices, local(): lax.psum_scatter(dx_part.astype(jnp.bfloat16), 'dp', scatter_dimension=0,...  116 us
    psum x1, blocking collectives, local(): grad_probs = lax.psum(prob_buf, 'expert')  115 us
    unnamed x1, blocking collectives  57.6 us
    all_to_all x1, waiting for transfers between devices, local(): lax.all_to_all(jnp.tile(w_up, (repl, 1)), 'expert', split_axis=0, concat_...  46 us
    unnamed x46, local copies, waits for them, and re-layouts  44.8 us
  transfers between devices with their start and end apart: 10, of which 6 were waited for; matrix products, arithmetic and copies ran while one was open for 10% of the time, Pallas kernels for 0%

commit v1 on v0

v1 whole, which is shorter than its diff:
```python
import jax
import jax.numpy as jnp
from jax import lax
from jax.experimental import pallas as pl
from jax.experimental.pallas import tpu as pltpu
from jax.sharding import Mesh, PartitionSpec as P

DP = ("x", "zh", "core")
EX = ("zl", "y")
BLK = 16
TOP = 6
EXPERTS = 16
DSH = 160
FSH = 96
TOKENS = 512
BLOCKS = TOKENS // BLK
ROWS = BLK * TOP
LANES = 128
PACK = TOP * 3 * FSH
COLS = 384
IDS_AT = 2 * DSH
PROBS_AT = IDS_AT + TOP
OUT_COLS = 256
VMEM = 56 * 1024 * 1024


def build_pick(xin_ref, pick_ref):
    ids = xin_ref[:, IDS_AT:IDS_AT + TOP].astype(jnp.float32).astype(jnp.int32)
    token = lax.broadcasted_iota(jnp.int32, (TOKENS, 1), 0) % BLK
    column = lax.broadcasted_iota(jnp.int32, (TOKENS, EXPERTS * BLK), 1)
    for k in range(TOP):
        hot = column == ids[:, k:k + 1] * BLK + token
        hot = jnp.where(hot, 1.0, 0.0).astype(jnp.bfloat16)
        pick_ref[:, k * BLK:(k + 1) * BLK, :] = hot.reshape(BLOCKS, BLK, EXPERTS * BLK)


def forward_kernel(xin_ref, wg_ref, wu_ref, wd_ref, out_ref, pick_ref, dense_ref, rows_ref):
    build_pick(xin_ref, pick_ref)
    x = xin_ref[:, :DSH]
    dy = xin_ref[:, DSH:2 * DSH]

    def expert(e, _):
        at = pl.ds(pl.multiple_of(e * BLK, BLK), BLK)
        for i, (rows, w_ref) in enumerate(((x, wg_ref), (x, wu_ref), (dy, wd_ref))):
            part = jnp.dot(rows, w_ref[e], preferred_element_type=jnp.float32)
            part = part.astype(jnp.bfloat16).reshape(BLOCKS, BLK, FSH)
            dense_ref[:, at, i * LANES:i * LANES + FSH] = part
        return 0

    lax.fori_loop(0, EXPERTS, expert, 0)

    def block(b, _):
        picked = jnp.dot(pick_ref[b], dense_ref[b], preferred_element_type=jnp.float32)
        for k in range(TOP):
            rows_ref[k, pl.ds(pl.multiple_of(b * BLK, BLK), BLK), :] = picked[k * BLK:(k + 1) * BLK]
        return 0

    lax.fori_loop(0, BLOCKS, block, 0, unroll=4)

    def pack(c, _):
        at = pl.ds(pl.multiple_of(c * 64, 64), 64)
        pieces = []
        for k in range(TOP):
            for i in range(3):
                pieces.append(rows_ref[k, at, i * LANES:i * LANES + FSH])
        out_ref[at, :] = jnp.concatenate(pieces, axis=1).astype(jnp.bfloat16)
        return 0

    lax.fori_loop(0, TOKENS // 64, pack, 0)


def backward_kernel(xin_ref, xt_ref, pre_ref, wg_ref, wu_ref, gg_ref, gu_ref, gd_ref, dx_ref,
                    pick_ref, grow_ref, dense_ref, acc_ref):
    build_pick(xin_ref, pick_ref)
    step = 64

    def act(c, _):
        at = pl.ds(pl.multiple_of(c * step, step), step)
        blocks = pl.ds(pl.multiple_of(c * (step // BLK), step // BLK), step // BLK)
        pre = pre_ref[at, :].astype(jnp.float32)
        probs = xin_ref[at, PROBS_AT:PROBS_AT + TOP].astype(jnp.float32)
        sums = []
        for k in range(TOP):
            base = k * 3 * FSH
            a = pre[:, base:base + FSH]
            b = pre[:, base + FSH:base + 2 * FSH]
            back = pre[:, base + 2 * FSH:base + 3 * FSH]
            gate = probs[:, k:k + 1]
            sig = jax.nn.sigmoid(a)
            act_ = a * sig
            hidden = act_ * b
            dh = gate * back
            d_gate = dh * b * sig * (1.0 + a * (1.0 - sig))
            d_up = dh * act_
            gated = gate * hidden
            for i, value in enumerate((d_gate, d_up, gated)):
                value = value.astype(jnp.bfloat16).reshape(step // BLK, BLK, FSH)
                grow_ref[blocks, k * BLK:(k + 1) * BLK, i * LANES:i * LANES + FSH] = value
            sums.append(jnp.sum(hidden * back, axis=1, keepdims=True))
        lane = lax.broadcasted_iota(jnp.int32, (step, LANES), 1)
        tail = jnp.zeros((step, LANES), jnp.float32)
        for k in range(TOP):
            tail = jnp.where(lane == k, sums[k], tail)
        acc_ref[at, OUT_COLS:OUT_COLS + LANES] = tail
        return 0

    lax.fori_loop(0, TOKENS // step, act, 0)

    def block(b, _):
        spread = lax.dot_general(pick_ref[b], grow_ref[b], (((0,), (0,)), ((), ())),
                                 preferred_element_type=jnp.float32)
        dense_ref[b] = spread.astype(jnp.bfloat16)
        return 0

    lax.fori_loop(0, BLOCKS, block, 0, unroll=4)
    acc_ref[:, :OUT_COLS] = jnp.zeros((TOKENS, OUT_COLS), jnp.float32)
    right = (((1,), (1,)), ((), ()))

    def expert(e, _):
        at = pl.ds(pl.multiple_of(e * BLK, BLK), BLK)
        d_gate = dense_ref[:, at, 0:FSH].reshape(TOKENS, FSH)
        d_up = dense_ref[:, at, LANES:LANES + FSH].reshape(TOKENS, FSH)
        gated = dense_ref[:, at, 2 * LANES:2 * LANES + FSH].reshape(TOKENS, FSH)
        xt = xt_ref[:DSH, :]
        dyt = xt_ref[DSH:2 * DSH, :]
        gg_ref[e] = jnp.dot(xt, d_gate, preferred_element_type=jnp.float32).astype(jnp.bfloat16)
        gu_ref[e] = jnp.dot(xt, d_up, preferred_element_type=jnp.float32).astype(jnp.bfloat16)
        gd_ref[e] = jnp.dot(dyt, gated, preferred_element_type=jnp.float32).astype(jnp.bfloat16)
        dx = lax.dot_general(d_gate, wg_ref[e], right, preferred_element_type=jnp.float32)
        dx = dx + lax.dot_general(d_up, wu_ref[e], right, preferred_element_type=jnp.float32)
        acc_ref[:, :DSH] += dx
        return 0

    lax.fori_loop(0, EXPERTS, expert, 0)
    dx_ref[:, :OUT_COLS] = acc_ref[:, :OUT_COLS].astype(jnp.bfloat16)
    dx_ref[:, OUT_COLS:] = acc_ref[:, OUT_COLS:].astype(jnp.bfloat16)


def vmem_spec():
    return pl.BlockSpec(memory_space=pltpu.VMEM)


def forward(xin, wg, wu, wd):
    return pl.pallas_call(
        forward_kernel,
        out_shape=jax.ShapeDtypeStruct((TOKENS, PACK), jnp.bfloat16),
        in_specs=[vmem_spec()] * 4,
        out_specs=vmem_spec(),
        scratch_shapes=[
            pltpu.VMEM((BLOCKS, ROWS, EXPERTS * BLK), jnp.bfloat16),
            pltpu.VMEM((BLOCKS, EXPERTS * BLK, COLS), jnp.bfloat16),
            pltpu.VMEM((TOP, TOKENS, COLS), jnp.float32),
        ],
        compiler_params=pltpu.CompilerParams(vmem_limit_bytes=VMEM),
    )(xin, wg, wu, wd)


def backward(xin, xt, pre, wg, wu):
    weight = jax.ShapeDtypeStruct((EXPERTS, DSH, FSH), jnp.bfloat16)
    return pl.pallas_call(
        backward_kernel,
        out_shape=[weight] * 3 + [jax.ShapeDtypeStruct((TOKENS, OUT_COLS + LANES), jnp.bfloat16)],
        in_specs=[vmem_spec()] * 5,
        out_specs=[vmem_spec()] * 4,
        scratch_shapes=[
            pltpu.VMEM((BLOCKS, ROWS, EXPERTS * BLK), jnp.bfloat16),
            pltpu.VMEM((BLOCKS, ROWS, COLS), jnp.bfloat16),
            pltpu.VMEM((BLOCKS, EXPERTS * BLK, COLS), jnp.bfloat16),
            pltpu.VMEM((TOKENS, OUT_COLS + LANES), jnp.float32),
        ],
        compiler_params=pltpu.CompilerParams(vmem_limit_bytes=VMEM),
    )(xin, xt, pre, wg, wu)


def exchange(value, axis):
    return lax.all_to_all(value, axis, split_axis=0, concat_axis=0, tiled=True)


def swap(value, axis):
    return lax.ppermute(value, axis, [(0, 1), (1, 0)])


def local(stash, scale_exp, grad_out, route_ids, route_probs, w_gate, w_up, w_down):
    bf16, f32 = jnp.bfloat16, jnp.float32
    factors = jnp.repeat(jnp.exp2(scale_exp.astype(f32)), DSH // scale_exp.shape[1], axis=1)
    x_local = (stash.astype(f32) * factors).astype(bf16)
    tok = stash.shape[0]
    pad = jnp.zeros((tok, COLS - PROBS_AT - TOP), bf16)
    xin = jnp.concatenate([x_local, grad_out, route_ids.astype(bf16), route_probs, pad], axis=1)
    with jax.named_scope("gather_tokens"):
        xin = lax.all_gather(xin, "zh", axis=0, tiled=True)
        xin = lax.all_gather(xin, "x", axis=0, tiled=True)
        xin = lax.all_gather(xin, "core", axis=0, tiled=True)
    wg = w_gate.reshape(EXPERTS, DSH, FSH)
    wu = w_up.reshape(EXPERTS, DSH, FSH)
    wd = w_down.reshape(EXPERTS, DSH, FSH)
    xt = xin[:, :2 * DSH].T
    pre = forward(xin, wg, wu, wd)
    with jax.named_scope("sum_pre"):
        pre = exchange(pre, "y").reshape(4, TOKENS // 4, PACK)
        pre = jnp.sum(pre.astype(f32), axis=0).astype(bf16)
        pre = exchange(pre, "zl").reshape(8, BLK, PACK)
        pre = jnp.sum(pre.astype(f32), axis=0).astype(bf16)
    with jax.named_scope("spread_pre"):
        pre = exchange(jnp.tile(pre, (8, 1)), "zl")
        pre = exchange(jnp.tile(pre, (4, 1)), "y")
    gg, gu, gd, dx = backward(xin, xt, pre, wg, wu)
    with jax.named_scope("sum_dx"):
        core = lax.axis_index("core")
        half = TOKENS // 2
        keep = lax.dynamic_slice_in_dim(dx, core * half, half, 0).astype(f32)
        give = lax.dynamic_slice_in_dim(dx, (1 - core) * half, half, 0)
        dx = (keep + swap(give, "core").astype(f32)).astype(bf16)
        dx = exchange(dx, "x").reshape(4, half // 4, dx.shape[1])
        dx = jnp.sum(dx.astype(f32), axis=0).astype(bf16)
        zh = lax.axis_index("zh")
        keep = lax.dynamic_slice_in_dim(dx, zh * tok, tok, 0).astype(f32)
        give = lax.dynamic_slice_in_dim(dx, (1 - zh) * tok, tok, 0)
        dx = keep + swap(give, "zh").astype(f32)
    grad_in = dx[:, :DSH].astype(bf16)
    grad_probs = dx[:, OUT_COLS:OUT_COLS + TOP]
    flat = w_gate.shape
    return (grad_in, grad_probs, gg.reshape(flat), gu.reshape(flat), gd.reshape(flat))


def solution(mesh):
    fine = Mesh(mesh.devices.reshape(4, 2, 2, 8, 4), DP + EX)
    in_specs = (
        P(DP, EX),
        P(DP, EX),
        P(DP, EX),
        P(DP, None),
        P(DP, None),
        P(None, DP + EX),
        P(None, DP + EX),
        P(None, DP + EX),
    )
    out_specs = (
        P(DP, EX),
        P(DP, None),
        P(None, DP + EX),
        P(None, DP + EX),
        P(None, DP + EX),
    )
    return jax.shard_map(local, mesh=fine, in_specs=in_specs, out_specs=out_specs, check_vma=False)
```

time: 1020 us -> 235 us (0.23)
  the two profiles are of different devices: /device:TPU:2 before, /device:TPU:1 now
where the time goes in v1:
time: 235 us; the launch traced here: 231 us
  blocking collectives  119 us (51%)
  Pallas kernels  37.9 us (16%)
  starting transfers between devices  23.5 us (10%)
  waiting for transfers between devices  23.1 us (10%)
  local copies, waits for them, and re-layouts  22.8 us (10%)
  other arithmetic  4.5 us (2%)
    all_to_all x3, blocking collectives, exchange(): return lax.all_to_all(value, axis, split_axis=0, concat_axis=0, tiled=True)  84.5 us
    pallas_call x1, Pallas kernels, backward(): pl.pallas_call(backward_kernel, out_shape=[weight] * 3 + [jax.ShapeDtypeS...  25.5 us
    all_to_all x2, waiting for transfers between devices, exchange(): return lax.all_to_all(value, axis, split_axis=0, concat_axis=0, tiled=True)  21.6 us
    ppermute x2, starting transfers between devices, swap(): return lax.ppermute(value, axis, [(0, 1), (1, 0)])  16.4 us
    all_gather x1, blocking collectives, local(): xin = lax.all_gather(xin, 'zh', axis=0, tiled=True)  16.3 us
    pallas_call x1, Pallas kernels, forward(): pl.pallas_call(forward_kernel, out_shape=jax.ShapeDtypeStruct((TOKENS, PA...  12.4 us
    all_gather x1, blocking collectives, local(): xin = lax.all_gather(xin, 'x', axis=0, tiled=True)  9.58 us
    all_gather x1, blocking collectives, local(): xin = lax.all_gather(xin, 'core', axis=0, tiled=True)  8.15 us
  transfers between devices with their start and end apart: 4, of which 4 were waited for; matrix products, arithmetic and copies ran while one was open for 3% of the time, Pallas kernels for 0%

profile of v1, /device:TPU:1, one launch (start us, length us, event | category | flops | bytes accessed | tf_op | source)
XLA Modules:
  0.0 231.2 jit_solution(15705781019213422182)
XLA Ops:
  0.6 0.0 copy-start.5
  0.6 0.7 multiply_exponential_fusion
  1.4 0.0 copy-start.6
  1.4 0.1 copy.61
  1.5 0.7 convert_element_type.37
  2.2 0.1 copy.62
  2.3 0.8 copy.63
  3.1 0.7 multiply_convert_fusion
  3.8 0.8 concatenate.3
  4.6 16.3 %all_gather.9 = bf16[64,384]{1,0:T(8,128)(2,1)S(1)} all-gather(bf16[32,384]{1,0:T(8,128)(2,1)S(1)} %concatenate.3), channel_id=1, replica_groups=mesh['x'=4,'zh'=2,'core'=2,'zl'=8,'y'=4] {'zh'}, dimensions={0}, use_global_device_ids=true | all-gather | bytes 73728 | tf_op jit(solution)/shard_map/gather_tokens/all_gather | solution.py:191
  21.0 9.6 %all_gather.10 = bf16[256,384]{1,0:T(8,128)(2,1)S(1)} all-gather(bf16[64,384]{1,0:T(8,128)(2,1)S(1)} %all_gather.9), channel_id=1, replica_groups=mesh['x'=4,'zh'=2,'core'=2,'zl'=8,'y'=4] {'x'}, dimensions={0}, use_global_device_ids=true | all-gather | bytes 245760 | tf_op jit(solution)/shard_map/gather_tokens/all_gather | solution.py:192
  30.6 0.1 copy.64
  30.7 0.0 copy-start.7
  30.7 8.2 %all_gather.11 = bf16[512,384]{0,1:T(8,128)(2,1)S(1)} all-gather(bf16[256,384]{0,1:T(8,128)(2,1)S(1)} %copy.64), channel_id=1, replica_groups=mesh['x'=4,'zh'=2,'core'=2,'zl'=8,'y'=4] {'core'}, dimensions={0}, use_global_device_ids=true | all-gather | bytes 589824 | tf_op jit(solution)/shard_map/gather_tokens/all_gather | solution.py:193
  38.9 0.0 copy-start
  38.9 0.9 copy.70.xin_ref
  39.8 0.0 copy-done.5
  39.8 1.5 reshape.59.wg_ref
  41.3 0.0 copy-done.6
  41.3 1.5 reshape.60.wu_ref
  42.8 0.0 copy-done.7
  42.8 1.5 reshape.61.wd_ref
  44.3 0.0 copy-done
  44.3 12.4 %shard_map.119 = bf16[512,1728]{1,0:T(8,128)(2,1)} custom-call(bf16[512,384]{1,0:T(8,128)(2,1)} %copy.70.xin_ref, bf16[16,160,96]{2,1,0:T(8,128)(2,1)} %reshape.59.wg_ref, bf16[16,160,96]{2,1,0:T(8,128)(2,1)} %reshape.60.wu_ref, bf16[16,160,96]{2,1,0:T(8,128)(2,1)} %reshape.61.wd_ref), custom_call_target="tpu_custom_call" | custom-call | tf_op jit(solution)/shard_map/pallas_call | solution.py:144
  56.7 2.9 %copy.66 = bf16[4,128,1728]{1,2,0:T(8,128)(2,1)S(1)} copy(bf16[4,128,1728]{2,1,0:T(8,128)(2,1)} %bitcast.9) | data formatting | bytes 3538944 | tf_op jit(solution)/shard_map/sum_pre/all_to_all | solution.py:176
  59.6 24.7 %all_to_all.41 = bf16[4,128,1728]{1,2,0:T(8,128)(2,1)S(1)} all-to-all(bf16[4,128,1728]{1,2,0:T(8,128)(2,1)S(1)} %copy.66), channel_id=1, replica_groups=mesh['x'=4,'zh'=2,'core'=2,'zl'=8,'y'=4] {'y'}, dimensions={0} | all-to-all | bytes 3538944 | tf_op jit(solution)/shard_map/sum_pre/all_to_all | solution.py:176
  84.3 0.5 reduce_sum.36
  84.8 0.2 copy.67
  85.0 29.5 %all_to_all.42 = bf16[8,16,1728]{2,1,0:T(8,128)(2,1)S(1)} all-to-all(bf16[8,16,1728]{2,1,0:T(8,128)(2,1)S(1)} %bitcast.10), channel_id=1, replica_groups=mesh['x'=4,'zh'=2,'core'=2,'zl'=8,'y'=4] {'zl'}, dimensions={0} | all-to-all | bytes 884736 | tf_op jit(solution)/shard_map/sum_pre/all_to_all | solution.py:176
  114.6 0.1 reduce_sum.37
  114.7 30.2 %all_to_all.43 = bf16[8,16,1728]{2,1,0:T(8,128)(2,1)S(1)} all-to-all(bf16[8,16,1728]{2,1,0:T(8,128)(2,1)S(1)} %tile.6), channel_id=1, replica_groups=mesh['x'=4,'zh'=2,'core'=2,'zl'=8,'y'=4] {'zl'}, dimensions={0} | all-to-all | bytes 884736 | tf_op jit(solution)/shard_map/spread_pre/all_to_all | solution.py:176
  144.9 0.3 copy.68
  145.2 1.5 tile.8
  146.7 0.0 copy-start.1
  146.7 3.7 %all-to-all-start.3 = ((bf16[4,128,1728]{1,2,0:T(8,128)(2,1)}), bf16[4,128,1728]{1,2,0:T(8,128)(2,1)S(1)}, u32[]{:S(2)}, u32[]{:S(2)}) async-start(bf16[4,128,1728]{1,2,0:T(8,128)(2,1)} %tile.8), calls=%async_computation.3 | async-start | bytes 3538944 | tf_op jit(solution)/shard_map/spread_pre/all_to_all | solution.py:176
  150.4 0.0 copy-done.1
  150.4 0.7 slice_bitcast_fusion.xt_ref
  151.2 16.3 %all-to-all-done.3 = bf16[4,128,1728]{1,2,0:T(8,128)(2,1)S(1)} async-done(((bf16[4,128,1728]{1,2,0:T(8,128)(2,1)}), bf16[4,128,1728]{1,2,0:T(8,128)(2,1)S(1)}, u32[]{:S(2)}, u32[]{:S(2)}) %all-to-all-start.3) | async-done | bytes 1769504 | tf_op jit(solution)/shard_map/spread_pre/all_to_all | solution.py:176
  167.5 2.5 %copy.69 = bf16[4,128,1728]{2,1,0:T(8,128)(2,1)} copy(bf16[4,128,1728]{1,2,0:T(8,128)(2,1)S(1)} %all-to-all-done.3) | data formatting | bytes 3538944 | tf_op jit(solution)/shard_map/spread_pre/all_to_all | solution.py:176
  170.0 25.5 %shard_map.120 = (bf16[16,160,96]{2,1,0:T(8,128)(2,1)}, bf16[16,160,96]{2,1,0:T(8,128)(2,1)}, bf16[16,160,96]{2,1,0:T(8,128)(2,1)}, bf16[512,384]{1,0:T(8,128)(2,1)}) custom-call(bf16[512,384]{1,0:T(8,128)(2,1)} %copy.70.xin_ref, bf16[320,512]{1,0:T(8,128)(2,1)} %slice_bitcast_fusion.xt_ref, bf16[512,1728]{1,0:T(8,128)(2,1)} %bitcast.8, ...), custom_call_target="tpu_custom_call" | custom-call | tf_op jit(solution)/shard_map/pallas_call | solution.py:160
  195.5 0.0 copy-start.4
  195.5 0.0 copy-start.3
  195.5 1.1 constant_dynamic-slice_fusion.1
  196.6 8.6 %collective-permute-start = (bf16[256,384]{1,0:T(8,128)(2,1)S(1)}, bf16[256,384]{1,0:T(8,128)(2,1)S(1)}, u32[]{:S(2)}, u32[]{:S(2)}) collective-permute-start(bf16[256,384]{1,0:T(8,128)(2,1)S(1)} %constant_dynamic-slice_fusion.1), channel_id=1, source_target_pairs={{0,32},{32,0},{1,33},{33,1},{2,34},{34,2},{3,35},{35,3},{4,36},{36... | collective-permute-start | bytes 589832 | tf_op jit(solution)/shard_map/sum_dx/ppermute | solution.py:180
  205.1 0.0 copy-start.2
  205.1 1.0 collective-permute-done
  206.2 1.7 add_convert_fusion
  207.8 3.4 %all-to-all-start.4 = ((bf16[4,64,384]{2,1,0:T(8,128)(2,1)}), bf16[4,64,384]{2,1,0:T(8,128)(2,1)S(1)}, u32[]{:S(2)}, u32[]{:S(2)}) async-start(bf16[4,64,384]{2,1,0:T(8,128)(2,1)} %bitcast.6), calls=%async_computation.4 | async-start | bytes 393216 | tf_op jit(solution)/shard_map/sum_dx/all_to_all | solution.py:176
  211.2 5.3 %all-to-all-done.4 = bf16[4,64,384]{2,1,0:T(8,128)(2,1)S(1)} async-done(((bf16[4,64,384]{2,1,0:T(8,128)(2,1)}), bf16[4,64,384]{2,1,0:T(8,128)(2,1)S(1)}, u32[]{:S(2)}, u32[]{:S(2)}) %all-to-all-start.4) | async-done | bytes 196640 | tf_op jit(solution)/shard_map/sum_dx/all_to_all | solution.py:176
  216.6 7.8 %collective-permute-start.1 = (bf16[32,384]{1,0:T(8,128)(2,1)S(1)}, bf16[32,384]{1,0:T(8,128)(2,1)S(1)}, u32[]{:S(2)}, u32[]{:S(2)}) collective-permute-start(bf16[32,384]{1,0:T(8,128)(2,1)S(1)} %constant_dynamic-slice_fusion), channel_id=1, source_target_pairs={{0,64},{64,0},{1,65},{65,1},{2,66},{66,2},{3,67},{67,3},{4,68},{68... | collective-permute-start | bytes 73736 | tf_op jit(solution)/shard_map/sum_dx/ppermute | solution.py:180
  224.4 0.0 copy-done.4
  224.4 1.7 reshape.62
  226.1 0.0 copy-done.3
  226.1 1.7 reshape.63
  227.8 0.0 copy-done.2
  227.8 1.7 reshape.64
  229.5 0.4 collective-permute-done.1
  229.9 0.6 slice.18
  230.5 0.7 copy.71
  (7 shorter events, 0.1 us)
Async XLA Ops:
  0.6 39.2 %copy-start.5 = (bf16[16,15360]{1,0:T(8,128)(2,1)S(1)}, bf16[16,15360]{1,0:T(8,128)(2,1)}, u32[]{:S(2)}) copy-start(bf16[16,15360]{1,0:T(8,128)(2,1)} %param.13) | copy-start | bytes 1474564
  1.4 39.9 %copy-start.6 = (bf16[16,15360]{1,0:T(8,128)(2,1)S(1)}, bf16[16,15360]{1,0:T(8,128)(2,1)}, u32[]{:S(2)}) copy-start(bf16[16,15360]{1,0:T(8,128)(2,1)} %param.14) | copy-start | bytes 1474564
  30.7 12.1 %copy-start.7 = (bf16[16,15360]{1,0:T(8,128)(2,1)S(1)}, bf16[16,15360]{1,0:T(8,128)(2,1)}, u32[]{:S(2)}) copy-start(bf16[16,15360]{1,0:T(8,128)(2,1)} %param.15) | copy-start | bytes 1474564
  38.9 5.4 %copy-start = (bf16[512,384]{0,1:T(8,128)(2,1)}, bf16[512,384]{0,1:T(8,128)(2,1)S(1)}, u32[]{:S(2)}) copy-start(bf16[512,384]{0,1:T(8,128)(2,1)S(1)} %all_gather.11) | copy-start | bytes 1179652
  146.7 3.7 %copy-start.1 = (bf16[512,384]{0,1:T(8,128)(2,1)S(1)}, bf16[512,384]{0,1:T(8,128)(2,1)}, u32[]{:S(2)}) copy-start(bf16[512,384]{0,1:T(8,128)(2,1)} %copy-done) | copy-start | bytes 1179652
  146.7 20.8 %all-to-all-start.3 = ((bf16[4,128,1728]{1,2,0:T(8,128)(2,1)}), bf16[4,128,1728]{1,2,0:T(8,128)(2,1)S(1)}, u32[]{:S(2)}, u32[]{:S(2)}) async-start(bf16[4,128,1728]{1,2,0:T(8,128)(2,1)} %tile.8), calls=%async_computation.3 | async-start | bytes 3538944 | tf_op jit(solution)/shard_map/spread_pre/all_to_all | solution.py:176
  195.5 28.9 %copy-start.4 = (bf16[16,160,96]{2,1,0:T(8,128)(2,1)S(1)}, bf16[16,160,96]{2,1,0:T(8,128)(2,1)}, u32[]{:S(2)}) copy-start(bf16[16,160,96]{2,1,0:T(8,128)(2,1)} %get-tuple-element.10) | copy-start | bytes 1474564
  195.5 30.6 %copy-start.3 = (bf16[16,160,96]{2,1,0:T(8,128)(2,1)S(1)}, bf16[16,160,96]{2,1,0:T(8,128)(2,1)}, u32[]{:S(2)}) copy-start(bf16[16,160,96]{2,1,0:T(8,128)(2,1)} %get-tuple-element.11) | copy-start | bytes 1474564
  196.6 9.6 %collective-permute-start = (bf16[256,384]{1,0:T(8,128)(2,1)S(1)}, bf16[256,384]{1,0:T(8,128)(2,1)S(1)}, u32[]{:S(2)}, u32[]{:S(2)}) collective-permute-start(bf16[256,384]{1,0:T(8,128)(2,1)S(1)} %constant_dynamic-slice_fusion.1), channel_id=1, source_target_pairs={{0,32},{32,0},{1,33},{33,1},{2,34},{34,2},{3,35},{35,3},{4,36},{36... | collective-permute-start | bytes 589832 | tf_op jit(solution)/shard_map/sum_dx/ppermute | solution.py:180
  205.1 22.7 %copy-start.2 = (bf16[16,160,96]{2,1,0:T(8,128)(2,1)S(1)}, bf16[16,160,96]{2,1,0:T(8,128)(2,1)}, u32[]{:S(2)}) copy-start(bf16[16,160,96]{2,1,0:T(8,128)(2,1)} %get-tuple-element.12) | copy-start | bytes 1474564
  207.8 8.7 %all-to-all-start.4 = ((bf16[4,64,384]{2,1,0:T(8,128)(2,1)}), bf16[4,64,384]{2,1,0:T(8,128)(2,1)S(1)}, u32[]{:S(2)}, u32[]{:S(2)}) async-start(bf16[4,64,384]{2,1,0:T(8,128)(2,1)} %bitcast.6), calls=%async_computation.4 | async-start | bytes 393216 | tf_op jit(solution)/shard_map/sum_dx/all_to_all | solution.py:176
  216.6 13.3 %collective-permute-start.1 = (bf16[32,384]{1,0:T(8,128)(2,1)S(1)}, bf16[32,384]{1,0:T(8,128)(2,1)S(1)}, u32[]{:S(2)}, u32[]{:S(2)}) collective-permute-start(bf16[32,384]{1,0:T(8,128)(2,1)S(1)} %constant_dynamic-slice_fusion), channel_id=1, source_target_pairs={{0,64},{64,0},{1,65},{65,1},{2,66},{66,2},{3,67},{67,3},{4,68},{68... | collective-permute-start | bytes 73736 | tf_op jit(solution)/shard_map/sum_dx/ppermute | solution.py:180

commit v2 on v1

v2 whole, which is shorter than its diff:
```python
import jax
import jax.numpy as jnp
from jax import lax
from jax.experimental import pallas as pl
from jax.experimental.pallas import tpu as pltpu
from jax.sharding import Mesh, PartitionSpec as P

DP = ("x", "zh", "core")
EX = ("zl", "y")
BLK = 16
TOP = 6
CAP = 8
EXPERTS = 16
DSH = 160
FSH = 96
SHARD = 32
TOKENS = 512
BLOCKS = TOKENS // BLK
LANES = 128
NG = 4
NE = EXPERTS // NG
NX = 4
SLOTS = BLOCKS * CAP
Q = DSH // 4
STEP = Q + 8
WIDE = 4 * STEP
COLS = 2 * WIDE
IDS_AT = Q
PROBS_AT = STEP + Q
TRIO = 3 * FSH
PACK = NE * TRIO
PAIR = 2 * LANES
DX_COLS = 256
VMEM = 56 * 1024 * 1024
BF16 = jnp.bfloat16
F32 = jnp.float32


def iota(shape, dim):
    return lax.broadcasted_iota(jnp.int32, shape, dim)


def dot(a, b):
    return jnp.dot(a, b, preferred_element_type=F32)


def dot_dims(a, b, left, right):
    return lax.dot_general(a, b, (((left,), (right,)), ((), ())), preferred_element_type=F32)


def feature_of(column):
    s = sum(jnp.where(column >= i * STEP, 1, 0) for i in range(1, 4))
    q = column - s * STEP
    return jnp.where((q < Q) & (column >= 0) & (column < WIDE), 4 * q + s, -1)


def ones(mask):
    return jnp.where(mask, 1.0, 0.0).astype(BF16)


def prepare_kernel(stash_ref, scale_ref, dy_ref, ids_ref, probs_ref, out_ref):
    scale = scale_ref[...]
    factor = jnp.where(scale == -2, 0.25, jnp.where(scale == -1, 0.5, jnp.where(scale == 0, 1.0, 2.0)))
    per = DSH // scale.shape[1]
    shape = (scale.shape[1], DSH)
    first = iota(shape, 0) * per
    expand = ones((iota(shape, 1) >= first) & (iota(shape, 1) < first + per))
    x = (stash_ref[...].astype(F32) * dot(factor.astype(BF16), expand)).astype(BF16)
    row, column = iota((DSH, COLS), 0), iota((DSH, COLS), 1)
    out = dot(x, ones(row == feature_of(column)))
    out = out + dot(dy_ref[...], ones(row == feature_of(column - WIDE)))
    row, column = iota((TOP, COLS), 0), iota((TOP, COLS), 1)
    out = out + dot(ids_ref[...].astype(F32).astype(BF16), ones(row == column - IDS_AT))
    out = out + dot(probs_ref[...], ones(row == column - PROBS_AT))
    out_ref[...] = out.astype(BF16)


def tokens_of(x_ref, g):
    return x_ref[:, :, g].reshape(TOKENS, COLS)


def forward_kernel(me_ref, x_ref, w_ref, pre_ref, xs_ref, ds_ref, wx_ref, gate_ref, slot_ref, pick_ref, wd_ref):
    first = me_ref[0] * NE
    head = tokens_of(x_ref, 0)[:, :LANES].astype(F32)
    ids = head[:, IDS_AT:IDS_AT + TOP]
    probs = head[:, PROBS_AT:PROBS_AT + TOP]
    lane = iota((TOKENS, LANES), 1)
    hit = jnp.zeros((TOKENS, LANES), F32)
    prob = jnp.zeros((TOKENS, LANES), F32)
    for k in range(TOP):
        same = ids[:, k:k + 1] == (lane + first).astype(F32)
        hit = jnp.where(same, 1.0, hit)
        prob = jnp.where(same, probs[:, k:k + 1], prob)
    hit = jnp.where(lane < NE, hit, 0.0)
    row, column = iota((TOKENS, TOKENS), 0), iota((TOKENS, TOKENS), 1)
    before = ones((column < row) & (column >= row - row % BLK))
    place = dot(before, hit.astype(BF16))
    block = iota((TOKENS, LANES), 0) // BLK
    slot = jnp.where(hit > 0.5, block.astype(F32) * CAP + place, -1.0)
    slot_ref[...] = slot
    slot_t = slot.T
    row = iota((SLOTS, TOKENS), 0).astype(F32)
    for e in range(NE):
        pick_ref[e * SLOTS:(e + 1) * SLOTS, :] = ones(row == slot_t[e:e + 1, :])
    pick = pick_ref[...]
    gate_ref[...] = dot(pick, prob.astype(BF16))
    for g in range(NG):
        xs_ref[g] = dot(pick, x_ref[:, :, g, :, :WIDE].reshape(TOKENS, WIDE)).astype(BF16)
        ds_ref[g] = dot(pick, x_ref[:, :, g, :, WIDE:].reshape(TOKENS, WIDE)).astype(BF16)
    low = jnp.zeros((STEP - Q, FSH), F32)
    side = jnp.zeros((STEP, LANES - FSH), F32)
    for g in range(NG):
        for e in range(NE):
            for i in range(3):
                w = w_ref[g, e, i].astype(F32)
                for s in range(4):
                    piece = jnp.concatenate([w[:, s * FSH:(s + 1) * FSH], low], axis=0)
                    piece = jnp.concatenate([piece, side], axis=1).astype(BF16)
                    if i < 2:
                        wx_ref[g, s * STEP:(s + 1) * STEP, e * PAIR + i * LANES:e * PAIR + (i + 1) * LANES] = piece
                    else:
                        wd_ref[g, s * STEP:(s + 1) * STEP, e * LANES:(e + 1) * LANES] = piece
    for e in range(NE):
        at = slice(e * SLOTS, (e + 1) * SLOTS)
        ab = jnp.zeros((SLOTS, PAIR), F32)
        back = jnp.zeros((SLOTS, LANES), F32)
        for g in range(NG):
            ab = ab + dot(xs_ref[g, at, :], wx_ref[g, :, e * PAIR:(e + 1) * PAIR])
            back = back + dot(ds_ref[g, at, :], wd_ref[g, :, e * LANES:(e + 1) * LANES])
        pieces = [ab[:, :FSH], ab[:, LANES:LANES + FSH], back[:, :FSH]]
        pre_ref[:, e * TRIO:(e + 1) * TRIO] = jnp.concatenate(pieces, axis=1).astype(BF16)


def middle_kernel(me_ref, x_ref, pre_ref, wx_ref, gate_ref, slot_ref, d_ref, dx_ref, spread_ref):
    first = me_ref[0] * NE
    side = jnp.zeros((SLOTS, LANES - FSH), F32)
    lane = iota((SLOTS, LANES - FSH), 1)
    slots = iota((TOKENS, SLOTS), 1).astype(F32)
    head = tokens_of(x_ref, 0)[:, :LANES].astype(F32)
    wide = iota((TOKENS, LANES), 1)
    tail = jnp.zeros((TOKENS, LANES), F32)
    for e in range(NE):
        pre = pre_ref[:, e * TRIO:(e + 1) * TRIO].astype(F32)
        a, b, back = (pre[:, i * FSH:(i + 1) * FSH] for i in range(3))
        gate = gate_ref[e * SLOTS:(e + 1) * SLOTS, e:e + 1]
        sig = jax.nn.sigmoid(a)
        act = a * sig
        hidden = act * b
        dh = gate * back
        d_gate = dh * b * sig * (1.0 + a * (1.0 - sig))
        prob = jnp.sum(hidden * back, axis=1, keepdims=True)
        prob = jnp.where(lane == 0, prob, 0.0)
        d = jnp.concatenate([d_gate, prob, dh * act, side, gate * hidden, side], axis=1).astype(BF16)
        d_ref[e] = d
        pick = ones(slots == slot_ref[:, e:e + 1])
        spread = dot(pick, d[:, :PAIR])
        spread_ref[:, e * PAIR:(e + 1) * PAIR] = spread.astype(BF16)
        for k in range(TOP):
            same = head[:, IDS_AT + k:IDS_AT + k + 1] == (first + e).astype(F32)
            tail = jnp.where((wide == k) & same, spread[:, FSH:FSH + 1], tail)
    tail = tail[:, :DX_COLS - WIDE]
    for g in range(NG):
        dx = dot_dims(spread_ref[...], wx_ref[g], 1, 1)
        dx = jnp.concatenate([dx, tail], axis=1).astype(BF16)
        dx_ref[:, :, g] = dx.reshape(2, NX, 2 * SHARD, DX_COLS)


def weight_kernel(xs_ref, ds_ref, d_ref, out_ref):
    for e in range(NE):
        at = slice(e * SLOTS, (e + 1) * SLOTS)
        for g in range(NG):
            both = dot_dims(xs_ref[g, at, :], d_ref[e, :, :PAIR], 0, 0)
            down = dot_dims(ds_ref[g, at, :], d_ref[e, :, PAIR:], 0, 0)
            for i, (grad, base) in enumerate(((both, 0), (both, LANES), (down, 0))):
                pieces = [grad[s * STEP:s * STEP + Q, base:base + FSH] for s in range(4)]
                out_ref[g, e, i] = jnp.concatenate(pieces, axis=1).astype(BF16)


def finish_kernel(dx_ref, got_ref, in_ref, probs_ref):
    total = dx_ref[...].astype(F32) + got_ref[...].astype(F32)
    row, column = iota((WIDE, DSH), 0), iota((WIDE, DSH), 1)
    order = ones(feature_of(row) == column)
    in_ref[...] = dot(total[:, :WIDE].astype(BF16), order).astype(BF16)
    probs_ref[...] = total[:, WIDE:WIDE + TOP]


def call(kernel, outs, args, scratch=(), scalar=False):
    vmem = pl.BlockSpec(memory_space=pltpu.VMEM)
    specs = [vmem] * len(args)
    if scalar:
        specs[0] = pl.BlockSpec(memory_space=pltpu.SMEM)
    return pl.pallas_call(
        kernel,
        out_shape=[jax.ShapeDtypeStruct(shape, dtype) for shape, dtype in outs],
        in_specs=specs,
        out_specs=[vmem] * len(outs),
        scratch_shapes=[pltpu.VMEM(shape, dtype) for shape, dtype in scratch],
        compiler_params=pltpu.CompilerParams(vmem_limit_bytes=VMEM),
    )(*args)


def exchange(value, axis):
    return lax.all_to_all(value, axis, split_axis=0, concat_axis=0, tiled=True)


def swap(value, axis):
    return lax.ppermute(value, axis, [(0, 1), (1, 0)])


def sum_first(value):
    return jnp.sum(value.astype(F32), axis=0).astype(BF16)


def local(stash, scale_exp, grad_out, route_ids, route_probs, w_gate, w_up, w_down):
    me = lax.axis_index("y").astype(jnp.int32).reshape(1)
    core = lax.axis_index("core")
    zh = lax.axis_index("zh")
    (xin,) = call(prepare_kernel, [((SHARD, COLS), BF16)], (stash, scale_exp, grad_out, route_ids, route_probs))
    with jax.named_scope("gather_tokens"):
        other = swap(xin, "zh")
        xin = jnp.where(zh == 0, jnp.concatenate([xin, other]), jnp.concatenate([other, xin]))
        xin = exchange(jnp.tile(xin, (NX * NG, 1)), ("x", "y"))
        other = swap(xin, "core")
        xin = jnp.where(core == 0, jnp.stack([xin, other]), jnp.stack([other, xin]))
        xin = xin.reshape(2, NX, NG, 2 * SHARD, COLS)
    with jax.named_scope("move_weights"):
        tiles = [w.reshape(EXPERTS, 1, Q, 4 * FSH) for w in (w_gate, w_up, w_down)]
        weights = exchange(jnp.concatenate(tiles, axis=1), "y")
        weights = weights.reshape(NG, NE, 3, Q, 4 * FSH)
    pre, xs, ds, wx, gate, slot = call(
        forward_kernel,
        [((SLOTS, PACK), BF16), ((NG, NE * SLOTS, WIDE), BF16), ((NG, NE * SLOTS, WIDE), BF16),
         ((NG, WIDE, NE * PAIR), BF16), ((NE * SLOTS, LANES), F32), ((TOKENS, LANES), F32)],
        (me, xin, weights),
        [((NE * SLOTS, TOKENS), BF16), ((NG, WIDE, NE * LANES), BF16)],
        True)
    with jax.named_scope("sum_pre"):
        pre = sum_first(exchange(pre, "zl").reshape(8, SLOTS // 8, PACK))
    with jax.named_scope("spread_pre"):
        pre = exchange(jnp.tile(pre, (8, 1)), "zl")
    d, dx = call(
        middle_kernel,
        [((NE, SLOTS, 3 * LANES), BF16), ((2, NX, NG, 2 * SHARD, DX_COLS), BF16)],
        (me, xin, pre, wx, gate, slot),
        [((TOKENS, NE * PAIR), BF16)],
        True)
    (grads,) = call(weight_kernel, [((NG, NE, 3, Q, 4 * FSH), BF16)], (xs, ds, d))
    with jax.named_scope("sum_dx"):
        keep = lax.dynamic_index_in_dim(dx, core, 0, False).astype(F32)
        give = lax.dynamic_index_in_dim(dx, 1 - core, 0, False)
        dx = (keep + swap(give, "core").astype(F32)).astype(BF16)
        dx = exchange(dx.reshape(NX * NG, 2 * SHARD, DX_COLS), ("x", "y"))
        dx = jnp.sum(dx.astype(F32), axis=0)
        keep = lax.dynamic_slice_in_dim(dx, zh * SHARD, SHARD, 0)
        give = lax.dynamic_slice_in_dim(dx, (1 - zh) * SHARD, SHARD, 0).astype(BF16)
        got = swap(give, "zh")
    with jax.named_scope("return_grads"):
        grads = exchange(grads.reshape(EXPERTS, 3, Q, 4 * FSH), "y")
        grads = [grads[:, i].reshape(w_gate.shape) for i in range(3)]
    grad_in, grad_probs = call(finish_kernel, [((SHARD, DSH), BF16), ((SHARD, TOP), F32)], (keep, got))
    return (grad_in, grad_probs, *grads)


def solution(mesh):
    fine = Mesh(mesh.devices.reshape(4, 2, 2, 8, 4), DP + EX)
    weight = P(None, DP + EX)
    in_specs = (P(DP, EX), P(DP, EX), P(DP, EX), P(DP, None), P(DP, None), weight, weight, weight)
    out_specs = (P(DP, EX), P(DP, None), weight, weight, weight)
    return jax.shard_map(local, mesh=fine, in_specs=in_specs, out_specs=out_specs, check_vma=False)
```

time: 235 us -> 208 us (0.89)
  blocking collectives: 119 us -> 36.6 us
  starting transfers between devices: 23.5 us -> 64.5 us
  waiting for transfers between devices: 23.1 us -> 57.7 us
  Pallas kernels: 37.9 us -> 26 us
  local copies, waits for them, and re-layouts: 22.8 us -> 14.6 us
    all_to_all x3 -> x1, blocking collectives: 84.5 us -> 36.6 us  [exchange(): return lax.all_to_all(value, axis, split_axis=0, concat_axis=0, tiled=True)]
    all_gather x3 -> x0, blocking collectives: 34.1 us -> none  [the longest x1 16.3 us: local(): xin = lax.all_gather(xin, 'zh', axis=0, tiled=True)]
    all_to_all x2 -> x5, waiting for transfers between devices: 21.6 us -> 48.2 us  [exchange(): return lax.all_to_all(value, axis, split_axis=0, concat_axis=0, tiled=True)]
    ppermute x2 -> x4, starting transfers between devices: 16.4 us -> 40.9 us  [swap(): return lax.ppermute(value, axis, [(0, 1), (1, 0)])]
    all_to_all x2 -> x5, starting transfers between devices: 7.08 us -> 23.6 us  [exchange(): return lax.all_to_all(value, axis, split_axis=0, concat_axis=0, tiled=True)]
    pallas_call x2 -> x5, Pallas kernels: 37.9 us -> 26 us  [call(): pl.pallas_call(kernel, out_shape=[jax.ShapeDtypeStruct(shape, dtype) for...]
    reshape x7 -> x0, local copies, waits for them, and re-layouts: 9.57 us -> none  [the longest x1 1.69 us: local(): gg.reshape(flat)]
    unnamed x18 -> x22, local copies, waits for them, and re-layouts: 1.48 us -> 10.9 us
  transfers between devices with their start and end apart: 4 -> 9, of which waited for: 4 -> 9; matrix products, arithmetic and copies ran while one was open for 3% -> 2% of each run, Pallas kernels for 0% -> 3%
where the time goes in v2:
time: 208 us; the launch traced here: 206 us
  starting transfers between devices  64.5 us (31%)
  waiting for transfers between devices  57.7 us (28%)
  blocking collectives  36.6 us (18%)
  Pallas kernels  26 us (12%)
  local copies, waits for them, and re-layouts  14.6 us (7%)
  other arithmetic  5.77 us (3%)
    all_to_all x5, waiting for transfers between devices, exchange(): return lax.all_to_all(value, axis, split_axis=0, concat_axis=0, tiled=True)  48.2 us
    ppermute x4, starting transfers between devices, swap(): return lax.ppermute(value, axis, [(0, 1), (1, 0)])  40.9 us
    all_to_all x1, blocking collectives, exchange(): return lax.all_to_all(value, axis, split_axis=0, concat_axis=0, tiled=True)  36.6 us
    pallas_call x5, Pallas kernels, call(): pl.pallas_call(kernel, out_shape=[jax.ShapeDtypeStruct(shape, dtype) for...  26 us
    all_to_all x5, starting transfers between devices, exchange(): return lax.all_to_all(value, axis, split_axis=0, concat_axis=0, tiled=True)  23.6 us
    unnamed x22, local copies, waits for them, and re-layouts  10.9 us
    ppermute x4, waiting for transfers between devices, swap(): return lax.ppermute(value, axis, [(0, 1), (1, 0)])  9.5 us
  transfers between devices with their start and end apart: 9, of which 9 were waited for; matrix products, arithmetic and copies ran while one was open for 2% of the time, Pallas kernels for 3%

profile of v2, /device:TPU:1, one launch (start us, length us, event | category | flops | bytes accessed | tf_op | source)
XLA Modules:
  0.0 206.0 jit_solution(1387049202881522124)
XLA Ops:
  0.6 0.0 copy-start.2
  0.6 1.4 copy.13.scale_ref
  2.1 1.4 copy.14.ids_ref
  3.4 1.4 copy.15.probs_ref
  4.8 1.6 shard_map.119
  6.5 16.3 %collective-permute-start = (bf16[32,384]{1,0:T(8,128)(2,1)}, bf16[32,384]{1,0:T(8,128)(2,1)S(1)}, u32[]{:S(2)}, u32[]{:S(2)}) collective-permute-start(bf16[32,384]{1,0:T(8,128)(2,1)} %shard_map.119), channel_id=1, source_target_pairs={{0,64},{64,0},{1,65},{65,1},{2,66},{66,2},{3,67},{67,3},{4,68},{68... | collective-permute-start | bytes 73736 | tf_op jit(solution)/shard_map/gather_tokens/ppermute | solution.py:207
  22.7 1.5 collective-permute-done
  24.2 0.8 maximum_select_fusion.1
  25.1 0.0 copy-start.3
  25.1 1.0 tile.4
  26.1 0.0 copy-start.4
  26.1 6.9 %all-to-all-start = ((bf16[16,64,384]{2,1,0:T(8,128)(2,1)}), bf16[16,64,384]{2,1,0:T(8,128)(2,1)S(1)}, u32[]{:S(2)}, u32[]{:S(2)}) async-start(bf16[16,64,384]{2,1,0:T(8,128)(2,1)} %tile.4), calls=%async_computation | async-start | bytes 1572864 | tf_op jit(solution)/shard_map/gather_tokens/all_to_all | solution.py:203
  33.0 0.0 copy-done.2
  33.0 0.1 copy.20
  33.0 0.0 copy-done.3
  33.0 0.1 copy.21
  33.1 0.0 copy-done.4
  33.1 0.1 copy.22
  33.2 1.3 pad_maximum_fusion
  34.5 11.0 %all-to-all-done = bf16[16,64,384]{2,1,0:T(8,128)(2,1)S(1)} async-done(((bf16[16,64,384]{2,1,0:T(8,128)(2,1)}), bf16[16,64,384]{2,1,0:T(8,128)(2,1)S(1)}, u32[]{:S(2)}, u32[]{:S(2)}) %all-to-all-start) | async-done | bytes 786464 | tf_op jit(solution)/shard_map/gather_tokens/all_to_all | solution.py:203
  45.5 3.6 %all-to-all-start.1 = ((bf16[16,3,40,384]{3,2,1,0:T(8,128)(2,1)}), bf16[16,3,40,384]{3,2,1,0:T(8,128)(2,1)S(1)}, u32[]{:S(2)}, u32[]{:S(2)}) async-start(bf16[16,3,40,384]{3,2,1,0:T(8,128)(2,1)} %pad_maximum_fusion), calls=%async_computation.1 | async-start | bytes 2949120 | tf_op jit(solution)/shard_map/move_weights/all_to_all | solution.py:203
  49.0 4.6 %collective-permute-start.1 = (bf16[1024,384]{1,0:T(8,128)(2,1)S(1)}, bf16[1024,384]{1,0:T(8,128)(2,1)S(1)}, u32[]{:S(2)}, u32[]{:S(2)}) collective-permute-start(bf16[1024,384]{1,0:T(8,128)(2,1)S(1)} %bitcast.43), channel_id=1, source_target_pairs={{0,32},{32,0},{1,33},{33,1},{2,34},{34,2},{3,35},{35,3},{4,36},{36... | collective-permute-start | bytes 2359304 | tf_op jit(solution)/shard_map/gather_tokens/ppermute | solution.py:207
  53.7 1.9 collective-permute-done.1
  55.6 1.5 maximum_select_fusion.x_ref
  57.0 8.9 %all-to-all-done.1 = bf16[16,3,40,384]{3,2,1,0:T(8,128)(2,1)S(1)} async-done(((bf16[16,3,40,384]{3,2,1,0:T(8,128)(2,1)}), bf16[16,3,40,384]{3,2,1,0:T(8,128)(2,1)S(1)}, u32[]{:S(2)}, u32[]{:S(2)}) %all-to-all-start.1) | async-done | bytes 1474592 | tf_op jit(solution)/shard_map/move_weights/all_to_all | solution.py:203
  66.0 0.0 copy-start
  66.0 1.2 copy-done
  67.2 7.6 %shard_map.120 = (bf16[256,1152]{1,0:T(8,128)(2,1)}, bf16[4,1024,192]{2,1,0:T(8,128)(2,1)}, bf16[4,1024,192]{2,1,0:T(8,128)(2,1)}, bf16[4,192,1024]{2,1,0:T(8,12...) custom-call(s32[1]{0:T(128)} %bitcast.me_ref, bf16[2,4,4,64,384]{4,3,2,1,0:T(8,128)(2,1)} %maximum_select_fusion.x_ref, ...), custom_call_target="tpu_custom_call" | custom-call | tf_op jit(solution)/shard_map/pallas_call | solution.py:192
  74.8 36.6 %all_to_all.41 = bf16[8,32,1152]{2,1,0:T(8,128)(2,1)S(1)} all-to-all(bf16[8,32,1152]{2,1,0:T(8,128)(2,1)} %bitcast.53), channel_id=1, replica_groups=mesh['x'=4,'zh'=2,'core'=2,'zl'=8,'y'=4] {'zl'}, dimensions={0} | all-to-all | bytes 1179648 | tf_op jit(solution)/shard_map/sum_pre/all_to_all | solution.py:203
  111.4 0.1 reduce_sum.21
  111.5 0.9 tile.5
  112.4 6.0 %all-to-all-start.3 = ((bf16[8,32,1152]{2,1,0:T(8,128)(2,1)}), bf16[8,32,1152]{2,1,0:T(8,128)(2,1)S(1)}, u32[]{:S(2)}, u32[]{:S(2)}) async-start(bf16[8,32,1152]{2,1,0:T(8,128)(2,1)} %tile.5), calls=%async_computation.3 | async-start | bytes 1179648 | tf_op jit(solution)/shard_map/spread_pre/all_to_all | solution.py:203
  118.4 22.4 %all-to-all-done.3 = bf16[8,32,1152]{2,1,0:T(8,128)(2,1)S(1)} async-done(((bf16[8,32,1152]{2,1,0:T(8,128)(2,1)}), bf16[8,32,1152]{2,1,0:T(8,128)(2,1)S(1)}, u32[]{:S(2)}, u32[]{:S(2)}) %all-to-all-start.3) | async-done | bytes 589856 | tf_op jit(solution)/shard_map/spread_pre/all_to_all | solution.py:203
  140.8 0.0 copy-start.1
  140.8 0.8 copy-done.1
  141.6 10.0 %shard_map.121 = (bf16[4,256,384]{2,1,0:T(8,128)(2,1)}, bf16[2,4,4,64,256]{4,3,2,1,0:T(8,128)(2,1)}) custom-call(s32[1]{0:T(128)} %bitcast.me_ref, bf16[2,4,4,64,384]{4,3,2,1,0:T(8,128)(2,1)} %maximum_select_fusion.x_ref, bf16[256,1152]{1,0:T(8,128)(2,1)} %bitcast.45, bf16[4,192,1024]{2,1,0:T(8,128)(2,1)} %get-tuple-element.16.wx_ref, ...), custom_call_target="tpu_custom_call" | custom-call | tf_op jit(solution)/shard_map/pallas_call | solution.py:192
  151.5 1.1 dynamic-slice_bitcast_fusion
  152.6 12.0 %collective-permute-start.2 = (bf16[4,4,64,256]{3,2,1,0:T(8,128)(2,1)S(1)}, bf16[4,4,64,256]{3,2,1,0:T(8,128)(2,1)S(1)}, u32[]{:S(2)}, u32[]{:S(2)}) collective-permute-start(bf16[4,4,64,256]{3,2,1,0:T(8,128)(2,1)S(1)} %dynamic-slice_bitcast_fusion), channel_id=1, source_target_pairs={{0,32},{32,0},{1,33},{33,1},{2,34},{34,2},{3,35},{35,3},{4,36},{36... | collective-permute-start | bytes 1572872 | tf_op jit(solution)/shard_map/sum_dx/ppermute | solution.py:207
  164.7 1.5 collective-permute-done.2
  166.2 2.0 fusion
  168.2 3.6 %all-to-all-start.4 = ((bf16[16,64,256]{2,1,0:T(8,128)(2,1)}), bf16[16,64,256]{2,1,0:T(8,128)(2,1)S(1)}, u32[]{:S(2)}, u32[]{:S(2)}) async-start(bf16[16,64,256]{2,1,0:T(8,128)(2,1)} %bitcast.12), calls=%async_computation.4 | async-start | bytes 1048576 | tf_op jit(solution)/shard_map/sum_dx/all_to_all | solution.py:203
  171.8 5.3 %shard_map.123 = bf16[4,4,3,40,384]{4,3,2,1,0:T(8,128)(2,1)} custom-call(bf16[4,1024,192]{2,1,0:T(8,128)(2,1)} %get-tuple-element.22.xs_ref, bf16[4,1024,192]{2,1,0:T(8,128)(2,1)} %get-tuple-element.23.ds_ref, bf16[4,256,384]{2,1,0:T(8,128)(2,1)} %get-tuple-element.24.d_ref), custom_call_target="tpu_custom_call" | custom-call | tf_op jit(solution)/shard_map/pallas_call | solution.py:192
  177.0 5.1 %all-to-all-done.4 = bf16[16,64,256]{2,1,0:T(8,128)(2,1)S(1)} async-done(((bf16[16,64,256]{2,1,0:T(8,128)(2,1)}), bf16[16,64,256]{2,1,0:T(8,128)(2,1)S(1)}, u32[]{:S(2)}, u32[]{:S(2)}) %all-to-all-start.4) | async-done | bytes 524320 | tf_op jit(solution)/shard_map/sum_dx/all_to_all | solution.py:203
  182.2 3.6 %all-to-all-start.5 = ((bf16[16,3,40,384]{3,2,1,0:T(8,128)(2,1)}), bf16[16,3,40,384]{3,2,1,0:T(8,128)(2,1)S(1)}, u32[]{:S(2)}, u32[]{:S(2)}) async-start(bf16[16,3,40,384]{3,2,1,0:T(8,128)(2,1)} %bitcast.42), calls=%async_computation.5 | async-start | bytes 2949120 | tf_op jit(solution)/shard_map/return_grads/all_to_all | solution.py:203
  185.7 0.1 convert_reduce_fusion
  185.8 8.0 %collective-permute-start.3 = (bf16[32,256]{1,0:T(8,128)(2,1)S(1)}, bf16[32,256]{1,0:T(8,128)(2,1)S(1)}, u32[]{:S(2)}, u32[]{:S(2)}) collective-permute-start(bf16[32,256]{1,0:T(8,128)(2,1)S(1)} %dynamic-slice_convert_fusion), channel_id=1, source_target_pairs={{0,64},{64,0},{1,65},{65,1},{2,66},{66,2},{3,67},{67,3},{4,68},{68... | collective-permute-start | bytes 49160 | tf_op jit(solution)/shard_map/sum_dx/ppermute | solution.py:207
  193.8 0.6 constant_dynamic-slice_fusion.dx_ref
  194.4 4.6 %collective-permute-done.3.got_ref = bf16[32,256]{1,0:T(8,128)(2,1)S(1)} collective-permute-done((bf16[32,256]{1,0:T(8,128)(2,1)S(1)}, bf16[32,256]{1,0:T(8,128)(2,1)S(1)}, u32[]{:S(2)}, u32[]{:S(2)}) %collective-permute-start.3) | collective-permute-done | bytes 16416 | tf_op jit(solution)/shard_map/sum_dx/ppermute | solution.py:207
  199.0 0.0 copy-start.5
  199.0 0.6 copy-done.5
  199.6 1.5 shard_map.122
  201.2 1.4 copy.19
  202.5 0.8 all-to-all-done.5
  203.4 0.2 fusion.1
  203.5 0.8 copy.23
  204.4 0.8 copy.24
  205.2 0.8 copy.25
  (1 shorter events, 0.0 us)
Async XLA Ops:
  0.6 32.3 %copy-start.2 = (bf16[16,15360]{1,0:T(8,128)(2,1)S(1)}, bf16[16,15360]{1,0:T(8,128)(2,1)}, u32[]{:S(2)}) copy-start(bf16[16,15360]{1,0:T(8,128)(2,1)} %param.13) | copy-start | bytes 1474564
  6.5 17.8 %collective-permute-start = (bf16[32,384]{1,0:T(8,128)(2,1)}, bf16[32,384]{1,0:T(8,128)(2,1)S(1)}, u32[]{:S(2)}, u32[]{:S(2)}) collective-permute-start(bf16[32,384]{1,0:T(8,128)(2,1)} %shard_map.119), channel_id=1, source_target_pairs={{0,64},{64,0},{1,65},{65,1},{2,66},{66,2},{3,67},{67,3},{4,68},{68... | collective-permute-start | bytes 73736 | tf_op jit(solution)/shard_map/gather_tokens/ppermute | solution.py:207
  25.1 8.0 %copy-start.3 = (bf16[16,15360]{1,0:T(8,128)(2,1)S(1)}, bf16[16,15360]{1,0:T(8,128)(2,1)}, u32[]{:S(2)}) copy-start(bf16[16,15360]{1,0:T(8,128)(2,1)} %param.14) | copy-start | bytes 1474564
  26.1 7.1 %copy-start.4 = (bf16[16,15360]{1,0:T(8,128)(2,1)S(1)}, bf16[16,15360]{1,0:T(8,128)(2,1)}, u32[]{:S(2)}) copy-start(bf16[16,15360]{1,0:T(8,128)(2,1)} %param.15) | copy-start | bytes 1474564
  26.1 19.4 %all-to-all-start = ((bf16[16,64,384]{2,1,0:T(8,128)(2,1)}), bf16[16,64,384]{2,1,0:T(8,128)(2,1)S(1)}, u32[]{:S(2)}, u32[]{:S(2)}) async-start(bf16[16,64,384]{2,1,0:T(8,128)(2,1)} %tile.4), calls=%async_computation | async-start | bytes 1572864 | tf_op jit(solution)/shard_map/gather_tokens/all_to_all | solution.py:203
  45.5 20.5 %all-to-all-start.1 = ((bf16[16,3,40,384]{3,2,1,0:T(8,128)(2,1)}), bf16[16,3,40,384]{3,2,1,0:T(8,128)(2,1)S(1)}, u32[]{:S(2)}, u32[]{:S(2)}) async-start(bf16[16,3,40,384]{3,2,1,0:T(8,128)(2,1)} %pad_maximum_fusion), calls=%async_computation.1 | async-start | bytes 2949120 | tf_op jit(solution)/shard_map/move_weights/all_to_all | solution.py:203
  49.0 6.5 %collective-permute-start.1 = (bf16[1024,384]{1,0:T(8,128)(2,1)S(1)}, bf16[1024,384]{1,0:T(8,128)(2,1)S(1)}, u32[]{:S(2)}, u32[]{:S(2)}) collective-permute-start(bf16[1024,384]{1,0:T(8,128)(2,1)S(1)} %bitcast.43), channel_id=1, source_target_pairs={{0,32},{32,0},{1,33},{33,1},{2,34},{34,2},{3,35},{35,3},{4,36},{36... | collective-permute-start | bytes 2359304 | tf_op jit(solution)/shard_map/gather_tokens/ppermute | solution.py:207
  66.0 1.2 copy-start
  112.4 28.4 %all-to-all-start.3 = ((bf16[8,32,1152]{2,1,0:T(8,128)(2,1)}), bf16[8,32,1152]{2,1,0:T(8,128)(2,1)S(1)}, u32[]{:S(2)}, u32[]{:S(2)}) async-start(bf16[8,32,1152]{2,1,0:T(8,128)(2,1)} %tile.5), calls=%async_computation.3 | async-start | bytes 1179648 | tf_op jit(solution)/shard_map/spread_pre/all_to_all | solution.py:203
  140.8 0.8 copy-start.1
  152.6 13.6 %collective-permute-start.2 = (bf16[4,4,64,256]{3,2,1,0:T(8,128)(2,1)S(1)}, bf16[4,4,64,256]{3,2,1,0:T(8,128)(2,1)S(1)}, u32[]{:S(2)}, u32[]{:S(2)}) collective-permute-start(bf16[4,4,64,256]{3,2,1,0:T(8,128)(2,1)S(1)} %dynamic-slice_bitcast_fusion), channel_id=1, source_target_pairs={{0,32},{32,0},{1,33},{33,1},{2,34},{34,2},{3,35},{35,3},{4,36},{36... | collective-permute-start | bytes 1572872 | tf_op jit(solution)/shard_map/sum_dx/ppermute | solution.py:207
  168.2 14.0 %all-to-all-start.4 = ((bf16[16,64,256]{2,1,0:T(8,128)(2,1)}), bf16[16,64,256]{2,1,0:T(8,128)(2,1)S(1)}, u32[]{:S(2)}, u32[]{:S(2)}) async-start(bf16[16,64,256]{2,1,0:T(8,128)(2,1)} %bitcast.12), calls=%async_computation.4 | async-start | bytes 1048576 | tf_op jit(solution)/shard_map/sum_dx/all_to_all | solution.py:203
  182.2 21.2 %all-to-all-start.5 = ((bf16[16,3,40,384]{3,2,1,0:T(8,128)(2,1)}), bf16[16,3,40,384]{3,2,1,0:T(8,128)(2,1)S(1)}, u32[]{:S(2)}, u32[]{:S(2)}) async-start(bf16[16,3,40,384]{3,2,1,0:T(8,128)(2,1)} %bitcast.42), calls=%async_computation.5 | async-start | bytes 2949120 | tf_op jit(solution)/shard_map/return_grads/all_to_all | solution.py:203
  185.8 13.2 %collective-permute-start.3 = (bf16[32,256]{1,0:T(8,128)(2,1)S(1)}, bf16[32,256]{1,0:T(8,128)(2,1)S(1)}, u32[]{:S(2)}, u32[]{:S(2)}) collective-permute-start(bf16[32,256]{1,0:T(8,128)(2,1)S(1)} %dynamic-slice_convert_fusion), channel_id=1, source_target_pairs={{0,64},{64,0},{1,65},{65,1},{2,66},{66,2},{3,67},{67,3},{4,68},{68... | collective-permute-start | bytes 49160 | tf_op jit(solution)/shard_map/sum_dx/ppermute | solution.py:207
  199.0 0.6 copy-start.5

commit v3 on v2

v3 whole, which is shorter than its diff:
```python
import jax
import jax.numpy as jnp
from jax import lax
from jax.experimental import pallas as pl
from jax.experimental.pallas import tpu as pltpu
from jax.sharding import Mesh, PartitionSpec as P

DP = ("x", "zh", "core")
EX = ("zq", "zp", "y")
GROUP = ("zp", "y")
BLK = 16
TOP = 6
CAP = 8
EXPERTS = 16
DSH = 160
FSH = 96
SHARD = 32
TOKENS = 512
BLOCKS = TOKENS // BLK
LANES = 128
NG = 8
NE = EXPERTS // NG
NX = 4
SLOTS = BLOCKS * CAP
HALF = TOKENS // 2
HSLOTS = SLOTS // 2
Q = DSH // 4
STEP = Q + 8
WIDE = 4 * STEP
COLS = 2 * WIDE
IDS_AT = Q
PROBS_AT = STEP + Q
TRIO = 3 * FSH
PACK = 2 * NE * TRIO
PAIR = 2 * LANES
VMEM = 56 * 1024 * 1024
BF16 = jnp.bfloat16
F32 = jnp.float32


def iota(shape, dim):
    return lax.broadcasted_iota(jnp.int32, shape, dim)


def dot(a, b):
    return jnp.dot(a, b, preferred_element_type=F32)


def dot_dims(a, b, left, right):
    return lax.dot_general(a, b, (((left,), (right,)), ((), ())), preferred_element_type=F32)


def feature_of(column):
    s = sum(jnp.where(column >= i * STEP, 1, 0) for i in range(1, 4))
    q = column - s * STEP
    return jnp.where((q < Q) & (column >= 0) & (column < WIDE), 4 * q + s, -1)


def ones(mask):
    return jnp.where(mask, 1.0, 0.0).astype(BF16)


def prepare_kernel(stash_ref, scale_ref, dy_ref, ids_ref, probs_ref, out_ref):
    scale = scale_ref[...]
    factor = jnp.where(scale == -2, 0.25, jnp.where(scale == -1, 0.5, jnp.where(scale == 0, 1.0, 2.0)))
    per = DSH // scale.shape[0]
    shape = (scale.shape[0], DSH)
    first = iota(shape, 0) * per
    expand = ones((iota(shape, 1) >= first) & (iota(shape, 1) < first + per))
    x = (stash_ref[...].astype(F32) * dot_dims(factor.astype(BF16), expand, 0, 0)).astype(BF16)
    row, column = iota((DSH, COLS), 0), iota((DSH, COLS), 1)
    out = dot(x, ones(row == feature_of(column)))
    out = out + dot(dy_ref[...], ones(row == feature_of(column - WIDE)))
    row, column = iota((TOP, COLS), 0), iota((TOP, COLS), 1)
    out = out + dot_dims(ids_ref[...].astype(F32).astype(BF16), ones(row == column - IDS_AT), 0, 0)
    out = out + dot_dims(probs_ref[...], ones(row == column - PROBS_AT), 0, 0)
    out_ref[...] = out.astype(BF16)


def forward_kernel(me_ref, x_ref, w_ref, give_ref, keep_ref, xs_ref, ds_ref, wx_ref, gate_ref, slot_ref,
                   pick_ref, wd_ref, pre_ref):
    first = me_ref[0] * NE
    head = x_ref[:, :, 0].reshape(TOKENS, COLS)[:, :LANES].astype(F32)
    ids = head[:, IDS_AT:IDS_AT + TOP]
    probs = head[:, PROBS_AT:PROBS_AT + TOP]
    lane = iota((TOKENS, LANES), 1)
    hit = jnp.zeros((TOKENS, LANES), F32)
    prob = jnp.zeros((TOKENS, LANES), F32)
    for k in range(TOP):
        same = ids[:, k:k + 1] == (lane + first).astype(F32)
        hit = jnp.where(same, 1.0, hit)
        prob = jnp.where(same, probs[:, k:k + 1], prob)
    hit = jnp.where(lane < NE, hit, 0.0)
    row, column = iota((HALF, HALF), 0), iota((HALF, HALF), 1)
    before = ones((column < row) & (column >= row - row % BLK))
    block = (iota((HALF, LANES), 0) // BLK).astype(F32)
    row = iota((HSLOTS, HALF), 0).astype(F32)
    for h in range(2):
        at = slice(h * HALF, (h + 1) * HALF)
        place = dot(before, hit[at].astype(BF16))
        slot = jnp.where(hit[at] > 0.5, block * CAP + place, -1.0)
        slot_ref[at, :] = jnp.where(lane[at] < NE, slot, head[at])
        slot_t = slot.T
        for e in range(NE):
            pick_ref[h, e * HSLOTS:(e + 1) * HSLOTS, :] = ones(row == slot_t[e:e + 1, :])
        gate = dot(pick_ref[h], prob[at].astype(BF16))
        for e in range(NE):
            gate_ref[e, h * HSLOTS:(h + 1) * HSLOTS, :] = gate[e * HSLOTS:(e + 1) * HSLOTS]
    for g in range(NG):
        for h in range(2):
            x = dot(pick_ref[h], x_ref[h, :, g, :, :WIDE].reshape(HALF, WIDE)).astype(BF16)
            dy = dot(pick_ref[h], x_ref[h, :, g, :, WIDE:].reshape(HALF, WIDE)).astype(BF16)
            for e in range(NE):
                at = slice(h * HSLOTS, (h + 1) * HSLOTS)
                xs_ref[g, e, at, :] = x[e * HSLOTS:(e + 1) * HSLOTS]
                ds_ref[g, e, at, :] = dy[e * HSLOTS:(e + 1) * HSLOTS]
    low = jnp.zeros((STEP - Q, FSH), F32)
    side = jnp.zeros((STEP, LANES - FSH), F32)
    for g in range(NG):
        for e in range(NE):
            for i in range(3):
                w = w_ref[g, e, i].astype(F32)
                for s in range(4):
                    piece = jnp.concatenate([w[:, s * FSH:(s + 1) * FSH], low], axis=0)
                    piece = jnp.concatenate([piece, side], axis=1).astype(BF16)
                    if i < 2:
                        wx_ref[g, s * STEP:(s + 1) * STEP, e * PAIR + i * LANES:e * PAIR + (i + 1) * LANES] = piece
                    else:
                        wd_ref[g, s * STEP:(s + 1) * STEP, e * LANES:(e + 1) * LANES] = piece
    for e in range(NE):
        ab = jnp.zeros((SLOTS, PAIR), F32)
        back = jnp.zeros((SLOTS, LANES), F32)
        for g in range(NG):
            ab = ab + dot(xs_ref[g, e], wx_ref[g, :, e * PAIR:(e + 1) * PAIR])
            back = back + dot(ds_ref[g, e], wd_ref[g, :, e * LANES:(e + 1) * LANES])
        trio = jnp.concatenate([ab[:, :FSH], ab[:, LANES:LANES + FSH], back[:, :FSH]], axis=1)
        for h in range(2):
            unit = 2 * e + h
            pre_ref[:, unit * TRIO:(unit + 1) * TRIO] = trio[h * HSLOTS:(h + 1) * HSLOTS]
    bit, half = me_ref[1], HSLOTS // 2
    keep_ref[...] = pre_ref[pl.ds(pl.multiple_of(bit * half, half), half), :]
    give_ref[...] = pre_ref[pl.ds(pl.multiple_of((1 - bit) * half, half), half), :].astype(BF16)


def middle_kernel(me_ref, pre_ref, wx_ref, gate_ref, slot_ref, d_ref, keep_ref, give_ref, spread_ref, tail_ref):
    first = me_ref[0] * NE
    side = jnp.zeros((HSLOTS, LANES - FSH), F32)
    lane = iota((HSLOTS, LANES - FSH), 1)
    slots = iota((HALF, HSLOTS), 1).astype(F32)
    wide = iota((HALF, LANES), 1)
    for h in range(2):
        info = slot_ref[h * HALF:(h + 1) * HALF, :]
        tail = jnp.zeros((HALF, LANES), F32)
        for e in range(NE):
            base = (2 * e + h) * TRIO
            pre = pre_ref[:, base:base + TRIO].astype(F32)
            a, b, back = (pre[:, i * FSH:(i + 1) * FSH] for i in range(3))
            gate = gate_ref[e, h * HSLOTS:(h + 1) * HSLOTS, e:e + 1]
            sig = jax.nn.sigmoid(a)
            act = a * sig
            hidden = act * b
            dh = gate * back
            d_gate = dh * b * sig * (1.0 + a * (1.0 - sig))
            prob = jnp.sum(hidden * back, axis=1, keepdims=True)
            prob = jnp.where(lane == 0, prob, 0.0)
            d = jnp.concatenate([d_gate, prob, dh * act, side, gate * hidden, side], axis=1).astype(BF16)
            d_ref[e, h * HSLOTS:(h + 1) * HSLOTS, :] = d
            spread = dot(ones(slots == info[:, e:e + 1]), d[:, :PAIR])
            spread_ref[h, :, e * PAIR:(e + 1) * PAIR] = spread.astype(BF16)
            mine = info == (first + e).astype(F32)
            mine = mine & (wide >= IDS_AT) & (wide < IDS_AT + TOP)
            tail = jnp.where(mine, spread[:, FSH:FSH + 1], tail)
        tail_ref[h] = tail
    none = jnp.zeros((HALF, WIDE - LANES), F32)
    for out_ref, h in ((keep_ref, me_ref[1]), (give_ref, 1 - me_ref[1])):
        tail = jnp.concatenate([tail_ref[h], none], axis=1)
        for g in range(NG):
            dx = dot_dims(spread_ref[h], wx_ref[g], 1, 1) + tail
            dx = dx.reshape(NX, 2, SHARD, WIDE)
            dx = jnp.concatenate([dx[:, 0], dx[:, 1]], axis=2)
            out_ref[:, g] = dx.astype(BF16)


def weight_kernel(xs_ref, ds_ref, d_ref, out_ref):
    for e in range(NE):
        for g in range(NG):
            both = dot_dims(xs_ref[g, e], d_ref[e, :, :PAIR], 0, 0)
            down = dot_dims(ds_ref[g, e], d_ref[e, :, PAIR:], 0, 0)
            for i, (grad, base) in enumerate(((both, 0), (both, LANES), (down, 0))):
                pieces = [grad[s * STEP:s * STEP + Q, base:base + FSH] for s in range(4)]
                out_ref[g, e, i] = jnp.concatenate(pieces, axis=1).astype(BF16)


def finish_kernel(dx_ref, got_ref, in_ref, probs_ref):
    total = dx_ref[...] + got_ref[...].astype(F32)
    row, column = iota((WIDE, DSH), 0), iota((WIDE, DSH), 1)
    order = ones(feature_of(row) == column)
    in_ref[...] = dot(total.astype(BF16), order).astype(BF16)
    probs_ref[...] = total[:, IDS_AT:IDS_AT + TOP]


def call(kernel, outs, args, scratch=(), scalar=False):
    vmem = pl.BlockSpec(memory_space=pltpu.VMEM)
    specs = [vmem] * len(args)
    if scalar:
        specs[0] = pl.BlockSpec(memory_space=pltpu.SMEM)
    return pl.pallas_call(
        kernel,
        out_shape=[jax.ShapeDtypeStruct(shape, dtype) for shape, dtype in outs],
        in_specs=specs,
        out_specs=[vmem] * len(outs),
        scratch_shapes=[pltpu.VMEM(shape, dtype) for shape, dtype in scratch],
        compiler_params=pltpu.CompilerParams(vmem_limit_bytes=VMEM),
    )(*args)


def exchange(value, axis):
    return lax.all_to_all(value, axis, split_axis=0, concat_axis=0, tiled=True)


def swap(value, axis):
    return lax.ppermute(value, axis, [(0, 1), (1, 0)])


def flip(value, axis, bit):
    return lax.ppermute(value, axis, [(i, i ^ bit) for i in range(lax.axis_size(axis))])


def local(stash, scale_exp, grad_out, route_ids, route_probs, w_gate, w_up, w_down):
    group = lax.axis_index(GROUP).astype(jnp.int32)
    core = lax.axis_index("core").astype(jnp.int32)
    zh = lax.axis_index("zh")
    zq = lax.axis_index("zq").astype(jnp.int32)
    near, far = zq % 2, zq // 2
    small = [v.T for v in (scale_exp, route_ids, route_probs)]
    (xin,) = call(prepare_kernel, [((SHARD, COLS), BF16)], (stash, small[0], grad_out, small[1], small[2]))
    other = swap(xin, "zh")
    with jax.named_scope("move_weights"):
        tiles = [w.reshape(EXPERTS, 1, Q, 4 * FSH) for w in (w_gate, w_up, w_down)]
        weights = exchange(jnp.concatenate(tiles, axis=1), GROUP)
        weights = weights.reshape(NG, NE, 3, Q, 4 * FSH)
    other, weights = lax.optimization_barrier((other, weights))
    with jax.named_scope("gather_tokens"):
        xin = jnp.where(zh == 0, jnp.concatenate([xin, other]), jnp.concatenate([other, xin]))
        xin = exchange(jnp.tile(xin, (NX * NG, 1)), ("x",) + GROUP)
        other = swap(xin, "core")
        xin = jnp.where(core == 0, jnp.stack([xin, other]), jnp.stack([other, xin]))
        xin = xin.reshape(2, NX, NG, 2 * SHARD, COLS)
    give, keep, xs, ds, wx, gate, slot = call(
        forward_kernel,
        [((HSLOTS // 2, PACK), BF16), ((HSLOTS // 2, PACK), F32), ((NG, NE, SLOTS, WIDE), BF16),
         ((NG, NE, SLOTS, WIDE), BF16), ((NG, WIDE, NE * PAIR), BF16), ((NE, SLOTS, LANES), F32),
         ((TOKENS, LANES), F32)],
        (jnp.stack([group, near]), xin, weights),
        [((2, HALF, HALF), BF16), ((NG, WIDE, NE * LANES), BF16), ((HSLOTS, PACK), F32)],
        True)
    rows = HSLOTS // 4
    with jax.named_scope("sum_pre"):
        pre = keep + flip(give, "zq", 1).astype(F32)
        keep = lax.dynamic_slice_in_dim(pre, far * rows, rows, 0)
        give = lax.dynamic_slice_in_dim(pre, (1 - far) * rows, rows, 0).astype(BF16)
        pre = (keep + flip(give, "zq", 2).astype(F32)).astype(BF16)
    with jax.named_scope("spread_pre"):
        other = flip(pre, "zq", 2)
        pre = jnp.where(far == 0, jnp.concatenate([pre, other]), jnp.concatenate([other, pre]))
        other = flip(pre, "zq", 1)
        pre = jnp.where(near == 0, jnp.concatenate([pre, other]), jnp.concatenate([other, pre]))
    d, keep, give = call(
        middle_kernel,
        [((NE, SLOTS, 3 * LANES), BF16), ((NX, NG, SHARD, COLS), BF16), ((NX, NG, SHARD, COLS), BF16)],
        (jnp.stack([group, core]), pre, wx, gate, slot),
        [((2, HALF, NE * PAIR), BF16), ((2, HALF, LANES), F32)],
        True)
    (grads,) = call(weight_kernel, [((NG, NE, 3, Q, 4 * FSH), BF16)], (xs, ds, d))
    with jax.named_scope("sum_dx"):
        dx = (keep.astype(F32) + swap(give, "core").astype(F32)).astype(BF16)
        dx = exchange(dx.reshape(NX * NG, SHARD, COLS), ("x",) + GROUP)
        dx = jnp.sum(dx.astype(F32), axis=0)
        low, high = dx[:, :WIDE], dx[:, WIDE:]
        got = swap(jnp.where(zh == 0, high, low).astype(BF16), "zh")
        keep = jnp.where(zh == 0, low, high)
    with jax.named_scope("return_grads"):
        grads = exchange(grads.reshape(EXPERTS, 3, Q, 4 * FSH), GROUP)
        grads = [grads[:, i].reshape(w_gate.shape) for i in range(3)]
    grad_in, grad_probs = call(finish_kernel, [((SHARD, DSH), BF16), ((SHARD, TOP), F32)], (keep, got))
    return (grad_in, grad_probs, *grads)


def solution(mesh):
    fine = Mesh(mesh.devices.reshape(4, 2, 2, 4, 2, 4), DP + EX)
    weight = P(None, DP + EX)
    in_specs = (P(DP, EX), P(DP, EX), P(DP, EX), P(DP, None), P(DP, None), weight, weight, weight)
    out_specs = (P(DP, EX), P(DP, None), weight, weight, weight)
    return jax.shard_map(local, mesh=fine, in_specs=in_specs, out_specs=out_specs, check_vma=False)
```

time: 208 us -> 193 us (0.928)
  waiting for transfers between devices: 57.7 us -> 71.5 us
  starting transfers between devices: 64.5 us -> 52.9 us
  blocking collectives: 36.6 us -> 26.3 us
  local copies, waits for them, and re-layouts: 14.6 us -> 7.21 us
  Pallas kernels: 26 us -> 21.4 us
  other arithmetic: 5.77 us -> 10.2 us
    all_to_all x5 -> x3, waiting for transfers between devices: 48.2 us -> 8.16 us  [exchange(): return lax.all_to_all(value, axis, split_axis=0, concat_axis=0, tiled=True)]
    ppermute x0 -> x4, waiting for transfers between devices: none -> 32.8 us  [flip(): lax.ppermute(value, axis, [(i, i ^ bit) for i in range(lax.axis_size(axis...]
    ppermute x4, waiting for transfers between devices: 9.5 us -> 30.6 us  [swap(): return lax.ppermute(value, axis, [(0, 1), (1, 0)])]
    ppermute x4, starting transfers between devices: 40.9 us -> 26.5 us  [swap(): return lax.ppermute(value, axis, [(0, 1), (1, 0)])]
    ppermute x0 -> x4, starting transfers between devices: none -> 12.5 us  [flip(): lax.ppermute(value, axis, [(i, i ^ bit) for i in range(lax.axis_size(axis...]
    all_to_all x1, blocking collectives: 36.6 us -> 26.3 us  [exchange(): return lax.all_to_all(value, axis, split_axis=0, concat_axis=0, tiled=True)]
    all_to_all x5 -> x3, starting transfers between devices: 23.6 us -> 13.9 us  [exchange(): return lax.all_to_all(value, axis, split_axis=0, concat_axis=0, tiled=True)]
    pallas_call x5, Pallas kernels: 26 us -> 21.4 us  [call(): pl.pallas_call(kernel, out_shape=[jax.ShapeDtypeStruct(shape, dtype) for...]
  transfers between devices with their start and end apart: 9 -> 11, of which waited for: 9 -> 9; matrix products, arithmetic and copies ran while one was open for 2% -> 2% of each run, Pallas kernels for 3% -> 4%
where the time goes in v3:
time: 193 us; the launch traced here: 190 us
  waiting for transfers between devices  71.5 us (37%)
  starting transfers between devices  52.9 us (27%)
  blocking collectives  26.3 us (14%)
  Pallas kernels  21.4 us (11%)
  other arithmetic  10.2 us (5%)
  local copies, waits for them, and re-layouts  7.21 us (4%)
    ppermute x4, waiting for transfers between devices, flip(): lax.ppermute(value, axis, [(i, i ^ bit) for i in range(lax.axis_size(axis...  32.8 us
    ppermute x4, waiting for transfers between devices, swap(): return lax.ppermute(value, axis, [(0, 1), (1, 0)])  30.6 us
    ppermute x4, starting transfers between devices, swap(): return lax.ppermute(value, axis, [(0, 1), (1, 0)])  26.5 us
    all_to_all x1, blocking collectives, exchange(): return lax.all_to_all(value, axis, split_axis=0, concat_axis=0, tiled=True)  26.3 us
    pallas_call x5, Pallas kernels, call(): pl.pallas_call(kernel, out_shape=[jax.ShapeDtypeStruct(shape, dtype) for...  21.4 us
    all_to_all x3, starting transfers between devices, exchange(): return lax.all_to_all(value, axis, split_axis=0, concat_axis=0, tiled=True)  13.9 us
    ppermute x4, starting transfers between devices, flip(): lax.ppermute(value, axis, [(i, i ^ bit) for i in range(lax.axis_size(axis...  12.5 us
    all_to_all x3, waiting for transfers between devices, exchange(): return lax.all_to_all(value, axis, split_axis=0, concat_axis=0, tiled=True)  8.16 us
  transfers between devices with their start and end apart: 11, of which 9 were waited for; matrix products, arithmetic and copies ran while one was open for 2% of the time, Pallas kernels for 4%

profile of v3, /device:TPU:1, one launch (start us, length us, event | category | flops | bytes accessed | tf_op | source)
XLA Modules:
  0.0 190.4 jit_solution(5744531510550068998)
XLA Ops:
  0.6 0.0 copy-start.1
  0.6 1.1 copy.17
  1.8 1.1 copy.18
  2.9 0.0 copy-done.1
  2.9 0.1 copy.19
  3.0 1.3 pad_maximum_fusion
  4.3 6.4 %all-to-all-start = ((bf16[16,3,40,384]{3,2,1,0:T(8,128)(2,1)}), bf16[16,3,40,384]{3,2,1,0:T(8,128)(2,1)S(1)}, u32[]{:S(2)}, u32[]{:S(2)}) async-start(bf16[16,3,40,384]{3,2,1,0:T(8,128)(2,1)} %pad_maximum_fusion), calls=%async_computation | async-start | bytes 2949120 | tf_op jit(solution)/shard_map/move_weights/all_to_all | solution.py:218
  10.7 1.7 shard_map.119
  12.4 14.5 %collective-permute-start = (bf16[32,384]{1,0:T(8,128)(2,1)}, bf16[32,384]{1,0:T(8,128)(2,1)S(1)}, u32[]{:S(2)}, u32[]{:S(2)}) collective-permute-start(bf16[32,384]{1,0:T(8,128)(2,1)} %shard_map.119), channel_id=1, source_target_pairs={{0,64},{64,0},{1,65},{65,1},{2,66},{66,2},{3,67},{67,3},{4,68},{68... | collective-permute-start | bytes 73736 | tf_op jit(solution)/shard_map/ppermute | solution.py:222
  26.9 13.6 %collective-permute-done = bf16[32,384]{1,0:T(8,128)(2,1)S(1)} collective-permute-done((bf16[32,384]{1,0:T(8,128)(2,1)}, bf16[32,384]{1,0:T(8,128)(2,1)S(1)}, u32[]{:S(2)}, u32[]{:S(2)}) %collective-permute-start) | collective-permute-done | bytes 24608 | tf_op jit(solution)/shard_map/ppermute | solution.py:222
  40.5 0.0 all-to-all-done
  40.5 0.0 copy-start
  40.5 0.8 maximum_select_fusion.3
  41.3 0.2 tile.2
  41.6 26.3 %all_to_all.24 = bf16[32,64,384]{2,1,0:T(8,128)(2,1)S(1)} all-to-all(bf16[32,64,384]{2,1,0:T(8,128)(2,1)S(1)} %tile.2), channel_id=1, replica_groups=mesh['x'=4,'zh'=2,'core'=2,'zq'=4,'zp'=2,'y'=4] {'x','zp','y'}, dimensions={0} | all-to-all | bytes 3145728 | tf_op jit(solution)/shard_map/gather_tokens/all_to_all | solution.py:218
  67.9 0.0 copy-done
  67.9 6.0 %collective-permute-start.1 = (bf16[2048,384]{1,0:T(8,128)(2,1)S(1)}, bf16[2048,384]{1,0:T(8,128)(2,1)S(1)}, u32[]{:S(2)}, u32[]{:S(2)}) collective-permute-start(bf16[2048,384]{1,0:T(8,128)(2,1)S(1)} %bitcast.39), channel_id=1, source_target_pairs={{0,32},{32,0},{1,33},{33,1},{2,34},{34,2},{3,35},{35,3},{4,36},{36... | collective-permute-start | bytes 4718600 | tf_op jit(solution)/shard_map/gather_tokens/ppermute | solution.py:222
  74.0 0.6 pad_add_fusion.1.me_ref
  74.6 2.4 %collective-permute-done.1 = bf16[2048,384]{1,0:T(8,128)(2,1)S(1)} collective-permute-done((bf16[2048,384]{1,0:T(8,128)(2,1)S(1)}, bf16[2048,384]{1,0:T(8,128)(2,1)S(1)}, u32[]{:S(2)}, u32[]{:S(2)}) %collective-permute-start.1) | collective-permute-done | bytes 1572896 | tf_op jit(solution)/shard_map/gather_tokens/ppermute | solution.py:222
  76.9 1.9 %maximum_select_fusion.x_ref = bf16[2,4,8,64,384]{4,3,2,1,0:T(8,128)(2,1)} fusion(bf16[1,4,8,64,384]{4,3,2,1,0:T(8,128)(2,1)S(1)} %bitcast.49, bf16[1,4,8,64,384]{4,3,2,1,0:T(8,128)(2,1)S(1)} %bitcast.40, pred[]{:T(512)S(6)} %eq.19), kind=kLoop, calls=%fused_computation | loop fusion | flops 4718592 | bytes 6291457 | tf_op jit(solution)/shard_map/gather_tokens/jit(_where)/select_n | solution.py:247
  78.9 7.5 %shard_map.120 = (bf16[64,1152]{1,0:T(8,128)(2,1)}, f32[64,1152]{1,0:T(8,128)}, bf16[8,2,256,192]{3,2,1,0:T(8,128)(2,1)}, bf16[8,2,256,192]{3,2,1,0:T(8,128)(2,1...) custom-call(s32[2]{0:T(128)} %pad_add_fusion.1.me_ref, ...), custom_call_target="tpu_custom_call" | custom-call | tf_op jit(solution)/shard_map/pallas_call | solution.py:207
  86.4 3.6 %collective-permute-start.2 = (bf16[64,1152]{1,0:T(8,128)(2,1)}, bf16[64,1152]{1,0:T(8,128)(2,1)S(1)}, u32[]{:S(2)}, u32[]{:S(2)}) collective-permute-start(bf16[64,1152]{1,0:T(8,128)(2,1)} %get-tuple-element.22), channel_id=1, source_target_pairs={{0,8},{8,0},{16,24},{24,16},{1,9},{9,1},{17,25},{25,17},{2,10},{10... | collective-permute-start | bytes 442376 | tf_op jit(solution)/shard_map/sum_pre/ppermute | solution.py:226
  90.0 7.9 %collective-permute-done.2 = bf16[64,1152]{1,0:T(8,128)(2,1)S(1)} collective-permute-done((bf16[64,1152]{1,0:T(8,128)(2,1)}, bf16[64,1152]{1,0:T(8,128)(2,1)S(1)}, u32[]{:S(2)}, u32[]{:S(2)}) %collective-permute-start.2) | collective-permute-done | bytes 147488 | tf_op jit(solution)/shard_map/sum_pre/ppermute | solution.py:226
  97.9 1.0 convert_add_fusion
  99.0 5.1 %collective-permute-start.3 = (bf16[32,1152]{1,0:T(8,128)(2,1)S(1)}, bf16[32,1152]{1,0:T(8,128)(2,1)S(1)}, u32[]{:S(2)}, u32[]{:S(2)}) collective-permute-start(bf16[32,1152]{1,0:T(8,128)(2,1)S(1)} %dynamic-slice_convert_fusion), channel_id=1, source_target_pairs={{0,16},{8,24},{16,0},{24,8},{1,17},{9,25},{17,1},{25,9},{2,18},{10... | collective-permute-start | bytes 221192 | tf_op jit(solution)/shard_map/sum_pre/ppermute | solution.py:226
  104.0 8.7 %collective-permute-done.3 = bf16[32,1152]{1,0:T(8,128)(2,1)S(1)} collective-permute-done((bf16[32,1152]{1,0:T(8,128)(2,1)S(1)}, bf16[32,1152]{1,0:T(8,128)(2,1)S(1)}, u32[]{:S(2)}, u32[]{:S(2)}) %collective-permute-start.3) | collective-permute-done | bytes 73760 | tf_op jit(solution)/shard_map/sum_pre/ppermute | solution.py:226
  112.7 1.9 %collective-permute-start.4 = (bf16[32,1152]{1,0:T(8,128)(2,1)S(1)}, bf16[32,1152]{1,0:T(8,128)(2,1)S(1)}, u32[]{:S(2)}, u32[]{:S(2)}) collective-permute-start(bf16[32,1152]{1,0:T(8,128)(2,1)S(1)} %add_convert_fusion.1), channel_id=1, source_target_pairs={{0,16},{8,24},{16,0},{24,8},{1,17},{9,25},{17,1},{25,9},{2,18},{10... | collective-permute-start | bytes 221192 | tf_op jit(solution)/shard_map/spread_pre/ppermute | solution.py:226
  114.6 9.1 %collective-permute-done.4 = bf16[32,1152]{1,0:T(8,128)(2,1)S(1)} collective-permute-done((bf16[32,1152]{1,0:T(8,128)(2,1)S(1)}, bf16[32,1152]{1,0:T(8,128)(2,1)S(1)}, u32[]{:S(2)}, u32[]{:S(2)}) %collective-permute-start.4) | collective-permute-done | bytes 73760 | tf_op jit(solution)/shard_map/spread_pre/ppermute | solution.py:226
  123.8 1.9 %collective-permute-start.5 = (bf16[64,1152]{1,0:T(8,128)(2,1)S(1)}, bf16[64,1152]{1,0:T(8,128)(2,1)S(1)}, u32[]{:S(2)}, u32[]{:S(2)}) collective-permute-start(bf16[64,1152]{1,0:T(8,128)(2,1)S(1)} %maximum_select_fusion.2), channel_id=1, source_target_pairs={{0,8},{8,0},{16,24},{24,16},{1,9},{9,1},{17,25},{25,17},{2,10},{10... | collective-permute-start | bytes 442376 | tf_op jit(solution)/shard_map/spread_pre/ppermute | solution.py:226
  125.7 0.6 pad_add_fusion.me_ref
  126.3 7.1 %collective-permute-done.5 = bf16[64,1152]{1,0:T(8,128)(2,1)S(1)} collective-permute-done((bf16[64,1152]{1,0:T(8,128)(2,1)S(1)}, bf16[64,1152]{1,0:T(8,128)(2,1)S(1)}, u32[]{:S(2)}, u32[]{:S(2)}) %collective-permute-start.5) | collective-permute-done | bytes 147488 | tf_op jit(solution)/shard_map/spread_pre/ppermute | solution.py:226
  133.4 0.8 maximum_select_fusion.1.pre_ref
  134.2 5.6 %shard_map.121 = (bf16[2,256,384]{2,1,0:T(8,128)(2,1)}, bf16[4,8,32,384]{3,2,1,0:T(8,128)(2,1)}, bf16[4,8,32,384]{3,2,1,0:T(8,128)(2,1)}) custom-call(s32[2]{0:T(128)} %pad_add_fusion.me_ref, bf16[128,1152]{1,0:T(8,128)(2,1)} %maximum_select_fusion.1.pre_ref, bf16[8,192,512]{2,1,0:T(8,128)(2,1)} %get-tuple-element.23.wx_ref, ...), custom_call_target="tpu_custom_call" | custom-call | tf_op jit(solution)/shard_map/pallas_call | solution.py:207
  139.8 2.4 %collective-permute-start.6 = (bf16[4,8,32,384]{3,2,1,0:T(8,128)(2,1)}, bf16[4,8,32,384]{3,2,1,0:T(8,128)(2,1)S(1)}, u32[]{:S(2)}, u32[]{:S(2)}) collective-permute-start(bf16[4,8,32,384]{3,2,1,0:T(8,128)(2,1)} %get-tuple-element.27), channel_id=1, source_target_pairs={{0,32},{32,0},{1,33},{33,1},{2,34},{34,2},{3,35},{35,3},{4,36},{36... | collective-permute-start | bytes 2359304 | tf_op jit(solution)/shard_map/sum_dx/ppermute | solution.py:222
  142.1 2.1 %collective-permute-done.6 = bf16[4,8,32,384]{3,2,1,0:T(8,128)(2,1)S(1)} collective-permute-done((bf16[4,8,32,384]{3,2,1,0:T(8,128)(2,1)}, bf16[4,8,32,384]{3,2,1,0:T(8,128)(2,1)S(1)}, u32[]{:S(2)}, u32[]{:S(2)}) %collective-permute-start.6) | collective-permute-done | bytes 786464 | tf_op jit(solution)/shard_map/sum_dx/ppermute | solution.py:222
  144.2 2.2 %add_convert_fusion = bf16[4,8,32,384]{3,2,1,0:T(8,128)(2,1)} fusion(bf16[4,8,32,384]{3,2,1,0:T(8,128)(2,1)S(1)} %collective-permute-done.6, bf16[4,8,32,384]{3,2,1,0:T(8,128)(2,1)} %get-tuple-element.26), kind=kLoop, calls=%fused_computation.2 | loop fusion | flops 1572864 | bytes 2359296 | tf_op jit(solution)/shard_map/sum_dx/convert_element_type | solution.py:276
  146.5 3.9 %all-to-all-start.2 = ((bf16[32,32,384]{2,1,0:T(8,128)(2,1)}), bf16[32,32,384]{2,1,0:T(8,128)(2,1)S(1)}, u32[]{:S(2)}, u32[]{:S(2)}) async-start(bf16[32,32,384]{2,1,0:T(8,128)(2,1)} %bitcast.13), calls=%async_computation.2 | async-start | bytes 1572864 | tf_op jit(solution)/shard_map/sum_dx/all_to_all | solution.py:218
  150.4 5.1 %shard_map.123 = bf16[8,2,3,40,384]{4,3,2,1,0:T(8,128)(2,1)} custom-call(bf16[8,2,256,192]{3,2,1,0:T(8,128)(2,1)} %get-tuple-element.30.xs_ref, bf16[8,2,256,192]{3,2,1,0:T(8,128)(2,1)} %get-tuple-element.31.ds_ref, bf16[2,256,384]{2,1,0:T(8,128)(2,1)} %get-tuple-element.32.d_ref), custom_call_target="tpu_custom_call" | custom-call | tf_op jit(solution)/shard_map/pallas_call | solution.py:207
  155.5 8.2 %all-to-all-done.2 = bf16[32,32,384]{2,1,0:T(8,128)(2,1)S(1)} async-done(((bf16[32,32,384]{2,1,0:T(8,128)(2,1)}), bf16[32,32,384]{2,1,0:T(8,128)(2,1)S(1)}, u32[]{:S(2)}, u32[]{:S(2)}) %all-to-all-start.2) | async-done | bytes 786464 | tf_op jit(solution)/shard_map/sum_dx/all_to_all | solution.py:218
  163.7 3.6 %all-to-all-start.3 = ((bf16[16,3,40,384]{3,2,1,0:T(8,128)(2,1)}), bf16[16,3,40,384]{3,2,1,0:T(8,128)(2,1)S(1)}, u32[]{:S(2)}, u32[]{:S(2)}) async-start(bf16[16,3,40,384]{3,2,1,0:T(8,128)(2,1)} %bitcast.42), calls=%async_computation.3 | async-start | bytes 2949120 | tf_op jit(solution)/shard_map/return_grads/all_to_all | solution.py:218
  167.2 0.1 convert_reduce_fusion
  167.4 0.1 select_convert_fusion
  167.4 3.6 %collective-permute-start.7 = (bf16[32,192]{1,0:T(8,128)(2,1)S(1)}, bf16[32,192]{1,0:T(8,128)(2,1)S(1)}, u32[]{:S(2)}, u32[]{:S(2)}) collective-permute-start(bf16[32,192]{1,0:T(8,128)(2,1)S(1)} %select_convert_fusion), channel_id=1, source_target_pairs={{0,64},{64,0},{1,65},{65,1},{2,66},{66,2},{3,67},{67,3},{4,68},{68... | collective-permute-start | bytes 36872 | tf_op jit(solution)/shard_map/sum_dx/ppermute | solution.py:222
  171.0 0.7 slice_select_fusion.dx_ref
  171.7 12.5 %collective-permute-done.7.got_ref = bf16[32,192]{1,0:T(8,128)(2,1)S(1)} collective-permute-done((bf16[32,192]{1,0:T(8,128)(2,1)S(1)}, bf16[32,192]{1,0:T(8,128)(2,1)S(1)}, u32[]{:S(2)}, u32[]{:S(2)}) %collective-permute-start.7) | collective-permute-done | bytes 12320 | tf_op jit(solution)/shard_map/sum_dx/ppermute | solution.py:222
  184.2 0.0 copy-start.2
  184.2 0.6 copy-done.2
  184.8 1.5 shard_map.122
  186.4 1.4 copy.16
  187.7 0.0 all-to-all-done.3
  187.7 0.2 fusion
  187.9 0.8 copy.22
  188.7 0.8 copy.21
  189.6 0.8 copy.20
  (3 shorter events, 0.1 us)
Async XLA Ops:
  0.6 2.3 %copy-start.1 = (bf16[16,15360]{1,0:T(8,128)(2,1)S(1)}, bf16[16,15360]{1,0:T(8,128)(2,1)}, u32[]{:S(2)}) copy-start(bf16[16,15360]{1,0:T(8,128)(2,1)} %param.15) | copy-start | bytes 1474564
  4.3 36.2 %all-to-all-start = ((bf16[16,3,40,384]{3,2,1,0:T(8,128)(2,1)}), bf16[16,3,40,384]{3,2,1,0:T(8,128)(2,1)S(1)}, u32[]{:S(2)}, u32[]{:S(2)}) async-start(bf16[16,3,40,384]{3,2,1,0:T(8,128)(2,1)} %pad_maximum_fusion), calls=%async_computation | async-start | bytes 2949120 | tf_op jit(solution)/shard_map/move_weights/all_to_all | solution.py:218
  12.4 28.1 %collective-permute-start = (bf16[32,384]{1,0:T(8,128)(2,1)}, bf16[32,384]{1,0:T(8,128)(2,1)S(1)}, u32[]{:S(2)}, u32[]{:S(2)}) collective-permute-start(bf16[32,384]{1,0:T(8,128)(2,1)} %shard_map.119), channel_id=1, source_target_pairs={{0,64},{64,0},{1,65},{65,1},{2,66},{66,2},{3,67},{67,3},{4,68},{68... | collective-permute-start | bytes 73736 | tf_op jit(solution)/shard_map/ppermute | solution.py:222
  40.5 27.4 %copy-start = (bf16[16,3,40,384]{3,2,1,0:T(8,128)(2,1)}, bf16[16,3,40,384]{3,2,1,0:T(8,128)(2,1)S(1)}, u32[]{:S(2)}) copy-start(bf16[16,3,40,384]{3,2,1,0:T(8,128)(2,1)S(1)} %all-to-all-done) | copy-start | bytes 4423684
  67.9 9.0 %collective-permute-start.1 = (bf16[2048,384]{1,0:T(8,128)(2,1)S(1)}, bf16[2048,384]{1,0:T(8,128)(2,1)S(1)}, u32[]{:S(2)}, u32[]{:S(2)}) collective-permute-start(bf16[2048,384]{1,0:T(8,128)(2,1)S(1)} %bitcast.39), channel_id=1, source_target_pairs={{0,32},{32,0},{1,33},{33,1},{2,34},{34,2},{3,35},{35,3},{4,36},{36... | collective-permute-start | bytes 4718600 | tf_op jit(solution)/shard_map/gather_tokens/ppermute | solution.py:222
  86.4 11.6 %collective-permute-start.2 = (bf16[64,1152]{1,0:T(8,128)(2,1)}, bf16[64,1152]{1,0:T(8,128)(2,1)S(1)}, u32[]{:S(2)}, u32[]{:S(2)}) collective-permute-start(bf16[64,1152]{1,0:T(8,128)(2,1)} %get-tuple-element.22), channel_id=1, source_target_pairs={{0,8},{8,0},{16,24},{24,16},{1,9},{9,1},{17,25},{25,17},{2,10},{10... | collective-permute-start | bytes 442376 | tf_op jit(solution)/shard_map/sum_pre/ppermute | solution.py:226
  99.0 13.7 %collective-permute-start.3 = (bf16[32,1152]{1,0:T(8,128)(2,1)S(1)}, bf16[32,1152]{1,0:T(8,128)(2,1)S(1)}, u32[]{:S(2)}, u32[]{:S(2)}) collective-permute-start(bf16[32,1152]{1,0:T(8,128)(2,1)S(1)} %dynamic-slice_convert_fusion), channel_id=1, source_target_pairs={{0,16},{8,24},{16,0},{24,8},{1,17},{9,25},{17,1},{25,9},{2,18},{10... | collective-permute-start | bytes 221192 | tf_op jit(solution)/shard_map/sum_pre/ppermute | solution.py:226
  112.7 11.0 %collective-permute-start.4 = (bf16[32,1152]{1,0:T(8,128)(2,1)S(1)}, bf16[32,1152]{1,0:T(8,128)(2,1)S(1)}, u32[]{:S(2)}, u32[]{:S(2)}) collective-permute-start(bf16[32,1152]{1,0:T(8,128)(2,1)S(1)} %add_convert_fusion.1), channel_id=1, source_target_pairs={{0,16},{8,24},{16,0},{24,8},{1,17},{9,25},{17,1},{25,9},{2,18},{10... | collective-permute-start | bytes 221192 | tf_op jit(solution)/shard_map/spread_pre/ppermute | solution.py:226
  123.8 9.6 %collective-permute-start.5 = (bf16[64,1152]{1,0:T(8,128)(2,1)S(1)}, bf16[64,1152]{1,0:T(8,128)(2,1)S(1)}, u32[]{:S(2)}, u32[]{:S(2)}) collective-permute-start(bf16[64,1152]{1,0:T(8,128)(2,1)S(1)} %maximum_select_fusion.2), channel_id=1, source_target_pairs={{0,8},{8,0},{16,24},{24,16},{1,9},{9,1},{17,25},{25,17},{2,10},{10... | collective-permute-start | bytes 442376 | tf_op jit(solution)/shard_map/spread_pre/ppermute | solution.py:226
  139.8 4.5 %collective-permute-start.6 = (bf16[4,8,32,384]{3,2,1,0:T(8,128)(2,1)}, bf16[4,8,32,384]{3,2,1,0:T(8,128)(2,1)S(1)}, u32[]{:S(2)}, u32[]{:S(2)}) collective-permute-start(bf16[4,8,32,384]{3,2,1,0:T(8,128)(2,1)} %get-tuple-element.27), channel_id=1, source_target_pairs={{0,32},{32,0},{1,33},{33,1},{2,34},{34,2},{3,35},{35,3},{4,36},{36... | collective-permute-start | bytes 2359304 | tf_op jit(solution)/shard_map/sum_dx/ppermute | solution.py:222
  146.5 17.2 %all-to-all-start.2 = ((bf16[32,32,384]{2,1,0:T(8,128)(2,1)}), bf16[32,32,384]{2,1,0:T(8,128)(2,1)S(1)}, u32[]{:S(2)}, u32[]{:S(2)}) async-start(bf16[32,32,384]{2,1,0:T(8,128)(2,1)} %bitcast.13), calls=%async_computation.2 | async-start | bytes 1572864 | tf_op jit(solution)/shard_map/sum_dx/all_to_all | solution.py:218
  163.7 24.1 %all-to-all-start.3 = ((bf16[16,3,40,384]{3,2,1,0:T(8,128)(2,1)}), bf16[16,3,40,384]{3,2,1,0:T(8,128)(2,1)S(1)}, u32[]{:S(2)}, u32[]{:S(2)}) async-start(bf16[16,3,40,384]{3,2,1,0:T(8,128)(2,1)} %bitcast.42), calls=%async_computation.3 | async-start | bytes 2949120 | tf_op jit(solution)/shard_map/return_grads/all_to_all | solution.py:218
  167.4 16.8 %collective-permute-start.7 = (bf16[32,192]{1,0:T(8,128)(2,1)S(1)}, bf16[32,192]{1,0:T(8,128)(2,1)S(1)}, u32[]{:S(2)}, u32[]{:S(2)}) collective-permute-start(bf16[32,192]{1,0:T(8,128)(2,1)S(1)} %select_convert_fusion), channel_id=1, source_target_pairs={{0,64},{64,0},{1,65},{65,1},{2,66},{66,2},{3,67},{67,3},{4,68},{68... | collective-permute-start | bytes 36872 | tf_op jit(solution)/shard_map/sum_dx/ppermute | solution.py:222
  184.2 0.6 copy-start.2

commit v4 on v3

v4 whole, which is shorter than its diff:
```python
import jax
import jax.numpy as jnp
from jax import lax
from jax.experimental import pallas as pl
from jax.experimental.pallas import tpu as pltpu
from jax.sharding import Mesh, PartitionSpec as P

DP = ("x", "zh", "core")
EX = ("zq", "zp", "y")
GROUP = ("zp", "y")
BLK = 16
TOP = 6
CAP = 8
EXPERTS = 16
DSH = 160
FSH = 96
SHARD = 32
TOKENS = 512
BLOCKS = TOKENS // BLK
LANES = 128
NG = 8
NE = EXPERTS // NG
NX = 4
SLOTS = BLOCKS * CAP
HALF = TOKENS // 2
HSLOTS = SLOTS // 2
PART = HSLOTS // 4
Q = DSH // 4
STEP = Q + 8
WIDE = 4 * STEP
COLS = 2 * WIDE
IDS_AT = Q
PROBS_AT = STEP + Q
TRIO = 3 * FSH
PACK = 2 * NE * TRIO
PAIR = 2 * LANES
VMEM = 56 * 1024 * 1024
BF16 = jnp.bfloat16
F32 = jnp.float32


def iota(shape, dim):
    return lax.broadcasted_iota(jnp.int32, shape, dim)


def dot(a, b):
    return jnp.dot(a, b, preferred_element_type=F32)


def dot_dims(a, b, left, right):
    return lax.dot_general(a, b, (((left,), (right,)), ((), ())), preferred_element_type=F32)


def feature_of(column):
    s = sum(jnp.where(column >= i * STEP, 1, 0) for i in range(1, 4))
    q = column - s * STEP
    return jnp.where((q < Q) & (column >= 0) & (column < WIDE), 4 * q + s, -1)


def ones(mask):
    return jnp.where(mask, 1.0, 0.0).astype(BF16)


def prepare_kernel(stash_ref, scale_ref, dy_ref, ids_ref, probs_ref, out_ref):
    scale = scale_ref[...]
    factor = jnp.where(scale == -2, 0.25, jnp.where(scale == -1, 0.5, jnp.where(scale == 0, 1.0, 2.0)))
    per = DSH // scale.shape[0]
    shape = (scale.shape[0], DSH)
    first = iota(shape, 0) * per
    expand = ones((iota(shape, 1) >= first) & (iota(shape, 1) < first + per))
    x = (stash_ref[...].astype(F32) * dot_dims(factor.astype(BF16), expand, 0, 0)).astype(BF16)
    row, column = iota((DSH, COLS), 0), iota((DSH, COLS), 1)
    out = dot(x, ones(row == feature_of(column)))
    out = out + dot(dy_ref[...], ones(row == feature_of(column - WIDE)))
    row, column = iota((TOP, COLS), 0), iota((TOP, COLS), 1)
    out = out + dot_dims(ids_ref[...].astype(F32).astype(BF16), ones(row == column - IDS_AT), 0, 0)
    out = out + dot_dims(probs_ref[...], ones(row == column - PROBS_AT), 0, 0)
    out_ref[...] = out.astype(BF16)


def layout_kernel(w_ref, wx_ref, wd_ref):
    low = jnp.zeros((STEP - Q, FSH), F32)
    side = jnp.zeros((STEP, LANES - FSH), F32)
    for g in range(NG):
        for e in range(NE):
            for i in range(3):
                w = w_ref[g, e, i].astype(F32)
                for s in range(4):
                    piece = jnp.concatenate([w[:, s * FSH:(s + 1) * FSH], low], axis=0)
                    piece = jnp.concatenate([piece, side], axis=1).astype(BF16)
                    if i < 2:
                        wx_ref[g, s * STEP:(s + 1) * STEP, e * PAIR + i * LANES:e * PAIR + (i + 1) * LANES] = piece
                    else:
                        wd_ref[g, s * STEP:(s + 1) * STEP, e * LANES:(e + 1) * LANES] = piece


def forward_kernel(me_ref, x0_ref, x1_ref, wx_ref, wd_ref, keep_ref, give1_ref, give2_ref, give3_ref,
                   xs_ref, ds_ref, gate_ref, slot_ref, pick_ref, pre_ref):
    first = me_ref[0] * NE
    lane = iota((HALF, LANES), 1)
    row, column = iota((HALF, HALF), 0), iota((HALF, HALF), 1)
    before = ones((column < row) & (column >= row - row % BLK))
    block = (iota((HALF, LANES), 0) // BLK).astype(F32)
    row = iota((HSLOTS, HALF), 0).astype(F32)
    for h, x_ref in enumerate((x0_ref, x1_ref)):
        at = slice(h * HALF, (h + 1) * HALF)
        head = x_ref[:, 0, :, :LANES].reshape(HALF, LANES).astype(F32)
        hit = jnp.zeros((HALF, LANES), F32)
        prob = jnp.zeros((HALF, LANES), F32)
        for k in range(TOP):
            same = head[:, IDS_AT + k:IDS_AT + k + 1] == (lane + first).astype(F32)
            hit = jnp.where(same, 1.0, hit)
            prob = jnp.where(same, head[:, PROBS_AT + k:PROBS_AT + k + 1], prob)
        place = dot(before, hit.astype(BF16))
        slot = jnp.where(hit > 0.5, block * CAP + place, -1.0)
        slot_ref[at, :] = jnp.where(lane < NE, slot, head)
        slot_t = slot.T
        for e in range(NE):
            pick_ref[h, e * HSLOTS:(e + 1) * HSLOTS, :] = ones(row == slot_t[e:e + 1, :])
        gate = dot(pick_ref[h], prob.astype(BF16))
        for e in range(NE):
            gate_ref[e, h * HSLOTS:(h + 1) * HSLOTS, :] = gate[e * HSLOTS:(e + 1) * HSLOTS]
    for g in range(NG):
        for h, x_ref in enumerate((x0_ref, x1_ref)):
            x = dot(pick_ref[h], x_ref[:, g, :, :WIDE].reshape(HALF, WIDE)).astype(BF16)
            dy = dot(pick_ref[h], x_ref[:, g, :, WIDE:].reshape(HALF, WIDE)).astype(BF16)
            at = slice(h * HSLOTS, (h + 1) * HSLOTS)
            for e in range(NE):
                xs_ref[g, e, at, :] = x[e * HSLOTS:(e + 1) * HSLOTS]
                ds_ref[g, e, at, :] = dy[e * HSLOTS:(e + 1) * HSLOTS]
    for e in range(NE):
        ab = jnp.zeros((SLOTS, PAIR), F32)
        back = jnp.zeros((SLOTS, LANES), F32)
        for g in range(NG):
            ab = ab + dot(xs_ref[g, e], wx_ref[g, :, e * PAIR:(e + 1) * PAIR])
            back = back + dot(ds_ref[g, e], wd_ref[g, :, e * LANES:(e + 1) * LANES])
        trio = jnp.concatenate([ab[:, :FSH], ab[:, LANES:LANES + FSH], back[:, :FSH]], axis=1)
        for h in range(2):
            unit = 2 * e + h
            pre_ref[:, unit * TRIO:(unit + 1) * TRIO] = trio[h * HSLOTS:(h + 1) * HSLOTS]
    for s, out_ref in enumerate((keep_ref, give1_ref, give2_ref, give3_ref)):
        rows = pl.ds(pl.multiple_of(me_ref[1 + s] * PART, PART), PART)
        out_ref[...] = pre_ref[rows, :].astype(out_ref.dtype)


def dx_of(spread, wx, tail):
    dx = dot_dims(spread, wx, 1, 1) + tail
    dx = dx.reshape(NX, 2, SHARD, WIDE)
    return jnp.concatenate([dx[:, 0], dx[:, 1]], axis=2)


def middle_kernel(me_ref, own_ref, pre1_ref, pre2_ref, pre3_ref, wx_ref, gate_ref, slot_ref,
                  d_ref, spread_ref, tail_ref, give_ref, pre_ref, far_ref):
    first = me_ref[0] * NE
    for s, part_ref in enumerate((own_ref, pre1_ref, pre2_ref, pre3_ref)):
        rows = pl.ds(pl.multiple_of(me_ref[1 + s] * PART, PART), PART)
        pre_ref[rows, :] = part_ref[...].astype(F32)
    side = jnp.zeros((HSLOTS, LANES - FSH), F32)
    lane = iota((HSLOTS, LANES - FSH), 1)
    slots = iota((HALF, HSLOTS), 1).astype(F32)
    wide = iota((HALF, LANES), 1)
    none = jnp.zeros((HALF, WIDE - LANES), F32)
    for h, out_ref in enumerate((spread_ref, far_ref)):
        info = slot_ref[h * HALF:(h + 1) * HALF, :]
        tail = jnp.zeros((HALF, LANES), F32)
        for e in range(NE):
            base = (2 * e + h) * TRIO
            pre = pre_ref[:, base:base + TRIO]
            a, b, back = (pre[:, i * FSH:(i + 1) * FSH] for i in range(3))
            gate = gate_ref[e, h * HSLOTS:(h + 1) * HSLOTS, e:e + 1]
            sig = jax.nn.sigmoid(a)
            act = a * sig
            hidden = act * b
            dh = gate * back
            d_gate = dh * b * sig * (1.0 + a * (1.0 - sig))
            prob = jnp.sum(hidden * back, axis=1, keepdims=True)
            prob = jnp.where(lane == 0, prob, 0.0)
            d = jnp.concatenate([d_gate, prob, dh * act, side, gate * hidden, side], axis=1).astype(BF16)
            d_ref[e, h * HSLOTS:(h + 1) * HSLOTS, :] = d
            spread = dot(ones(slots == info[:, e:e + 1]), d[:, :PAIR])
            out_ref[:, e * PAIR:(e + 1) * PAIR] = spread.astype(BF16)
            mine = info == (first + e).astype(F32)
            mine = mine & (wide >= IDS_AT) & (wide < IDS_AT + TOP)
            tail = jnp.where(mine, spread[:, FSH:FSH + 1], tail)
        if h == 0:
            tail_ref[...] = tail
    tail = jnp.concatenate([tail, none], axis=1)
    for g in range(NG):
        give_ref[:, g] = dx_of(far_ref[...], wx_ref[g], tail).astype(BF16)


def input_kernel(got_ref, spread_ref, tail_ref, wx_ref, dx_ref):
    none = jnp.zeros((HALF, WIDE - LANES), F32)
    tail = jnp.concatenate([tail_ref[...], none], axis=1)
    for g in range(NG):
        dx = dx_of(spread_ref[...], wx_ref[g], tail) + got_ref[:, g].astype(F32)
        dx_ref[:, g] = dx.astype(BF16)


def weight_kernel(xs_ref, ds_ref, d_ref, out_ref):
    for e in range(NE):
        for g in range(NG):
            both = dot_dims(xs_ref[g, e], d_ref[e, :, :PAIR], 0, 0)
            down = dot_dims(ds_ref[g, e], d_ref[e, :, PAIR:], 0, 0)
            for i, (grad, base) in enumerate(((both, 0), (both, LANES), (down, 0))):
                pieces = [grad[s * STEP:s * STEP + Q, base:base + FSH] for s in range(4)]
                out_ref[g, e, i] = jnp.concatenate(pieces, axis=1).astype(BF16)


def finish_kernel(dx_ref, got_ref, in_ref, probs_ref):
    total = dx_ref[...] + got_ref[...].astype(F32)
    row, column = iota((WIDE, DSH), 0), iota((WIDE, DSH), 1)
    order = ones(feature_of(row) == column)
    in_ref[...] = dot(total.astype(BF16), order).astype(BF16)
    probs_ref[...] = total[:, :LANES].T[IDS_AT:IDS_AT + TOP, :]


def call(kernel, outs, args, scratch=(), scalar=False):
    vmem = pl.BlockSpec(memory_space=pltpu.VMEM)
    specs = [vmem] * len(args)
    if scalar:
        specs[0] = pl.BlockSpec(memory_space=pltpu.SMEM)
    return pl.pallas_call(
        kernel,
        out_shape=[jax.ShapeDtypeStruct(shape, dtype) for shape, dtype in outs],
        in_specs=specs,
        out_specs=[vmem] * len(outs),
        scratch_shapes=[pltpu.VMEM(shape, dtype) for shape, dtype in scratch],
        compiler_params=pltpu.CompilerParams(vmem_limit_bytes=VMEM),
    )(*args)


def exchange(value, axis):
    return lax.all_to_all(value, axis, split_axis=0, concat_axis=0, tiled=True)


def swap(value, axis):
    return lax.ppermute(value, axis, [(0, 1), (1, 0)])


def flip(value, axis, bit):
    return lax.ppermute(value, axis, [(i, i ^ bit) for i in range(lax.axis_size(axis))])


def local(stash, scale_exp, grad_out, route_ids, route_probs, w_gate, w_up, w_down):
    group = lax.axis_index(GROUP).astype(jnp.int32)
    zq = lax.axis_index("zq").astype(jnp.int32)
    me = jnp.stack([group] + [zq ^ s for s in range(4)])
    small = [v.T for v in (scale_exp, route_ids, route_probs)]
    (xin,) = call(prepare_kernel, [((SHARD, COLS), BF16)], (stash, small[0], grad_out, small[1], small[2]))
    other = swap(xin, "zh")
    with jax.named_scope("move_weights"):
        xin, w_gate, w_up, w_down = lax.optimization_barrier((xin, w_gate, w_up, w_down))
        tiles = [w.reshape(EXPERTS, 1, Q, 4 * FSH) for w in (w_gate, w_up, w_down)]
        weights = exchange(jnp.concatenate(tiles, axis=1), GROUP)
        weights = weights.reshape(NG, NE, 3, Q, 4 * FSH)
    other, weights = lax.optimization_barrier((other, weights))
    with jax.named_scope("gather_tokens"):
        xin = jnp.tile(jnp.concatenate([xin, other]), (NX * NG, 1))
        x0 = exchange(xin, ("x",) + GROUP).reshape(NX, NG, 2 * SHARD, COLS)
        x1 = swap(x0, "core")
    wx, wd = call(layout_kernel, [((NG, WIDE, NE * PAIR), BF16), ((NG, WIDE, NE * LANES), BF16)], (weights,))
    part = ((PART, PACK), BF16)
    keep, give1, give2, give3, xs, ds, gate, slot = call(
        forward_kernel,
        [((PART, PACK), F32), part, part, part, ((NG, NE, SLOTS, WIDE), BF16), ((NG, NE, SLOTS, WIDE), BF16),
         ((NE, SLOTS, LANES), F32), ((TOKENS, LANES), F32)],
        (me, x0, x1, wx, wd),
        [((2, HALF, HALF), BF16), ((HSLOTS, PACK), F32)],
        True)
    with jax.named_scope("sum_pre"):
        got = [flip(give, "zq", 1 + i) for i, give in enumerate((give1, give2, give3))]
        pre = (keep + sum(v.astype(F32) for v in got)).astype(BF16)
    with jax.named_scope("spread_pre"):
        pre = [pre] + [flip(pre, "zq", s) for s in range(1, 4)]
    dx_shape = (NX, NG, SHARD, COLS)
    d, spread, tail, give = call(
        middle_kernel,
        [((NE, SLOTS, 3 * LANES), BF16), ((HALF, NE * PAIR), BF16), ((HALF, LANES), F32), (dx_shape, BF16)],
        (me, *pre, wx, gate, slot),
        [((HSLOTS, PACK), F32), ((HALF, NE * PAIR), BF16)],
        True)
    with jax.named_scope("sum_dx"):
        (dx,) = call(input_kernel, [(dx_shape, BF16)], (swap(give, "core"), spread, tail, wx))
        dx, d = lax.optimization_barrier((dx, d))
        dx = exchange(dx.reshape(NX * NG, SHARD, COLS), ("x",) + GROUP)
        dx = jnp.sum(dx.astype(F32), axis=0)
        keep, give = dx[:, :WIDE], dx[:, WIDE:].astype(BF16)
    (grads,) = call(weight_kernel, [((NG, NE, 3, Q, 4 * FSH), BF16)], (xs, ds, d))
    give, grads = lax.optimization_barrier((give, grads))
    got = swap(give, "zh")
    with jax.named_scope("return_grads"):
        grads = exchange(grads.reshape(EXPERTS, 3, Q, 4 * FSH), GROUP)
        grads = [grads[:, i].reshape(w_gate.shape) for i in range(3)]
    keep, *grads = lax.optimization_barrier((keep, *grads))
    grad_in, grad_probs = call(finish_kernel, [((SHARD, DSH), BF16), ((TOP, SHARD), F32)], (keep, got))
    return (grad_in, grad_probs.T, *grads)


def solution(mesh):
    fine = Mesh(mesh.devices.reshape(4, 2, 2, 4, 2, 4), DP + EX)
    weight = P(None, DP + EX)
    in_specs = (P(DP, EX), P(DP, EX), P(DP, EX), P(DP, None), P(DP, None), weight, weight, weight)
    out_specs = (P(DP, EX), P(DP, None), weight, weight, weight)
    return jax.shard_map(local, mesh=fine, in_specs=in_specs, out_specs=out_specs, check_vma=False)
```

time: 193 us -> 193 us (level)
  waiting for transfers between devices: 71.5 us -> 54.6 us
  starting transfers between devices: 52.9 us -> 69.7 us
  other arithmetic: 10.2 us -> 2.4 us
  Pallas kernels: 21.4 us -> 28.5 us
  local copies, waits for them, and re-layouts: 7.21 us -> 9.76 us
    ppermute x4 -> x6, waiting for transfers between devices: 32.8 us -> 14.5 us  [flip(): lax.ppermute(value, axis, [(i, i ^ bit) for i in range(lax.axis_size(axis...]
    all_to_all x3, waiting for transfers between devices: 8.16 us -> 22.7 us  [exchange(): return lax.all_to_all(value, axis, split_axis=0, concat_axis=0, tiled=True)]
    ppermute x4 -> x6, starting transfers between devices: 12.5 us -> 26.3 us  [flip(): lax.ppermute(value, axis, [(i, i ^ bit) for i in range(lax.axis_size(axis...]
    ppermute x4, waiting for transfers between devices: 30.6 us -> 17.4 us  [swap(): return lax.ppermute(value, axis, [(0, 1), (1, 0)])]
    pallas_call x5 -> x7, Pallas kernels: 21.4 us -> 28.5 us  [call(): pl.pallas_call(kernel, out_shape=[jax.ShapeDtypeStruct(shape, dtype) for...]
    select_n x5 -> x0, other arithmetic: 4.24 us -> none  [the longest x1 1.92 us: local(): xin = jnp.where(core == 0, jnp.stack([xin, other]), jnp.stack([other, xin]))]
    ppermute x4, starting transfers between devices: 26.5 us -> 29.3 us  [swap(): return lax.ppermute(value, axis, [(0, 1), (1, 0)])]
    unnamed x13 -> x28, local copies, waits for them, and re-layouts: 6.81 us -> 8.09 us
  transfers between devices with their start and end apart: 11 -> 13, of which waited for: 9 -> 7; matrix products, arithmetic and copies ran while one was open for 2% -> 2% of each run, Pallas kernels for 4% -> 5%
where the time goes in v4:
time: 193 us; the launch traced here: 192 us
  starting transfers between devices  69.7 us (36%)
  waiting for transfers between devices  54.6 us (28%)
  Pallas kernels  28.5 us (15%)
  blocking collectives  26.3 us (14%)
  local copies, waits for them, and re-layouts  9.76 us (5%)
  other arithmetic  2.4 us (1%)
    ppermute x4, starting transfers between devices, swap(): return lax.ppermute(value, axis, [(0, 1), (1, 0)])  29.3 us
    pallas_call x7, Pallas kernels, call(): pl.pallas_call(kernel, out_shape=[jax.ShapeDtypeStruct(shape, dtype) for...  28.5 us
    ppermute x6, starting transfers between devices, flip(): lax.ppermute(value, axis, [(i, i ^ bit) for i in range(lax.axis_size(axis...  26.3 us
    all_to_all x1, blocking collectives, exchange(): return lax.all_to_all(value, axis, split_axis=0, concat_axis=0, tiled=True)  26.3 us
    all_to_all x3, waiting for transfers between devices, exchange(): return lax.all_to_all(value, axis, split_axis=0, concat_axis=0, tiled=True)  22.7 us
    ppermute x4, waiting for transfers between devices, swap(): return lax.ppermute(value, axis, [(0, 1), (1, 0)])  17.4 us
    ppermute x6, waiting for transfers between devices, flip(): lax.ppermute(value, axis, [(i, i ^ bit) for i in range(lax.axis_size(axis...  14.5 us
    all_to_all x3, starting transfers between devices, exchange(): return lax.all_to_all(value, axis, split_axis=0, concat_axis=0, tiled=True)  14 us
  transfers between devices with their start and end apart: 13, of which 7 were waited for; matrix products, arithmetic and copies ran while one was open for 2% of the time, Pallas kernels for 5%

profile of v4, /device:TPU:1, one launch (start us, length us, event | category | flops | bytes accessed | tf_op | source)
XLA Modules:
  0.0 192.0 jit_solution(6554266843911517995)
XLA Ops:
  0.6 0.0 copy-start.4
  0.6 1.7 shard_map.119
  2.4 1.1 copy.16
  3.5 1.1 copy.17
  4.6 0.0 copy-done.4
  4.6 0.1 copy.18
  4.7 1.3 pad_maximum_fusion
  6.0 0.0 copy-start.6
  6.0 6.5 %all-to-all-start = ((bf16[16,3,40,384]{3,2,1,0:T(8,128)(2,1)}), bf16[16,3,40,384]{3,2,1,0:T(8,128)(2,1)S(1)}, u32[]{:S(2)}, u32[]{:S(2)}) async-start(bf16[16,3,40,384]{3,2,1,0:T(8,128)(2,1)} %pad_maximum_fusion), calls=%async_computation | async-start | bytes 2949120 | tf_op jit(solution)/shard_map/move_weights/all_to_all | solution.py:234
  12.5 0.0 copy-done.6
  12.5 14.5 %collective-permute-start = (bf16[32,384]{1,0:T(8,128)(2,1)S(1)}, bf16[32,384]{1,0:T(8,128)(2,1)S(1)}, u32[]{:S(2)}, u32[]{:S(2)}) collective-permute-start(bf16[32,384]{1,0:T(8,128)(2,1)S(1)} %copy-done.6), channel_id=1, source_target_pairs={{0,64},{64,0},{1,65},{65,1},{2,66},{66,2},{3,67},{67,3},{4,68},{68... | collective-permute-start | bytes 73736 | tf_op jit(solution)/shard_map/ppermute | solution.py:238
  27.0 15.3 %collective-permute-done = bf16[32,384]{1,0:T(8,128)(2,1)S(1)} collective-permute-done((bf16[32,384]{1,0:T(8,128)(2,1)S(1)}, bf16[32,384]{1,0:T(8,128)(2,1)S(1)}, u32[]{:S(2)}, u32[]{:S(2)}) %collective-permute-start) | collective-permute-done | bytes 24608 | tf_op jit(solution)/shard_map/ppermute | solution.py:238
  42.3 0.0 all-to-all-done
  42.3 0.0 copy-start.1
  42.3 0.2 tile.2
  42.6 26.3 %all_to_all.21 = bf16[32,64,384]{2,1,0:T(8,128)(2,1)S(1)} all-to-all(bf16[32,64,384]{2,1,0:T(8,128)(2,1)S(1)} %tile.2), channel_id=1, replica_groups=mesh['x'=4,'zh'=2,'core'=2,'zq'=4,'zp'=2,'y'=4] {'x','zp','y'}, dimensions={0} | all-to-all | bytes 3145728 | tf_op jit(solution)/shard_map/gather_tokens/all_to_all | solution.py:234
  68.9 0.0 copy-done.1
  68.9 6.0 %collective-permute-start.1 = (bf16[4,8,64,384]{3,2,1,0:T(8,128)(2,1)S(1)}, bf16[4,8,64,384]{3,2,1,0:T(8,128)(2,1)S(1)}, u32[]{:S(2)}, u32[]{:S(2)}) collective-permute-start(bf16[4,8,64,384]{3,2,1,0:T(8,128)(2,1)S(1)} %bitcast.40), channel_id=1, source_target_pairs={{0,32},{32,0},{1,33},{33,1},{2,34},{34,2},{3,35},{35,3},{4,36},{36... | collective-permute-start | bytes 4718600 | tf_op jit(solution)/shard_map/gather_tokens/ppermute | solution.py:238
  75.0 0.6 stack.23.me_ref
  75.6 3.6 %shard_map.120 = (bf16[8,192,512]{2,1,0:T(8,128)(2,1)}, bf16[8,192,256]{2,1,0:T(8,128)(2,1)}) custom-call(bf16[8,2,3,40,384]{4,3,2,1,0:T(8,128)(2,1)} %bitcast.42), custom_call_target="tpu_custom_call" | custom-call | tf_op jit(solution)/shard_map/pallas_call | solution.py:223
  79.1 0.0 collective-permute-done.1.x1_ref
  79.1 0.0 copy-done
  79.1 1.2 copy-done.2
  80.3 7.5 %shard_map.121 = (f32[32,1152]{1,0:T(8,128)}, bf16[32,1152]{1,0:T(8,128)(2,1)}, bf16[32,1152]{1,0:T(8,128)(2,1)}, bf16[32,1152]{1,0:T(8,128)(2,1)}, bf16[8,2,256...) custom-call(s32[5]{0:T(128)} %stack.23.me_ref, ...), custom_call_target="tpu_custom_call" | custom-call | tf_op jit(solution)/shard_map/pallas_call | solution.py:223
  87.8 3.6 %collective-permute-start.2 = (bf16[32,1152]{1,0:T(8,128)(2,1)}, bf16[32,1152]{1,0:T(8,128)(2,1)S(1)}, u32[]{:S(2)}, u32[]{:S(2)}) collective-permute-start(bf16[32,1152]{1,0:T(8,128)(2,1)} %get-tuple-element.44), channel_id=1, source_target_pairs={{0,8},{8,0},{16,24},{24,16},{1,9},{9,1},{17,25},{25,17},{2,10},{10... | collective-permute-start | bytes 221192 | tf_op jit(solution)/shard_map/sum_pre/ppermute | solution.py:242
  91.5 4.8 %collective-permute-start.3 = (bf16[32,1152]{1,0:T(8,128)(2,1)}, bf16[32,1152]{1,0:T(8,128)(2,1)S(1)}, u32[]{:S(2)}, u32[]{:S(2)}) collective-permute-start(bf16[32,1152]{1,0:T(8,128)(2,1)} %get-tuple-element.45), channel_id=1, source_target_pairs={{0,16},{8,24},{16,0},{24,8},{1,17},{9,25},{17,1},{25,9},{2,18},{10... | collective-permute-start | bytes 221192 | tf_op jit(solution)/shard_map/sum_pre/ppermute | solution.py:242
  96.3 4.7 %collective-permute-start.4 = (bf16[32,1152]{1,0:T(8,128)(2,1)}, bf16[32,1152]{1,0:T(8,128)(2,1)S(1)}, u32[]{:S(2)}, u32[]{:S(2)}) collective-permute-start(bf16[32,1152]{1,0:T(8,128)(2,1)} %get-tuple-element.46), channel_id=1, source_target_pairs={{0,24},{8,16},{16,8},{24,0},{1,25},{9,17},{17,9},{25,1},{2,26},{10... | collective-permute-start | bytes 221192 | tf_op jit(solution)/shard_map/sum_pre/ppermute | solution.py:242
  101.0 0.0 collective-permute-done.2
  101.0 9.8 %collective-permute-done.3 = bf16[32,1152]{1,0:T(8,128)(2,1)S(1)} collective-permute-done((bf16[32,1152]{1,0:T(8,128)(2,1)}, bf16[32,1152]{1,0:T(8,128)(2,1)S(1)}, u32[]{:S(2)}, u32[]{:S(2)}) %collective-permute-start.3) | collective-permute-done | bytes 73760 | tf_op jit(solution)/shard_map/sum_pre/ppermute | solution.py:242
  110.8 0.0 collective-permute-done.4
  110.8 1.0 add_convert_fusion.own_ref
  111.8 0.0 copy-start.5
  111.8 1.9 %collective-permute-start.7 = (bf16[32,1152]{1,0:T(8,128)(2,1)S(1)}, bf16[32,1152]{1,0:T(8,128)(2,1)S(1)}, u32[]{:S(2)}, u32[]{:S(2)}) collective-permute-start(bf16[32,1152]{1,0:T(8,128)(2,1)S(1)} %add_convert_fusion.own_ref), channel_id=1, source_target_pairs={{0,24},{8,16},{16,8},{24,0},{1,25},{9,17},{17,9},{25,1},{2,26},{10... | collective-permute-start | bytes 221192 | tf_op jit(solution)/shard_map/spread_pre/ppermute | solution.py:242
  113.7 7.0 %collective-permute-start.6 = (bf16[32,1152]{1,0:T(8,128)(2,1)S(1)}, bf16[32,1152]{1,0:T(8,128)(2,1)S(1)}, u32[]{:S(2)}, u32[]{:S(2)}) collective-permute-start(bf16[32,1152]{1,0:T(8,128)(2,1)S(1)} %add_convert_fusion.own_ref), channel_id=1, source_target_pairs={{0,16},{8,24},{16,0},{24,8},{1,17},{9,25},{17,1},{25,9},{2,18},{10... | collective-permute-start | bytes 221192 | tf_op jit(solution)/shard_map/spread_pre/ppermute | solution.py:242
  120.8 4.2 %collective-permute-start.5 = (bf16[32,1152]{1,0:T(8,128)(2,1)S(1)}, bf16[32,1152]{1,0:T(8,128)(2,1)S(1)}, u32[]{:S(2)}, u32[]{:S(2)}) collective-permute-start(bf16[32,1152]{1,0:T(8,128)(2,1)S(1)} %add_convert_fusion.own_ref), channel_id=1, source_target_pairs={{0,8},{8,0},{16,24},{24,16},{1,9},{9,1},{17,25},{25,17},{2,10},{10... | collective-permute-start | bytes 221192 | tf_op jit(solution)/shard_map/spread_pre/ppermute | solution.py:242
  125.0 0.0 collective-permute-done.7.pre3_ref
  125.0 0.0 copy-start.7
  125.0 4.2 %collective-permute-done.6.pre2_ref = bf16[32,1152]{1,0:T(8,128)(2,1)S(1)} collective-permute-done((bf16[32,1152]{1,0:T(8,128)(2,1)S(1)}, bf16[32,1152]{1,0:T(8,128)(2,1)S(1)}, u32[]{:S(2)}, u32[]{:S(2)}) %collective-permute-start.6) | collective-permute-done | bytes 73760 | tf_op jit(solution)/shard_map/spread_pre/ppermute | solution.py:242
  129.2 0.5 collective-permute-done.5.pre1_ref
  129.7 0.0 copy-done.5
  129.7 0.0 copy-done.7
  129.8 0.1 copy-done.8
  129.8 0.5 copy-done.9
  130.4 5.5 %shard_map.122 = (bf16[2,256,384]{2,1,0:T(8,128)(2,1)}, bf16[256,512]{1,0:T(8,128)(2,1)}, f32[256,128]{1,0:T(8,128)}, bf16[4,8,32,384]{3,2,1,0:T(8,128)(2,1)}) custom-call(s32[5]{0:T(128)} %stack.23.me_ref, bf16[32,1152]{1,0:T(8,128)(2,1)} %copy-done.5, bf16[32,1152]{1,0:T(8,128)(2,1)} %copy-done.9, bf16[32,1152]{1,0:T(8,128)(2,1)} %copy-done.8, ...), custom_call_target="tpu_custom_call" | custom-call | tf_op jit(solution)/shard_map/pallas_call | solution.py:223
  135.9 4.5 %collective-permute-start.8 = (bf16[4,8,32,384]{3,2,1,0:T(8,128)(2,1)}, bf16[4,8,32,384]{3,2,1,0:T(8,128)(2,1)S(1)}, u32[]{:S(2)}, u32[]{:S(2)}) collective-permute-start(bf16[4,8,32,384]{3,2,1,0:T(8,128)(2,1)} %get-tuple-element.49), channel_id=1, source_target_pairs={{0,32},{32,0},{1,33},{33,1},{2,34},{34,2},{3,35},{35,3},{4,36},{36... | collective-permute-start | bytes 2359304 | tf_op jit(solution)/shard_map/sum_dx/ppermute | solution.py:238
  140.4 2.1 %collective-permute-done.8.got_ref = bf16[4,8,32,384]{3,2,1,0:T(8,128)(2,1)S(1)} collective-permute-done((bf16[4,8,32,384]{3,2,1,0:T(8,128)(2,1)}, bf16[4,8,32,384]{3,2,1,0:T(8,128)(2,1)S(1)}, u32[]{:S(2)}, u32[]{:S(2)}) %collective-permute-start.8) | collective-permute-done | bytes 786464 | tf_op jit(solution)/shard_map/sum_dx/ppermute | solution.py:238
  142.5 0.9 copy-done.3
  143.4 3.5 %sum_dx.1 = bf16[4,8,32,384]{3,2,1,0:T(8,128)(2,1)} custom-call(bf16[4,8,32,384]{3,2,1,0:T(8,128)(2,1)} %copy-done.3, bf16[256,512]{1,0:T(8,128)(2,1)} %get-tuple-element.50.spread_ref, f32[256,128]{1,0:T(8,128)} %get-tuple-element.51.tail_ref, bf16[8,192,512]{2,1,0:T(8,128)(2,1)} %get-tuple-element.41.wx_ref), custom_call_target="tpu_custom_call" | custom-call | tf_op jit(solution)/shard_map/sum_dx/pallas_call | solution.py:223
  146.8 3.9 %all-to-all-start.2 = ((bf16[32,32,384]{2,1,0:T(8,128)(2,1)}), bf16[32,32,384]{2,1,0:T(8,128)(2,1)S(1)}, u32[]{:S(2)}, u32[]{:S(2)}) async-start(bf16[32,32,384]{2,1,0:T(8,128)(2,1)} %bitcast.44), calls=%async_computation.2 | async-start | bytes 1572864 | tf_op jit(solution)/shard_map/sum_dx/all_to_all | solution.py:234
  150.7 5.1 %shard_map.123 = bf16[8,2,3,40,384]{4,3,2,1,0:T(8,128)(2,1)} custom-call(bf16[8,2,256,192]{3,2,1,0:T(8,128)(2,1)} %get-tuple-element.54.xs_ref, bf16[8,2,256,192]{3,2,1,0:T(8,128)(2,1)} %get-tuple-element.55.ds_ref, bf16[2,256,384]{2,1,0:T(8,128)(2,1)} %get-tuple-element.56.d_ref), custom_call_target="tpu_custom_call" | custom-call | tf_op jit(solution)/shard_map/pallas_call | solution.py:223
  155.9 8.1 %all-to-all-done.2 = bf16[32,32,384]{2,1,0:T(8,128)(2,1)S(1)} async-done(((bf16[32,32,384]{2,1,0:T(8,128)(2,1)}), bf16[32,32,384]{2,1,0:T(8,128)(2,1)S(1)}, u32[]{:S(2)}, u32[]{:S(2)}) %all-to-all-start.2) | async-done | bytes 786464 | tf_op jit(solution)/shard_map/sum_dx/all_to_all | solution.py:234
  164.0 0.1 convert_reduce_fusion
  164.1 0.1 slice.27
  164.2 3.6 %all-to-all-start.3 = ((bf16[16,3,40,384]{3,2,1,0:T(8,128)(2,1)}), bf16[16,3,40,384]{3,2,1,0:T(8,128)(2,1)S(1)}, u32[]{:S(2)}, u32[]{:S(2)}) async-start(bf16[16,3,40,384]{3,2,1,0:T(8,128)(2,1)} %bitcast.43), calls=%async_computation.3 | async-start | bytes 2949120 | tf_op jit(solution)/shard_map/return_grads/all_to_all | solution.py:234
  167.8 0.6 slice.21.dx_ref
  168.4 4.3 %collective-permute-start.9 = (bf16[32,192]{1,0:T(8,128)(2,1)S(1)}, bf16[32,192]{1,0:T(8,128)(2,1)S(1)}, u32[]{:S(2)}, u32[]{:S(2)}) collective-permute-start(bf16[32,192]{1,0:T(8,128)(2,1)S(1)} %slice.27), channel_id=1, source_target_pairs={{0,64},{64,0},{1,65},{65,1},{2,66},{66,2},{3,67},{67,3},{4,68},{68... | collective-permute-start | bytes 36872 | tf_op jit(solution)/shard_map/ppermute | solution.py:238
  172.7 14.5 %all-to-all-done.3 = bf16[16,3,40,384]{3,2,1,0:T(8,128)(2,1)S(1)} async-done(((bf16[16,3,40,384]{3,2,1,0:T(8,128)(2,1)}), bf16[16,3,40,384]{3,2,1,0:T(8,128)(2,1)S(1)}, u32[]{:S(2)}, u32[]{:S(2)}) %all-to-all-start.3) | async-done | bytes 1474592 | tf_op jit(solution)/shard_map/return_grads/all_to_all | solution.py:234
  187.3 0.2 fusion
  187.4 0.8 copy.21
  188.3 0.8 copy.20
  189.1 0.8 copy.19
  189.9 0.0 collective-permute-done.9.got_ref
  189.9 0.6 copy-done.10
  190.5 1.5 shard_map.124
  (7 shorter events, 0.0 us)
Async XLA Ops:
  0.6 4.0 %copy-start.4 = (bf16[16,15360]{1,0:T(8,128)(2,1)S(1)}, bf16[16,15360]{1,0:T(8,128)(2,1)}, u32[]{:S(2)}) copy-start(bf16[16,15360]{1,0:T(8,128)(2,1)} %param.15) | copy-start | bytes 1474564
  6.0 6.5 %copy-start.6 = (bf16[32,384]{1,0:T(8,128)(2,1)S(1)}, bf16[32,384]{1,0:T(8,128)(2,1)}, u32[]{:S(2)}) copy-start(bf16[32,384]{1,0:T(8,128)(2,1)} %shard_map.119) | copy-start | bytes 73732
  6.0 36.3 %all-to-all-start = ((bf16[16,3,40,384]{3,2,1,0:T(8,128)(2,1)}), bf16[16,3,40,384]{3,2,1,0:T(8,128)(2,1)S(1)}, u32[]{:S(2)}, u32[]{:S(2)}) async-start(bf16[16,3,40,384]{3,2,1,0:T(8,128)(2,1)} %pad_maximum_fusion), calls=%async_computation | async-start | bytes 2949120 | tf_op jit(solution)/shard_map/move_weights/all_to_all | solution.py:234
  12.5 29.8 %collective-permute-start = (bf16[32,384]{1,0:T(8,128)(2,1)S(1)}, bf16[32,384]{1,0:T(8,128)(2,1)S(1)}, u32[]{:S(2)}, u32[]{:S(2)}) collective-permute-start(bf16[32,384]{1,0:T(8,128)(2,1)S(1)} %copy-done.6), channel_id=1, source_target_pairs={{0,64},{64,0},{1,65},{65,1},{2,66},{66,2},{3,67},{67,3},{4,68},{68... | collective-permute-start | bytes 73736 | tf_op jit(solution)/shard_map/ppermute | solution.py:238
  42.3 26.6 %copy-start.1 = (bf16[16,3,40,384]{3,2,1,0:T(8,128)(2,1)}, bf16[16,3,40,384]{3,2,1,0:T(8,128)(2,1)S(1)}, u32[]{:S(2)}) copy-start(bf16[16,3,40,384]{3,2,1,0:T(8,128)(2,1)S(1)} %all-to-all-done) | copy-start | bytes 4423684
  68.9 10.2 %copy-start = (bf16[32,64,384]{2,1,0:T(8,128)(2,1)}, bf16[32,64,384]{2,1,0:T(8,128)(2,1)S(1)}, u32[]{:S(2)}) copy-start(bf16[32,64,384]{2,1,0:T(8,128)(2,1)S(1)} %all_to_all.21) | copy-start | bytes 4718596
  68.9 10.2 %collective-permute-start.1 = (bf16[4,8,64,384]{3,2,1,0:T(8,128)(2,1)S(1)}, bf16[4,8,64,384]{3,2,1,0:T(8,128)(2,1)S(1)}, u32[]{:S(2)}, u32[]{:S(2)}) collective-permute-start(bf16[4,8,64,384]{3,2,1,0:T(8,128)(2,1)S(1)} %bitcast.40), channel_id=1, source_target_pairs={{0,32},{32,0},{1,33},{33,1},{2,34},{34,2},{3,35},{35,3},{4,36},{36... | collective-permute-start | bytes 4718600 | tf_op jit(solution)/shard_map/gather_tokens/ppermute | solution.py:238
  79.1 1.2 copy-start.2
  87.8 13.2 %collective-permute-start.2 = (bf16[32,1152]{1,0:T(8,128)(2,1)}, bf16[32,1152]{1,0:T(8,128)(2,1)S(1)}, u32[]{:S(2)}, u32[]{:S(2)}) collective-permute-start(bf16[32,1152]{1,0:T(8,128)(2,1)} %get-tuple-element.44), channel_id=1, source_target_pairs={{0,8},{8,0},{16,24},{24,16},{1,9},{9,1},{17,25},{25,17},{2,10},{10... | collective-permute-start | bytes 221192 | tf_op jit(solution)/shard_map/sum_pre/ppermute | solution.py:242
  91.5 19.4 %collective-permute-start.3 = (bf16[32,1152]{1,0:T(8,128)(2,1)}, bf16[32,1152]{1,0:T(8,128)(2,1)S(1)}, u32[]{:S(2)}, u32[]{:S(2)}) collective-permute-start(bf16[32,1152]{1,0:T(8,128)(2,1)} %get-tuple-element.45), channel_id=1, source_target_pairs={{0,16},{8,24},{16,0},{24,8},{1,17},{9,25},{17,1},{25,9},{2,18},{10... | collective-permute-start | bytes 221192 | tf_op jit(solution)/shard_map/sum_pre/ppermute | solution.py:242
  96.3 14.6 %collective-permute-start.4 = (bf16[32,1152]{1,0:T(8,128)(2,1)}, bf16[32,1152]{1,0:T(8,128)(2,1)S(1)}, u32[]{:S(2)}, u32[]{:S(2)}) collective-permute-start(bf16[32,1152]{1,0:T(8,128)(2,1)} %get-tuple-element.46), channel_id=1, source_target_pairs={{0,24},{8,16},{16,8},{24,0},{1,25},{9,17},{17,9},{25,1},{2,26},{10... | collective-permute-start | bytes 221192 | tf_op jit(solution)/shard_map/sum_pre/ppermute | solution.py:242
  111.8 18.0 %copy-start.5 = (bf16[32,1152]{1,0:T(8,128)(2,1)}, bf16[32,1152]{1,0:T(8,128)(2,1)S(1)}, u32[]{:S(2)}) copy-start(bf16[32,1152]{1,0:T(8,128)(2,1)S(1)} %add_convert_fusion.own_ref) | copy-start | bytes 221188
  111.8 13.2 %collective-permute-start.7 = (bf16[32,1152]{1,0:T(8,128)(2,1)S(1)}, bf16[32,1152]{1,0:T(8,128)(2,1)S(1)}, u32[]{:S(2)}, u32[]{:S(2)}) collective-permute-start(bf16[32,1152]{1,0:T(8,128)(2,1)S(1)} %add_convert_fusion.own_ref), channel_id=1, source_target_pairs={{0,24},{8,16},{16,8},{24,0},{1,25},{9,17},{17,9},{25,1},{2,26},{10... | collective-permute-start | bytes 221192 | tf_op jit(solution)/shard_map/spread_pre/ppermute | solution.py:242
  113.7 15.5 %collective-permute-start.6 = (bf16[32,1152]{1,0:T(8,128)(2,1)S(1)}, bf16[32,1152]{1,0:T(8,128)(2,1)S(1)}, u32[]{:S(2)}, u32[]{:S(2)}) collective-permute-start(bf16[32,1152]{1,0:T(8,128)(2,1)S(1)} %add_convert_fusion.own_ref), channel_id=1, source_target_pairs={{0,16},{8,24},{16,0},{24,8},{1,17},{9,25},{17,1},{25,9},{2,18},{10... | collective-permute-start | bytes 221192 | tf_op jit(solution)/shard_map/spread_pre/ppermute | solution.py:242
  120.8 9.0 %collective-permute-start.5 = (bf16[32,1152]{1,0:T(8,128)(2,1)S(1)}, bf16[32,1152]{1,0:T(8,128)(2,1)S(1)}, u32[]{:S(2)}, u32[]{:S(2)}) collective-permute-start(bf16[32,1152]{1,0:T(8,128)(2,1)S(1)} %add_convert_fusion.own_ref), channel_id=1, source_target_pairs={{0,8},{8,0},{16,24},{24,16},{1,9},{9,1},{17,25},{25,17},{2,10},{10... | collective-permute-start | bytes 221192 | tf_op jit(solution)/shard_map/spread_pre/ppermute | solution.py:242
  125.0 4.7 %copy-start.7 = (bf16[32,1152]{1,0:T(8,128)(2,1)}, bf16[32,1152]{1,0:T(8,128)(2,1)S(1)}, u32[]{:S(2)}) copy-start(bf16[32,1152]{1,0:T(8,128)(2,1)S(1)} %collective-permute-done.7.pre3_ref) | copy-start | bytes 221188
  129.2 0.6 copy-start.8
  129.7 0.6 copy-start.9
  135.9 6.6 %collective-permute-start.8 = (bf16[4,8,32,384]{3,2,1,0:T(8,128)(2,1)}, bf16[4,8,32,384]{3,2,1,0:T(8,128)(2,1)S(1)}, u32[]{:S(2)}, u32[]{:S(2)}) collective-permute-start(bf16[4,8,32,384]{3,2,1,0:T(8,128)(2,1)} %get-tuple-element.49), channel_id=1, source_target_pairs={{0,32},{32,0},{1,33},{33,1},{2,34},{34,2},{3,35},{35,3},{4,36},{36... | collective-permute-start | bytes 2359304 | tf_op jit(solution)/shard_map/sum_dx/ppermute | solution.py:238
  142.5 0.9 copy-start.3
  146.8 17.2 %all-to-all-start.2 = ((bf16[32,32,384]{2,1,0:T(8,128)(2,1)}), bf16[32,32,384]{2,1,0:T(8,128)(2,1)S(1)}, u32[]{:S(2)}, u32[]{:S(2)}) async-start(bf16[32,32,384]{2,1,0:T(8,128)(2,1)} %bitcast.44), calls=%async_computation.2 | async-start | bytes 1572864 | tf_op jit(solution)/shard_map/sum_dx/all_to_all | solution.py:234
  164.2 23.0 %all-to-all-start.3 = ((bf16[16,3,40,384]{3,2,1,0:T(8,128)(2,1)}), bf16[16,3,40,384]{3,2,1,0:T(8,128)(2,1)S(1)}, u32[]{:S(2)}, u32[]{:S(2)}) async-start(bf16[16,3,40,384]{3,2,1,0:T(8,128)(2,1)} %bitcast.43), calls=%async_computation.3 | async-start | bytes 2949120 | tf_op jit(solution)/shard_map/return_grads/all_to_all | solution.py:234
  168.4 21.5 %collective-permute-start.9 = (bf16[32,192]{1,0:T(8,128)(2,1)S(1)}, bf16[32,192]{1,0:T(8,128)(2,1)S(1)}, u32[]{:S(2)}, u32[]{:S(2)}) collective-permute-start(bf16[32,192]{1,0:T(8,128)(2,1)S(1)} %slice.27), channel_id=1, source_target_pairs={{0,64},{64,0},{1,65},{65,1},{2,66},{66,2},{3,67},{67,3},{4,68},{68... | collective-permute-start | bytes 36872 | tf_op jit(solution)/shard_map/ppermute | solution.py:238
  189.9 0.6 copy-start.10

commit v5 on v4

--- a/solution.py
+++ b/solution.py
@@ -78,33 +78,22 @@
     out_ref[...] = out.astype(BF16)
 
 
-def layout_kernel(w_ref, wx_ref, wd_ref):
-    low = jnp.zeros((STEP - Q, FSH), F32)
-    side = jnp.zeros((STEP, LANES - FSH), F32)
-    for g in range(NG):
-        for e in range(NE):
-            for i in range(3):
-                w = w_ref[g, e, i].astype(F32)
-                for s in range(4):
-                    piece = jnp.concatenate([w[:, s * FSH:(s + 1) * FSH], low], axis=0)
-                    piece = jnp.concatenate([piece, side], axis=1).astype(BF16)
-                    if i < 2:
-                        wx_ref[g, s * STEP:(s + 1) * STEP, e * PAIR + i * LANES:e * PAIR + (i + 1) * LANES] = piece
-                    else:
-                        wd_ref[g, s * STEP:(s + 1) * STEP, e * LANES:(e + 1) * LANES] = piece
-
-
-def forward_kernel(me_ref, x0_ref, x1_ref, wx_ref, wd_ref, keep_ref, give1_ref, give2_ref, give3_ref,
-                   xs_ref, ds_ref, gate_ref, slot_ref, pick_ref, pre_ref):
+def select_kernel(me_ref, a0_ref, b0_ref, a1_ref, b1_ref, xs_ref, ds_ref, gate_ref, slot_ref, pick_ref):
     first = me_ref[0] * NE
     lane = iota((HALF, LANES), 1)
     row, column = iota((HALF, HALF), 0), iota((HALF, HALF), 1)
     before = ones((column < row) & (column >= row - row % BLK))
     block = (iota((HALF, LANES), 0) // BLK).astype(F32)
     row = iota((HSLOTS, HALF), 0).astype(F32)
-    for h, x_ref in enumerate((x0_ref, x1_ref)):
+    pairs = ((a0_ref, b0_ref), (a1_ref, b1_ref))
+
+    def tokens(pair, g, lanes):
+        rows = HALF // 2
+        return jnp.concatenate([ref[:, g, :, lanes].reshape(rows, lanes.stop - lanes.start) for ref in pair], axis=0)
+
+    for h, pair in enumerate(pairs):
         at = slice(h * HALF, (h + 1) * HALF)
-        head = x_ref[:, 0, :, :LANES].reshape(HALF, LANES).astype(F32)
+        head = tokens(pair, 0, slice(0, LANES)).astype(F32)
         hit = jnp.zeros((HALF, LANES), F32)
         prob = jnp.zeros((HALF, LANES), F32)
         for k in range(TOP):
@@ -121,13 +110,29 @@
         for e in range(NE):
             gate_ref[e, h * HSLOTS:(h + 1) * HSLOTS, :] = gate[e * HSLOTS:(e + 1) * HSLOTS]
     for g in range(NG):
-        for h, x_ref in enumerate((x0_ref, x1_ref)):
-            x = dot(pick_ref[h], x_ref[:, g, :, :WIDE].reshape(HALF, WIDE)).astype(BF16)
-            dy = dot(pick_ref[h], x_ref[:, g, :, WIDE:].reshape(HALF, WIDE)).astype(BF16)
+        for h, pair in enumerate(pairs):
+            x = dot(pick_ref[h], tokens(pair, g, slice(0, WIDE))).astype(BF16)
+            dy = dot(pick_ref[h], tokens(pair, g, slice(WIDE, COLS))).astype(BF16)
             at = slice(h * HSLOTS, (h + 1) * HSLOTS)
             for e in range(NE):
                 xs_ref[g, e, at, :] = x[e * HSLOTS:(e + 1) * HSLOTS]
                 ds_ref[g, e, at, :] = dy[e * HSLOTS:(e + 1) * HSLOTS]
+
+
+def forward_kernel(me_ref, w_ref, xs_ref, ds_ref, keep_ref, give1_ref, give2_ref, give3_ref, wx_ref, wd_ref, pre_ref):
+    low = jnp.zeros((STEP - Q, FSH), F32)
+    side = jnp.zeros((STEP, LANES - FSH), F32)
+    for g in range(NG):
+        for e in range(NE):
+            for i in range(3):
+                w = w_ref[g, e, i].astype(F32)
+                for s in range(4):
+                    piece = jnp.concatenate([w[:, s * FSH:(s + 1) * FSH], low], axis=0)
+                    piece = jnp.concatenate([piece, side], axis=1).astype(BF16)
+                    if i < 2:
+                        wx_ref[g, s * STEP:(s + 1) * STEP, e * PAIR + i * LANES:e * PAIR + (i + 1) * LANES] = piece
+                    else:
+                        wd_ref[g, s * STEP:(s + 1) * STEP, e * LANES:(e + 1) * LANES] = piece
     for e in range(NE):
         ab = jnp.zeros((SLOTS, PAIR), F32)
         back = jnp.zeros((SLOTS, LANES), F32)
@@ -145,8 +150,7 @@
 
 def dx_of(spread, wx, tail):
     dx = dot_dims(spread, wx, 1, 1) + tail
-    dx = dx.reshape(NX, 2, SHARD, WIDE)
-    return jnp.concatenate([dx[:, 0], dx[:, 1]], axis=2)
+    return jnp.concatenate([dx[:HALF // 2], dx[HALF // 2:]], axis=1).reshape(NX, SHARD, COLS)
 
 
 def middle_kernel(me_ref, own_ref, pre1_ref, pre2_ref, pre3_ref, wx_ref, gate_ref, slot_ref,
@@ -248,25 +252,30 @@
     me = jnp.stack([group] + [zq ^ s for s in range(4)])
     small = [v.T for v in (scale_exp, route_ids, route_probs)]
     (xin,) = call(prepare_kernel, [((SHARD, COLS), BF16)], (stash, small[0], grad_out, small[1], small[2]))
-    other = swap(xin, "zh")
+    with jax.named_scope("gather_tokens"):
+        other = swap(xin, "zh")
+        a0 = exchange(jnp.tile(xin, (NX * NG, 1)), ("x",) + GROUP).reshape(NX, NG, SHARD, COLS)
+        other, a0 = lax.optimization_barrier((other, a0))
+        b0 = exchange(jnp.tile(other, (NX * NG, 1)), ("x",) + GROUP).reshape(NX, NG, SHARD, COLS)
+        a1 = swap(a0, "core")
+        b1 = swap(b0, "core")
     with jax.named_scope("move_weights"):
-        xin, w_gate, w_up, w_down = lax.optimization_barrier((xin, w_gate, w_up, w_down))
         tiles = [w.reshape(EXPERTS, 1, Q, 4 * FSH) for w in (w_gate, w_up, w_down)]
-        weights = exchange(jnp.concatenate(tiles, axis=1), GROUP)
-        weights = weights.reshape(NG, NE, 3, Q, 4 * FSH)
-    other, weights = lax.optimization_barrier((other, weights))
-    with jax.named_scope("gather_tokens"):
-        xin = jnp.tile(jnp.concatenate([xin, other]), (NX * NG, 1))
-        x0 = exchange(xin, ("x",) + GROUP).reshape(NX, NG, 2 * SHARD, COLS)
-        x1 = swap(x0, "core")
-    wx, wd = call(layout_kernel, [((NG, WIDE, NE * PAIR), BF16), ((NG, WIDE, NE * LANES), BF16)], (weights,))
+        weights, b0 = lax.optimization_barrier((jnp.concatenate(tiles, axis=1), b0))
+        weights = exchange(weights, GROUP).reshape(NG, NE, 3, Q, 4 * FSH)
+    rows = ((NG, NE, SLOTS, WIDE), BF16)
+    xs, ds, gate, slot = call(
+        select_kernel,
+        [rows, rows, ((NE, SLOTS, LANES), F32), ((TOKENS, LANES), F32)],
+        (me, a0, b0, a1, b1),
+        [((2, HALF, HALF), BF16)],
+        True)
     part = ((PART, PACK), BF16)
-    keep, give1, give2, give3, xs, ds, gate, slot = call(
+    keep, give1, give2, give3, wx = call(
         forward_kernel,
-        [((PART, PACK), F32), part, part, part, ((NG, NE, SLOTS, WIDE), BF16), ((NG, NE, SLOTS, WIDE), BF16),
-         ((NE, SLOTS, LANES), F32), ((TOKENS, LANES), F32)],
-        (me, x0, x1, wx, wd),
-        [((2, HALF, HALF), BF16), ((HSLOTS, PACK), F32)],
+        [((PART, PACK), F32), part, part, part, ((NG, WIDE, NE * PAIR), BF16)],
+        (me, weights, xs, ds),
+        [((NG, WIDE, NE * LANES), BF16), ((HSLOTS, PACK), F32)],
         True)
     with jax.named_scope("sum_pre"):
         got = [flip(give, "zq", 1 + i) for i, give in enumerate((give1, give2, give3))]

time: 193 us -> 188 us (0.974)
  blocking collectives: 26.3 us -> 0 us
  starting transfers between devices: 69.7 us -> 94.9 us
  waiting for transfers between devices: 54.6 us -> 49.6 us
    all_to_all x1 -> x0, blocking collectives: 26.3 us -> none  [exchange(): return lax.all_to_all(value, axis, split_axis=0, concat_axis=0, tiled=True)]
    all_to_all x3 -> x5, starting transfers between devices: 14 us -> 28.9 us  [exchange(): return lax.all_to_all(value, axis, split_axis=0, concat_axis=0, tiled=True)]
    ppermute x4 -> x5, starting transfers between devices: 29.3 us -> 39.6 us  [swap(): return lax.ppermute(value, axis, [(0, 1), (1, 0)])]
    ppermute x4 -> x5, waiting for transfers between devices: 17.4 us -> 10.5 us  [swap(): return lax.ppermute(value, axis, [(0, 1), (1, 0)])]
    all_to_all x3 -> x5, waiting for transfers between devices: 22.7 us -> 29.6 us  [exchange(): return lax.all_to_all(value, axis, split_axis=0, concat_axis=0, tiled=True)]
    ppermute x6, waiting for transfers between devices: 14.5 us -> 9.51 us  [flip(): lax.ppermute(value, axis, [(i, i ^ bit) for i in range(lax.axis_size(axis...]
    another operation x1 -> x2, local copies, waits for them, and re-layouts: 0.23 us -> 2.81 us  [the longest x1 1.76 us: local(): jnp.tile(xin, (NX * NG, 1))]
    unnamed x28 -> x32, local copies, waits for them, and re-layouts: 8.09 us -> 5.97 us
  transfers between devices with their start and end apart: 13 -> 16, of which waited for: 7 -> 9; matrix products, arithmetic and copies ran while one was open for 2% -> 3% of each run, Pallas kernels for 5% -> 6%
where the time goes in v5:
time: 188 us; the launch traced here: 187 us
  starting transfers between devices  94.9 us (50%)
  waiting for transfers between devices  49.6 us (26%)
  Pallas kernels  28.9 us (15%)
  local copies, waits for them, and re-layouts  10.3 us (5%)
  other arithmetic  2.4 us (1%)
    ppermute x5, starting transfers between devices, swap(): return lax.ppermute(value, axis, [(0, 1), (1, 0)])  39.6 us
    all_to_all x5, waiting for transfers between devices, exchange(): return lax.all_to_all(value, axis, split_axis=0, concat_axis=0, tiled=True)  29.6 us
    all_to_all x5, starting transfers between devices, exchange(): return lax.all_to_all(value, axis, split_axis=0, concat_axis=0, tiled=True)  28.9 us
    pallas_call x7, Pallas kernels, call(): pl.pallas_call(kernel, out_shape=[jax.ShapeDtypeStruct(shape, dtype) for...  28.9 us
    ppermute x6, starting transfers between devices, flip(): lax.ppermute(value, axis, [(i, i ^ bit) for i in range(lax.axis_size(axis...  26.3 us
    ppermute x5, waiting for transfers between devices, swap(): return lax.ppermute(value, axis, [(0, 1), (1, 0)])  10.5 us
    ppermute x6, waiting for transfers between devices, flip(): lax.ppermute(value, axis, [(i, i ^ bit) for i in range(lax.axis_size(axis...  9.51 us
    unnamed x32, local copies, waits for them, and re-layouts  5.97 us
  transfers between devices with their start and end apart: 16, of which 9 were waited for; matrix products, arithmetic and copies ran while one was open for 3% of the time, Pallas kernels for 6%

profile of v5, /device:TPU:1, one launch (start us, length us, event | category | flops | bytes accessed | tf_op | source)
XLA Modules:
  0.0 187.0 jit_solution(9770732170256200507)
XLA Ops:
  0.6 1.7 shard_map.119
  2.3 1.8 tile.4
  4.1 9.2 %all-to-all-start = ((bf16[32,32,384]{2,1,0:T(8,128)(2,1)}), bf16[32,32,384]{2,1,0:T(8,128)(2,1)S(1)}, u32[]{:S(2)}, u32[]{:S(2)}) async-start(bf16[32,32,384]{2,1,0:T(8,128)(2,1)} %tile.4), calls=%async_computation | async-start | bytes 1572864 | tf_op jit(solution)/shard_map/gather_tokens/all_to_all | solution.py:238
  13.3 0.0 copy-done.8
  13.3 0.0 copy-start.4
  13.3 14.7 %collective-permute-start = (bf16[32,384]{1,0:T(8,128)(2,1)S(1)}, bf16[32,384]{1,0:T(8,128)(2,1)S(1)}, u32[]{:S(2)}, u32[]{:S(2)}) collective-permute-start(bf16[32,384]{1,0:T(8,128)(2,1)S(1)} %copy-done.8), channel_id=1, source_target_pairs={{0,64},{64,0},{1,65},{65,1},{2,66},{66,2},{3,67},{67,3},{4,68},{68... | collective-permute-start | bytes 73736 | tf_op jit(solution)/shard_map/gather_tokens/ppermute | solution.py:242
  28.0 6.6 %collective-permute-done = bf16[32,384]{1,0:T(8,128)(2,1)S(1)} collective-permute-done((bf16[32,384]{1,0:T(8,128)(2,1)S(1)}, bf16[32,384]{1,0:T(8,128)(2,1)S(1)}, u32[]{:S(2)}, u32[]{:S(2)}) %collective-permute-start) | collective-permute-done | bytes 24608 | tf_op jit(solution)/shard_map/gather_tokens/ppermute | solution.py:242
  34.7 0.0 all-to-all-done
  34.7 1.0 tile.5
  35.7 7.7 %all-to-all-start.1 = ((bf16[32,32,384]{2,1,0:T(8,128)(2,1)}), bf16[32,32,384]{2,1,0:T(8,128)(2,1)S(1)}, u32[]{:S(2)}, u32[]{:S(2)}) async-start(bf16[32,32,384]{2,1,0:T(8,128)(2,1)} %tile.5), calls=%async_computation.1 | async-start | bytes 1572864 | tf_op jit(solution)/shard_map/gather_tokens/all_to_all | solution.py:238
  43.4 0.0 copy-done.4
  43.4 0.1 copy.16
  43.5 0.0 copy-done.5
  43.5 0.1 copy.17
  43.6 0.1 copy.18
  43.7 1.3 pad_maximum_fusion
  45.0 10.0 %all-to-all-done.1 = bf16[32,32,384]{2,1,0:T(8,128)(2,1)S(1)} async-done(((bf16[32,32,384]{2,1,0:T(8,128)(2,1)}), bf16[32,32,384]{2,1,0:T(8,128)(2,1)S(1)}, u32[]{:S(2)}, u32[]{:S(2)}) %all-to-all-start.1) | async-done | bytes 786464 | tf_op jit(solution)/shard_map/gather_tokens/all_to_all | solution.py:238
  54.9 3.6 %all-to-all-start.2 = ((bf16[16,3,40,384]{3,2,1,0:T(8,128)(2,1)}), bf16[16,3,40,384]{3,2,1,0:T(8,128)(2,1)S(1)}, u32[]{:S(2)}, u32[]{:S(2)}) async-start(bf16[16,3,40,384]{3,2,1,0:T(8,128)(2,1)} %pad_maximum_fusion), calls=%async_computation.2 | async-start | bytes 2949120 | tf_op jit(solution)/shard_map/move_weights/all_to_all | solution.py:238
  58.5 5.3 %collective-permute-start.1 = (bf16[4,8,32,384]{3,2,1,0:T(8,128)(2,1)S(1)}, bf16[4,8,32,384]{3,2,1,0:T(8,128)(2,1)}, u32[]{:S(2)}, u32[]{:S(2)}) collective-permute-start(bf16[4,8,32,384]{3,2,1,0:T(8,128)(2,1)S(1)} %bitcast.44), channel_id=1, source_target_pairs={{0,32},{32,0},{1,33},{33,1},{2,34},{34,2},{3,35},{35,3},{4,36},{36... | collective-permute-start | bytes 2359304 | tf_op jit(solution)/shard_map/gather_tokens/ppermute | solution.py:242
  63.9 1.9 %collective-permute-start.2 = (bf16[4,8,32,384]{3,2,1,0:T(8,128)(2,1)S(1)}, bf16[4,8,32,384]{3,2,1,0:T(8,128)(2,1)}, u32[]{:S(2)}, u32[]{:S(2)}) collective-permute-start(bf16[4,8,32,384]{3,2,1,0:T(8,128)(2,1)S(1)} %bitcast.46), channel_id=1, source_target_pairs={{0,32},{32,0},{1,33},{33,1},{2,34},{34,2},{3,35},{35,3},{4,36},{36... | collective-permute-start | bytes 2359304 | tf_op jit(solution)/shard_map/gather_tokens/ppermute | solution.py:242
  65.8 0.7 stack.23.me_ref
  66.5 0.0 collective-permute-done.1.a1_ref
  66.5 1.7 collective-permute-done.2.b1_ref
  68.2 6.0 %shard_map.120 = (bf16[8,2,256,192]{3,2,1,0:T(8,128)(2,1)}, bf16[8,2,256,192]{3,2,1,0:T(8,128)(2,1)}, f32[2,256,128]{2,1,0:T(8,128)}, f32[512,128]{1,0:T(8,128)}) custom-call(s32[5]{0:T(128)} %stack.23.me_ref, bf16[4,8,32,384]{3,2,1,0:T(8,128)(2,1)} %bitcast.45, bf16[4,8,32,384]{3,2,1,0:T(8,128)(2,1)} %bitcast.47, ...), custom_call_target="tpu_custom_call" | custom-call | tf_op jit(solution)/shard_map/pallas_call | solution.py:227
  74.2 0.1 all-to-all-done.2
  74.2 1.1 copy-done
  75.4 5.6 %shard_map.121 = (f32[32,1152]{1,0:T(8,128)}, bf16[32,1152]{1,0:T(8,128)(2,1)}, bf16[32,1152]{1,0:T(8,128)(2,1)}, bf16[32,1152]{1,0:T(8,128)(2,1)}, bf16[8,192,512]{2,1,0:T(8,128)(2,1)}) custom-call(s32[5]{0:T(128)} %stack.23.me_ref, bf16[8,2,3,40,384]{4,3,2,1,0:T(8,128)(2,1)} %bitcast.41, bf16[8,2,256,192]{3,2,1,0:T(8,128)(2,1)} %get-tuple-element.36.xs_ref, ...), custom_call_target="tpu_custom_call" | custom-call | tf_op jit(solution)/shard_map/pallas_call | solution.py:227
  81.0 3.1 %collective-permute-start.3 = (bf16[32,1152]{1,0:T(8,128)(2,1)}, bf16[32,1152]{1,0:T(8,128)(2,1)S(1)}, u32[]{:S(2)}, u32[]{:S(2)}) collective-permute-start(bf16[32,1152]{1,0:T(8,128)(2,1)} %get-tuple-element.39), channel_id=1, source_target_pairs={{0,8},{8,0},{16,24},{24,16},{1,9},{9,1},{17,25},{25,17},{2,10},{10... | collective-permute-start | bytes 221192 | tf_op jit(solution)/shard_map/sum_pre/ppermute | solution.py:246
  84.1 4.5 %collective-permute-start.4 = (bf16[32,1152]{1,0:T(8,128)(2,1)}, bf16[32,1152]{1,0:T(8,128)(2,1)S(1)}, u32[]{:S(2)}, u32[]{:S(2)}) collective-permute-start(bf16[32,1152]{1,0:T(8,128)(2,1)} %get-tuple-element.40), channel_id=1, source_target_pairs={{0,16},{8,24},{16,0},{24,8},{1,17},{9,25},{17,1},{25,9},{2,18},{10... | collective-permute-start | bytes 221192 | tf_op jit(solution)/shard_map/sum_pre/ppermute | solution.py:246
  88.6 5.6 %collective-permute-start.5 = (bf16[32,1152]{1,0:T(8,128)(2,1)}, bf16[32,1152]{1,0:T(8,128)(2,1)S(1)}, u32[]{:S(2)}, u32[]{:S(2)}) collective-permute-start(bf16[32,1152]{1,0:T(8,128)(2,1)} %get-tuple-element.41), channel_id=1, source_target_pairs={{0,24},{8,16},{16,8},{24,0},{1,25},{9,17},{17,9},{25,1},{2,26},{10... | collective-permute-start | bytes 221192 | tf_op jit(solution)/shard_map/sum_pre/ppermute | solution.py:246
  94.2 0.0 collective-permute-done.3
  94.2 0.0 collective-permute-done.4
  94.2 7.0 %collective-permute-done.5 = bf16[32,1152]{1,0:T(8,128)(2,1)S(1)} collective-permute-done((bf16[32,1152]{1,0:T(8,128)(2,1)}, bf16[32,1152]{1,0:T(8,128)(2,1)S(1)}, u32[]{:S(2)}, u32[]{:S(2)}) %collective-permute-start.5) | collective-permute-done | bytes 73760 | tf_op jit(solution)/shard_map/sum_pre/ppermute | solution.py:246
  101.2 1.0 add_convert_fusion.own_ref
  102.1 0.0 copy-start.7
  102.1 4.5 %collective-permute-start.8 = (bf16[32,1152]{1,0:T(8,128)(2,1)S(1)}, bf16[32,1152]{1,0:T(8,128)(2,1)S(1)}, u32[]{:S(2)}, u32[]{:S(2)}) collective-permute-start(bf16[32,1152]{1,0:T(8,128)(2,1)S(1)} %add_convert_fusion.own_ref), channel_id=1, source_target_pairs={{0,24},{8,16},{16,8},{24,0},{1,25},{9,17},{17,9},{25,1},{2,26},{10... | collective-permute-start | bytes 221192 | tf_op jit(solution)/shard_map/spread_pre/ppermute | solution.py:246
  106.6 1.9 %collective-permute-start.7 = (bf16[32,1152]{1,0:T(8,128)(2,1)S(1)}, bf16[32,1152]{1,0:T(8,128)(2,1)S(1)}, u32[]{:S(2)}, u32[]{:S(2)}) collective-permute-start(bf16[32,1152]{1,0:T(8,128)(2,1)S(1)} %add_convert_fusion.own_ref), channel_id=1, source_target_pairs={{0,16},{8,24},{16,0},{24,8},{1,17},{9,25},{17,1},{25,9},{2,18},{10... | collective-permute-start | bytes 221192 | tf_op jit(solution)/shard_map/spread_pre/ppermute | solution.py:246
  108.5 6.8 %collective-permute-start.6 = (bf16[32,1152]{1,0:T(8,128)(2,1)S(1)}, bf16[32,1152]{1,0:T(8,128)(2,1)S(1)}, u32[]{:S(2)}, u32[]{:S(2)}) collective-permute-start(bf16[32,1152]{1,0:T(8,128)(2,1)S(1)} %add_convert_fusion.own_ref), channel_id=1, source_target_pairs={{0,8},{8,0},{16,24},{24,16},{1,9},{9,1},{17,25},{25,17},{2,10},{10... | collective-permute-start | bytes 221192 | tf_op jit(solution)/shard_map/spread_pre/ppermute | solution.py:246
  115.4 0.0 collective-permute-done.8.pre3_ref
  115.4 2.5 %collective-permute-done.7.pre2_ref = bf16[32,1152]{1,0:T(8,128)(2,1)S(1)} collective-permute-done((bf16[32,1152]{1,0:T(8,128)(2,1)S(1)}, bf16[32,1152]{1,0:T(8,128)(2,1)S(1)}, u32[]{:S(2)}, u32[]{:S(2)}) %collective-permute-start.7) | collective-permute-done | bytes 73760 | tf_op jit(solution)/shard_map/spread_pre/ppermute | solution.py:246
  117.9 0.0 collective-permute-done.6.pre1_ref
  117.9 0.6 copy-done.10
  118.5 0.0 copy-done.11
  118.5 5.5 %shard_map.122 = (bf16[2,256,384]{2,1,0:T(8,128)(2,1)}, bf16[256,512]{1,0:T(8,128)(2,1)}, f32[256,128]{1,0:T(8,128)}, bf16[4,8,32,384]{3,2,1,0:T(8,128)(2,1)}) custom-call(s32[5]{0:T(128)} %stack.23.me_ref, bf16[32,1152]{1,0:T(8,128)(2,1)} %copy-done.7, bf16[32,1152]{1,0:T(8,128)(2,1)} %copy-done.11, bf16[32,1152]{1,0:T(8,128)(2,1)} %copy-done.10, ...), custom_call_target="tpu_custom_call" | custom-call | tf_op jit(solution)/shard_map/pallas_call | solution.py:227
  124.1 10.6 %collective-permute-start.9 = (bf16[4,8,32,384]{3,2,1,0:T(8,128)(2,1)}, bf16[4,8,32,384]{3,2,1,0:T(8,128)(2,1)S(1)}, u32[]{:S(2)}, u32[]{:S(2)}) collective-permute-start(bf16[4,8,32,384]{3,2,1,0:T(8,128)(2,1)} %get-tuple-element.45), channel_id=1, source_target_pairs={{0,32},{32,0},{1,33},{33,1},{2,34},{34,2},{3,35},{35,3},{4,36},{36... | collective-permute-start | bytes 2359304 | tf_op jit(solution)/shard_map/sum_dx/ppermute | solution.py:242
  134.6 2.1 %collective-permute-done.9.got_ref = bf16[4,8,32,384]{3,2,1,0:T(8,128)(2,1)S(1)} collective-permute-done((bf16[4,8,32,384]{3,2,1,0:T(8,128)(2,1)}, bf16[4,8,32,384]{3,2,1,0:T(8,128)(2,1)S(1)}, u32[]{:S(2)}, u32[]{:S(2)}) %collective-permute-start.9) | collective-permute-done | bytes 786464 | tf_op jit(solution)/shard_map/sum_dx/ppermute | solution.py:242
  136.8 0.9 copy-done.3
  137.6 3.4 %sum_dx.1 = bf16[4,8,32,384]{3,2,1,0:T(8,128)(2,1)} custom-call(bf16[4,8,32,384]{3,2,1,0:T(8,128)(2,1)} %copy-done.3, bf16[256,512]{1,0:T(8,128)(2,1)} %get-tuple-element.46.spread_ref, f32[256,128]{1,0:T(8,128)} %get-tuple-element.47.tail_ref, bf16[8,192,512]{2,1,0:T(8,128)(2,1)} %get-tuple-element.42.wx_ref), custom_call_target="tpu_custom_call" | custom-call | tf_op jit(solution)/shard_map/sum_dx/pallas_call | solution.py:227
  141.1 4.8 %all-to-all-start.3 = ((bf16[32,32,384]{2,1,0:T(8,128)(2,1)}), bf16[32,32,384]{2,1,0:T(8,128)(2,1)S(1)}, u32[]{:S(2)}, u32[]{:S(2)}) async-start(bf16[32,32,384]{2,1,0:T(8,128)(2,1)} %bitcast.43), calls=%async_computation.3 | async-start | bytes 1572864 | tf_op jit(solution)/shard_map/sum_dx/all_to_all | solution.py:238
  145.9 5.1 %shard_map.123 = bf16[8,2,3,40,384]{4,3,2,1,0:T(8,128)(2,1)} custom-call(bf16[8,2,256,192]{3,2,1,0:T(8,128)(2,1)} %get-tuple-element.36.xs_ref, bf16[8,2,256,192]{3,2,1,0:T(8,128)(2,1)} %get-tuple-element.37.ds_ref, bf16[2,256,384]{2,1,0:T(8,128)(2,1)} %get-tuple-element.50.d_ref), custom_call_target="tpu_custom_call" | custom-call | tf_op jit(solution)/shard_map/pallas_call | solution.py:227
  151.0 7.9 %all-to-all-done.3 = bf16[32,32,384]{2,1,0:T(8,128)(2,1)S(1)} async-done(((bf16[32,32,384]{2,1,0:T(8,128)(2,1)}), bf16[32,32,384]{2,1,0:T(8,128)(2,1)S(1)}, u32[]{:S(2)}, u32[]{:S(2)}) %all-to-all-start.3) | async-done | bytes 786464 | tf_op jit(solution)/shard_map/sum_dx/all_to_all | solution.py:238
  158.8 0.1 convert_reduce_fusion
  159.0 0.1 slice.27
  159.0 3.7 %all-to-all-start.4 = ((bf16[16,3,40,384]{3,2,1,0:T(8,128)(2,1)}), bf16[16,3,40,384]{3,2,1,0:T(8,128)(2,1)S(1)}, u32[]{:S(2)}, u32[]{:S(2)}) async-start(bf16[16,3,40,384]{3,2,1,0:T(8,128)(2,1)} %bitcast.42), calls=%async_computation.4 | async-start | bytes 2949120 | tf_op jit(solution)/shard_map/return_grads/all_to_all | solution.py:238
  162.7 0.6 slice.21.dx_ref
  163.3 7.1 %collective-permute-start.10 = (bf16[32,192]{1,0:T(8,128)(2,1)S(1)}, bf16[32,192]{1,0:T(8,128)(2,1)S(1)}, u32[]{:S(2)}, u32[]{:S(2)}) collective-permute-start(bf16[32,192]{1,0:T(8,128)(2,1)S(1)} %slice.27), channel_id=1, source_target_pairs={{0,64},{64,0},{1,65},{65,1},{2,66},{66,2},{3,67},{67,3},{4,68},{68... | collective-permute-start | bytes 36872 | tf_op jit(solution)/shard_map/ppermute | solution.py:242
  170.4 11.7 %all-to-all-done.4 = bf16[16,3,40,384]{3,2,1,0:T(8,128)(2,1)S(1)} async-done(((bf16[16,3,40,384]{3,2,1,0:T(8,128)(2,1)}), bf16[16,3,40,384]{3,2,1,0:T(8,128)(2,1)S(1)}, u32[]{:S(2)}, u32[]{:S(2)}) %all-to-all-start.4) | async-done | bytes 1474592 | tf_op jit(solution)/shard_map/return_grads/all_to_all | solution.py:238
  182.2 0.2 fusion
  182.3 0.8 copy.21
  183.2 0.8 copy.20
  184.0 0.8 copy.19
  184.9 0.0 collective-permute-done.10.got_ref
  184.9 0.6 copy-done.12
  185.4 1.5 shard_map.124
  (16 shorter events, 0.0 us)
Async XLA Ops:
  2.3 11.0 %copy-start.8 = (bf16[32,384]{1,0:T(8,128)(2,1)S(1)}, bf16[32,384]{1,0:T(8,128)(2,1)}, u32[]{:S(2)}) copy-start(bf16[32,384]{1,0:T(8,128)(2,1)} %shard_map.119) | copy-start | bytes 73732
  4.1 30.6 %all-to-all-start = ((bf16[32,32,384]{2,1,0:T(8,128)(2,1)}), bf16[32,32,384]{2,1,0:T(8,128)(2,1)S(1)}, u32[]{:S(2)}, u32[]{:S(2)}) async-start(bf16[32,32,384]{2,1,0:T(8,128)(2,1)} %tile.4), calls=%async_computation | async-start | bytes 1572864 | tf_op jit(solution)/shard_map/gather_tokens/all_to_all | solution.py:238
  13.3 30.1 %copy-start.4 = (bf16[16,15360]{1,0:T(8,128)(2,1)S(1)}, bf16[16,15360]{1,0:T(8,128)(2,1)}, u32[]{:S(2)}) copy-start(bf16[16,15360]{1,0:T(8,128)(2,1)} %param.13) | copy-start | bytes 1474564
  13.3 21.3 %collective-permute-start = (bf16[32,384]{1,0:T(8,128)(2,1)S(1)}, bf16[32,384]{1,0:T(8,128)(2,1)S(1)}, u32[]{:S(2)}, u32[]{:S(2)}) collective-permute-start(bf16[32,384]{1,0:T(8,128)(2,1)S(1)} %copy-done.8), channel_id=1, source_target_pairs={{0,64},{64,0},{1,65},{65,1},{2,66},{66,2},{3,67},{67,3},{4,68},{68... | collective-permute-start | bytes 73736 | tf_op jit(solution)/shard_map/gather_tokens/ppermute | solution.py:242
  34.7 23.9 %copy-start.1 = (bf16[32,32,384]{2,1,0:T(8,128)(2,1)}, bf16[32,32,384]{2,1,0:T(8,128)(2,1)S(1)}, u32[]{:S(2)}) copy-start(bf16[32,32,384]{2,1,0:T(8,128)(2,1)S(1)} %all-to-all-done) | copy-start | bytes 2359300
  35.7 7.8 %copy-start.5 = (bf16[16,15360]{1,0:T(8,128)(2,1)S(1)}, bf16[16,15360]{1,0:T(8,128)(2,1)}, u32[]{:S(2)}) copy-start(bf16[16,15360]{1,0:T(8,128)(2,1)} %param.14) | copy-start | bytes 1474564
  35.7 7.8 %copy-start.6 = (bf16[16,15360]{1,0:T(8,128)(2,1)S(1)}, bf16[16,15360]{1,0:T(8,128)(2,1)}, u32[]{:S(2)}) copy-start(bf16[16,15360]{1,0:T(8,128)(2,1)} %param.15) | copy-start | bytes 1474564
  35.7 19.2 %all-to-all-start.1 = ((bf16[32,32,384]{2,1,0:T(8,128)(2,1)}), bf16[32,32,384]{2,1,0:T(8,128)(2,1)S(1)}, u32[]{:S(2)}, u32[]{:S(2)}) async-start(bf16[32,32,384]{2,1,0:T(8,128)(2,1)} %tile.5), calls=%async_computation.1 | async-start | bytes 1572864 | tf_op jit(solution)/shard_map/gather_tokens/all_to_all | solution.py:238
  54.9 8.9 %copy-start.2 = (bf16[32,32,384]{2,1,0:T(8,128)(2,1)}, bf16[32,32,384]{2,1,0:T(8,128)(2,1)S(1)}, u32[]{:S(2)}) copy-start(bf16[32,32,384]{2,1,0:T(8,128)(2,1)S(1)} %all-to-all-done.1) | copy-start | bytes 2359300
  54.9 19.3 %all-to-all-start.2 = ((bf16[16,3,40,384]{3,2,1,0:T(8,128)(2,1)}), bf16[16,3,40,384]{3,2,1,0:T(8,128)(2,1)S(1)}, u32[]{:S(2)}, u32[]{:S(2)}) async-start(bf16[16,3,40,384]{3,2,1,0:T(8,128)(2,1)} %pad_maximum_fusion), calls=%async_computation.2 | async-start | bytes 2949120 | tf_op jit(solution)/shard_map/move_weights/all_to_all | solution.py:238
  58.5 7.9 %collective-permute-start.1 = (bf16[4,8,32,384]{3,2,1,0:T(8,128)(2,1)S(1)}, bf16[4,8,32,384]{3,2,1,0:T(8,128)(2,1)}, u32[]{:S(2)}, u32[]{:S(2)}) collective-permute-start(bf16[4,8,32,384]{3,2,1,0:T(8,128)(2,1)S(1)} %bitcast.44), channel_id=1, source_target_pairs={{0,32},{32,0},{1,33},{33,1},{2,34},{34,2},{3,35},{35,3},{4,36},{36... | collective-permute-start | bytes 2359304 | tf_op jit(solution)/shard_map/gather_tokens/ppermute | solution.py:242
  63.9 4.3 %collective-permute-start.2 = (bf16[4,8,32,384]{3,2,1,0:T(8,128)(2,1)S(1)}, bf16[4,8,32,384]{3,2,1,0:T(8,128)(2,1)}, u32[]{:S(2)}, u32[]{:S(2)}) collective-permute-start(bf16[4,8,32,384]{3,2,1,0:T(8,128)(2,1)S(1)} %bitcast.46), channel_id=1, source_target_pairs={{0,32},{32,0},{1,33},{33,1},{2,34},{34,2},{3,35},{35,3},{4,36},{36... | collective-permute-start | bytes 2359304 | tf_op jit(solution)/shard_map/gather_tokens/ppermute | solution.py:242
  74.2 1.1 copy-start
  81.0 13.2 %collective-permute-start.3 = (bf16[32,1152]{1,0:T(8,128)(2,1)}, bf16[32,1152]{1,0:T(8,128)(2,1)S(1)}, u32[]{:S(2)}, u32[]{:S(2)}) collective-permute-start(bf16[32,1152]{1,0:T(8,128)(2,1)} %get-tuple-element.39), channel_id=1, source_target_pairs={{0,8},{8,0},{16,24},{24,16},{1,9},{9,1},{17,25},{25,17},{2,10},{10... | collective-permute-start | bytes 221192 | tf_op jit(solution)/shard_map/sum_pre/ppermute | solution.py:246
  84.1 10.1 %collective-permute-start.4 = (bf16[32,1152]{1,0:T(8,128)(2,1)}, bf16[32,1152]{1,0:T(8,128)(2,1)S(1)}, u32[]{:S(2)}, u32[]{:S(2)}) collective-permute-start(bf16[32,1152]{1,0:T(8,128)(2,1)} %get-tuple-element.40), channel_id=1, source_target_pairs={{0,16},{8,24},{16,0},{24,8},{1,17},{9,25},{17,1},{25,9},{2,18},{10... | collective-permute-start | bytes 221192 | tf_op jit(solution)/shard_map/sum_pre/ppermute | solution.py:246
  88.6 12.6 %collective-permute-start.5 = (bf16[32,1152]{1,0:T(8,128)(2,1)}, bf16[32,1152]{1,0:T(8,128)(2,1)S(1)}, u32[]{:S(2)}, u32[]{:S(2)}) collective-permute-start(bf16[32,1152]{1,0:T(8,128)(2,1)} %get-tuple-element.41), channel_id=1, source_target_pairs={{0,24},{8,16},{16,8},{24,0},{1,25},{9,17},{17,9},{25,1},{2,26},{10... | collective-permute-start | bytes 221192 | tf_op jit(solution)/shard_map/sum_pre/ppermute | solution.py:246
  102.1 15.7 %copy-start.7 = (bf16[32,1152]{1,0:T(8,128)(2,1)}, bf16[32,1152]{1,0:T(8,128)(2,1)S(1)}, u32[]{:S(2)}) copy-start(bf16[32,1152]{1,0:T(8,128)(2,1)S(1)} %add_convert_fusion.own_ref) | copy-start | bytes 221188
  102.1 13.2 %collective-permute-start.8 = (bf16[32,1152]{1,0:T(8,128)(2,1)S(1)}, bf16[32,1152]{1,0:T(8,128)(2,1)S(1)}, u32[]{:S(2)}, u32[]{:S(2)}) collective-permute-start(bf16[32,1152]{1,0:T(8,128)(2,1)S(1)} %add_convert_fusion.own_ref), channel_id=1, source_target_pairs={{0,24},{8,16},{16,8},{24,0},{1,25},{9,17},{17,9},{25,1},{2,26},{10... | collective-permute-start | bytes 221192 | tf_op jit(solution)/shard_map/spread_pre/ppermute | solution.py:246
  106.6 11.3 %collective-permute-start.7 = (bf16[32,1152]{1,0:T(8,128)(2,1)S(1)}, bf16[32,1152]{1,0:T(8,128)(2,1)S(1)}, u32[]{:S(2)}, u32[]{:S(2)}) collective-permute-start(bf16[32,1152]{1,0:T(8,128)(2,1)S(1)} %add_convert_fusion.own_ref), channel_id=1, source_target_pairs={{0,16},{8,24},{16,0},{24,8},{1,17},{9,25},{17,1},{25,9},{2,18},{10... | collective-permute-start | bytes 221192 | tf_op jit(solution)/shard_map/spread_pre/ppermute | solution.py:246
  108.5 9.3 %collective-permute-start.6 = (bf16[32,1152]{1,0:T(8,128)(2,1)S(1)}, bf16[32,1152]{1,0:T(8,128)(2,1)S(1)}, u32[]{:S(2)}, u32[]{:S(2)}) collective-permute-start(bf16[32,1152]{1,0:T(8,128)(2,1)S(1)} %add_convert_fusion.own_ref), channel_id=1, source_target_pairs={{0,8},{8,0},{16,24},{24,16},{1,9},{9,1},{17,25},{25,17},{2,10},{10... | collective-permute-start | bytes 221192 | tf_op jit(solution)/shard_map/spread_pre/ppermute | solution.py:246
  115.4 2.5 %copy-start.9 = (bf16[32,1152]{1,0:T(8,128)(2,1)}, bf16[32,1152]{1,0:T(8,128)(2,1)S(1)}, u32[]{:S(2)}) copy-start(bf16[32,1152]{1,0:T(8,128)(2,1)S(1)} %collective-permute-done.8.pre3_ref) | copy-start | bytes 221188
  117.9 0.6 copy-start.10
  117.9 0.7 copy-start.11
  124.1 12.7 %collective-permute-start.9 = (bf16[4,8,32,384]{3,2,1,0:T(8,128)(2,1)}, bf16[4,8,32,384]{3,2,1,0:T(8,128)(2,1)S(1)}, u32[]{:S(2)}, u32[]{:S(2)}) collective-permute-start(bf16[4,8,32,384]{3,2,1,0:T(8,128)(2,1)} %get-tuple-element.45), channel_id=1, source_target_pairs={{0,32},{32,0},{1,33},{33,1},{2,34},{34,2},{3,35},{35,3},{4,36},{36... | collective-permute-start | bytes 2359304 | tf_op jit(solution)/shard_map/sum_dx/ppermute | solution.py:242
  136.7 0.9 copy-start.3
  141.1 17.8 %all-to-all-start.3 = ((bf16[32,32,384]{2,1,0:T(8,128)(2,1)}), bf16[32,32,384]{2,1,0:T(8,128)(2,1)S(1)}, u32[]{:S(2)}, u32[]{:S(2)}) async-start(bf16[32,32,384]{2,1,0:T(8,128)(2,1)} %bitcast.43), calls=%async_computation.3 | async-start | bytes 1572864 | tf_op jit(solution)/shard_map/sum_dx/all_to_all | solution.py:238
  159.0 23.1 %all-to-all-start.4 = ((bf16[16,3,40,384]{3,2,1,0:T(8,128)(2,1)}), bf16[16,3,40,384]{3,2,1,0:T(8,128)(2,1)S(1)}, u32[]{:S(2)}, u32[]{:S(2)}) async-start(bf16[16,3,40,384]{3,2,1,0:T(8,128)(2,1)} %bitcast.42), calls=%async_computation.4 | async-start | bytes 2949120 | tf_op jit(solution)/shard_map/return_grads/all_to_all | solution.py:238
  163.3 21.5 %collective-permute-start.10 = (bf16[32,192]{1,0:T(8,128)(2,1)S(1)}, bf16[32,192]{1,0:T(8,128)(2,1)S(1)}, u32[]{:S(2)}, u32[]{:S(2)}) collective-permute-start(bf16[32,192]{1,0:T(8,128)(2,1)S(1)} %slice.27), channel_id=1, source_target_pairs={{0,64},{64,0},{1,65},{65,1},{2,66},{66,2},{3,67},{67,3},{4,68},{68... | collective-permute-start | bytes 36872 | tf_op jit(solution)/shard_map/ppermute | solution.py:242
  184.9 0.6 copy-start.12

commit v6 on v5

--- a/solution.py
+++ b/solution.py
@@ -78,22 +78,20 @@
     out_ref[...] = out.astype(BF16)
 
 
-def select_kernel(me_ref, a0_ref, b0_ref, a1_ref, b1_ref, xs_ref, ds_ref, gate_ref, slot_ref, pick_ref):
+def select_kernel(me_ref, x0_ref, x1_ref, xs_ref, ds_ref, gate_ref, slot_ref, pick_ref):
     first = me_ref[0] * NE
     lane = iota((HALF, LANES), 1)
     row, column = iota((HALF, HALF), 0), iota((HALF, HALF), 1)
     before = ones((column < row) & (column >= row - row % BLK))
     block = (iota((HALF, LANES), 0) // BLK).astype(F32)
     row = iota((HSLOTS, HALF), 0).astype(F32)
-    pairs = ((a0_ref, b0_ref), (a1_ref, b1_ref))
-
-    def tokens(pair, g, lanes):
-        rows = HALF // 2
-        return jnp.concatenate([ref[:, g, :, lanes].reshape(rows, lanes.stop - lanes.start) for ref in pair], axis=0)
-
-    for h, pair in enumerate(pairs):
+
+    def tokens(x_ref, g, lanes):
+        return x_ref[:, g, :, lanes].reshape(HALF, lanes.stop - lanes.start)
+
+    for h, x_ref in enumerate((x0_ref, x1_ref)):
         at = slice(h * HALF, (h + 1) * HALF)
-        head = tokens(pair, 0, slice(0, LANES)).astype(F32)
+        head = tokens(x_ref, 0, slice(0, LANES)).astype(F32)
         hit = jnp.zeros((HALF, LANES), F32)
         prob = jnp.zeros((HALF, LANES), F32)
         for k in range(TOP):
@@ -110,9 +108,9 @@
         for e in range(NE):
             gate_ref[e, h * HSLOTS:(h + 1) * HSLOTS, :] = gate[e * HSLOTS:(e + 1) * HSLOTS]
     for g in range(NG):
-        for h, pair in enumerate(pairs):
-            x = dot(pick_ref[h], tokens(pair, g, slice(0, WIDE))).astype(BF16)
-            dy = dot(pick_ref[h], tokens(pair, g, slice(WIDE, COLS))).astype(BF16)
+        for h, x_ref in enumerate((x0_ref, x1_ref)):
+            x = dot(pick_ref[h], tokens(x_ref, g, slice(0, WIDE))).astype(BF16)
+            dy = dot(pick_ref[h], tokens(x_ref, g, slice(WIDE, COLS))).astype(BF16)
             at = slice(h * HSLOTS, (h + 1) * HSLOTS)
             for e in range(NE):
                 xs_ref[g, e, at, :] = x[e * HSLOTS:(e + 1) * HSLOTS]
@@ -150,7 +148,8 @@
 
 def dx_of(spread, wx, tail):
     dx = dot_dims(spread, wx, 1, 1) + tail
-    return jnp.concatenate([dx[:HALF // 2], dx[HALF // 2:]], axis=1).reshape(NX, SHARD, COLS)
+    dx = dx.reshape(NX, 2, SHARD, WIDE)
+    return jnp.concatenate([dx[:, 0], dx[:, 1]], axis=2)
 
 
 def middle_kernel(me_ref, own_ref, pre1_ref, pre2_ref, pre3_ref, wx_ref, gate_ref, slot_ref,
@@ -253,21 +252,18 @@
     small = [v.T for v in (scale_exp, route_ids, route_probs)]
     (xin,) = call(prepare_kernel, [((SHARD, COLS), BF16)], (stash, small[0], grad_out, small[1], small[2]))
     with jax.named_scope("gather_tokens"):
-        other = swap(xin, "zh")
-        a0 = exchange(jnp.tile(xin, (NX * NG, 1)), ("x",) + GROUP).reshape(NX, NG, SHARD, COLS)
-        other, a0 = lax.optimization_barrier((other, a0))
-        b0 = exchange(jnp.tile(other, (NX * NG, 1)), ("x",) + GROUP).reshape(NX, NG, SHARD, COLS)
-        a1 = swap(a0, "core")
-        b1 = swap(b0, "core")
+        xin = jnp.concatenate([xin, swap(xin, "zh")])
+        x0 = exchange(jnp.tile(xin, (NX * NG, 1)), ("x",) + GROUP).reshape(NX, NG, 2 * SHARD, COLS)
+        x1 = swap(x0, "core")
     with jax.named_scope("move_weights"):
         tiles = [w.reshape(EXPERTS, 1, Q, 4 * FSH) for w in (w_gate, w_up, w_down)]
-        weights, b0 = lax.optimization_barrier((jnp.concatenate(tiles, axis=1), b0))
+        weights, x0 = lax.optimization_barrier((jnp.concatenate(tiles, axis=1), x0))
         weights = exchange(weights, GROUP).reshape(NG, NE, 3, Q, 4 * FSH)
     rows = ((NG, NE, SLOTS, WIDE), BF16)
     xs, ds, gate, slot = call(
         select_kernel,
         [rows, rows, ((NE, SLOTS, LANES), F32), ((TOKENS, LANES), F32)],
-        (me, a0, b0, a1, b1),
+        (me, x0, x1),
         [((2, HALF, HALF), BF16)],
         True)
     part = ((PART, PACK), BF16)

time: 188 us -> 190 us (1.011); the launches traced: 187 us -> 187 us
  starting transfers between devices: 94.9 us -> 88.5 us
  waiting for transfers between devices: 49.6 us -> 55.7 us
    all_to_all x5 -> x4, starting transfers between devices: 28.9 us -> 21 us  [exchange(): return lax.all_to_all(value, axis, split_axis=0, concat_axis=0, tiled=True)]
    all_to_all x5 -> x4, waiting for transfers between devices: 29.6 us -> 37.1 us  [exchange(): return lax.all_to_all(value, axis, split_axis=0, concat_axis=0, tiled=True)]
    ppermute x5 -> x4, waiting for transfers between devices: 10.5 us -> 7.52 us  [swap(): return lax.ppermute(value, axis, [(0, 1), (1, 0)])]
    unnamed x32 -> x28, local copies, waits for them, and re-layouts: 5.97 us -> 6.8 us
    ppermute x5 -> x4, starting transfers between devices: 39.6 us -> 40.2 us  [swap(): return lax.ppermute(value, axis, [(0, 1), (1, 0)])]
  transfers between devices with their start and end apart: 16 -> 14, of which waited for: 9 -> 11; matrix products, arithmetic and copies ran while one was open for 3% -> 3% of each run, Pallas kernels for 6% -> 6%
where the time goes in v6:
time: 190 us; the launch traced here: 187 us
  starting transfers between devices  88.5 us (47%)
  waiting for transfers between devices  55.7 us (29%)
  Pallas kernels  29 us (15%)
  local copies, waits for them, and re-layouts  9.67 us (5%)
  other arithmetic  3.18 us (2%)
    ppermute x4, starting transfers between devices, swap(): return lax.ppermute(value, axis, [(0, 1), (1, 0)])  40.2 us
    all_to_all x4, waiting for transfers between devices, exchange(): return lax.all_to_all(value, axis, split_axis=0, concat_axis=0, tiled=True)  37.1 us
    pallas_call x7, Pallas kernels, call(): pl.pallas_call(kernel, out_shape=[jax.ShapeDtypeStruct(shape, dtype) for...  29 us
    ppermute x6, starting transfers between devices, flip(): lax.ppermute(value, axis, [(i, i ^ bit) for i in range(lax.axis_size(axis...  27.3 us
    all_to_all x4, starting transfers between devices, exchange(): return lax.all_to_all(value, axis, split_axis=0, concat_axis=0, tiled=True)  21 us
    ppermute x6, waiting for transfers between devices, flip(): lax.ppermute(value, axis, [(i, i ^ bit) for i in range(lax.axis_size(axis...  11.1 us
    ppermute x4, waiting for transfers between devices, swap(): return lax.ppermute(value, axis, [(0, 1), (1, 0)])  7.52 us
    unnamed x28, local copies, waits for them, and re-layouts  6.8 us
  transfers between devices with their start and end apart: 14, of which 11 were waited for; matrix products, arithmetic and copies ran while one was open for 3% of the time, Pallas kernels for 6%

profile of v6, /device:TPU:1, one launch (start us, length us, event | category | flops | bytes accessed | tf_op | source)
XLA Modules:
  0.0 186.9 jit_solution(6810351703814003655)
XLA Ops:
  0.6 1.7 shard_map.119
  2.3 16.3 %collective-permute-start = (bf16[32,384]{1,0:T(8,128)(2,1)}, bf16[32,384]{1,0:T(8,128)(2,1)S(1)}, u32[]{:S(2)}, u32[]{:S(2)}) collective-permute-start(bf16[32,384]{1,0:T(8,128)(2,1)} %shard_map.119), channel_id=1, source_target_pairs={{0,64},{64,0},{1,65},{65,1},{2,66},{66,2},{3,67},{67,3},{4,68},{68... | collective-permute-start | bytes 73736 | tf_op jit(solution)/shard_map/gather_tokens/ppermute | solution.py:241
  18.6 1.5 collective-permute-done
  20.1 0.7 pad_maximum_fusion.1
  20.9 1.4 tile.2
  22.3 7.5 %all-to-all-start = ((bf16[32,64,384]{2,1,0:T(8,128)(2,1)}), bf16[32,64,384]{2,1,0:T(8,128)(2,1)S(1)}, u32[]{:S(2)}, u32[]{:S(2)}) async-start(bf16[32,64,384]{2,1,0:T(8,128)(2,1)} %tile.2), calls=%async_computation | async-start | bytes 3145728 | tf_op jit(solution)/shard_map/gather_tokens/all_to_all | solution.py:237
  29.8 0.0 copy-start.5
  29.8 0.0 copy-done.3
  29.8 0.1 copy.16
  29.9 0.0 copy-done.4
  29.9 0.1 copy.17
  30.0 0.9 copy-done.5
  30.9 0.1 copy.18
  30.9 1.4 pad_maximum_fusion
  32.3 17.4 %all-to-all-done = bf16[32,64,384]{2,1,0:T(8,128)(2,1)S(1)} async-done(((bf16[32,64,384]{2,1,0:T(8,128)(2,1)}), bf16[32,64,384]{2,1,0:T(8,128)(2,1)S(1)}, u32[]{:S(2)}, u32[]{:S(2)}) %all-to-all-start) | async-done | bytes 1572896 | tf_op jit(solution)/shard_map/gather_tokens/all_to_all | solution.py:237
  49.7 4.3 %all-to-all-start.1 = ((bf16[16,3,40,384]{3,2,1,0:T(8,128)(2,1)}), bf16[16,3,40,384]{3,2,1,0:T(8,128)(2,1)S(1)}, u32[]{:S(2)}, u32[]{:S(2)}) async-start(bf16[16,3,40,384]{3,2,1,0:T(8,128)(2,1)} %pad_maximum_fusion), calls=%async_computation.1 | async-start | bytes 2949120 | tf_op jit(solution)/shard_map/move_weights/all_to_all | solution.py:237
  54.0 0.0 copy-done
  54.0 4.8 %collective-permute-start.1 = (bf16[4,8,64,384]{3,2,1,0:T(8,128)(2,1)S(1)}, bf16[4,8,64,384]{3,2,1,0:T(8,128)(2,1)}, u32[]{:S(2)}, u32[]{:S(2)}) collective-permute-start(bf16[4,8,64,384]{3,2,1,0:T(8,128)(2,1)S(1)} %bitcast.40), channel_id=1, source_target_pairs={{0,32},{32,0},{1,33},{33,1},{2,34},{34,2},{3,35},{35,3},{4,36},{36... | collective-permute-start | bytes 4718600 | tf_op jit(solution)/shard_map/gather_tokens/ppermute | solution.py:241
  58.8 0.6 stack.23.me_ref
  59.4 2.5 %collective-permute-done.1.x1_ref = bf16[4,8,64,384]{3,2,1,0:T(8,128)(2,1)} collective-permute-done((bf16[4,8,64,384]{3,2,1,0:T(8,128)(2,1)S(1)}, bf16[4,8,64,384]{3,2,1,0:T(8,128)(2,1)}, u32[]{:S(2)}, u32[]{:S(2)}) %collective-permute-start.1) | collective-permute-done | bytes 1572896 | tf_op jit(solution)/shard_map/gather_tokens/ppermute | solution.py:241
  62.0 6.0 %shard_map.120 = (bf16[8,2,256,192]{3,2,1,0:T(8,128)(2,1)}, bf16[8,2,256,192]{3,2,1,0:T(8,128)(2,1)}, f32[2,256,128]{2,1,0:T(8,128)}, f32[512,128]{1,0:T(8,128)}) custom-call(s32[5]{0:T(128)} %stack.23.me_ref, bf16[4,8,64,384]{3,2,1,0:T(8,128)(2,1)} %bitcast.41, bf16[4,8,64,384]{3,2,1,0:T(8,128)(2,1)} %collective-permute-done.1.x1_ref), custom_call_target="tpu_custom_call" | custom-call | tf_op jit(solution)/shard_map/pallas_call | solution.py:226
  68.0 2.8 %all-to-all-done.1 = bf16[16,3,40,384]{3,2,1,0:T(8,128)(2,1)S(1)} async-done(((bf16[16,3,40,384]{3,2,1,0:T(8,128)(2,1)}), bf16[16,3,40,384]{3,2,1,0:T(8,128)(2,1)S(1)}, u32[]{:S(2)}, u32[]{:S(2)}) %all-to-all-start.1) | async-done | bytes 1474592 | tf_op jit(solution)/shard_map/move_weights/all_to_all | solution.py:237
  70.8 1.1 copy-done.1
  71.9 5.6 %shard_map.121 = (f32[32,1152]{1,0:T(8,128)}, bf16[32,1152]{1,0:T(8,128)(2,1)}, bf16[32,1152]{1,0:T(8,128)(2,1)}, bf16[32,1152]{1,0:T(8,128)(2,1)}, bf16[8,192,512]{2,1,0:T(8,128)(2,1)}) custom-call(s32[5]{0:T(128)} %stack.23.me_ref, bf16[8,2,3,40,384]{4,3,2,1,0:T(8,128)(2,1)} %bitcast.42, bf16[8,2,256,192]{3,2,1,0:T(8,128)(2,1)} %get-tuple-element.32.xs_ref, ...), custom_call_target="tpu_custom_call" | custom-call | tf_op jit(solution)/shard_map/pallas_call | solution.py:226
  77.5 4.1 %collective-permute-start.2 = (bf16[32,1152]{1,0:T(8,128)(2,1)}, bf16[32,1152]{1,0:T(8,128)(2,1)S(1)}, u32[]{:S(2)}, u32[]{:S(2)}) collective-permute-start(bf16[32,1152]{1,0:T(8,128)(2,1)} %get-tuple-element.35), channel_id=1, source_target_pairs={{0,8},{8,0},{16,24},{24,16},{1,9},{9,1},{17,25},{25,17},{2,10},{10... | collective-permute-start | bytes 221192 | tf_op jit(solution)/shard_map/sum_pre/ppermute | solution.py:245
  81.6 8.1 %collective-permute-start.3 = (bf16[32,1152]{1,0:T(8,128)(2,1)}, bf16[32,1152]{1,0:T(8,128)(2,1)S(1)}, u32[]{:S(2)}, u32[]{:S(2)}) collective-permute-start(bf16[32,1152]{1,0:T(8,128)(2,1)} %get-tuple-element.36), channel_id=1, source_target_pairs={{0,16},{8,24},{16,0},{24,8},{1,17},{9,25},{17,1},{25,9},{2,18},{10... | collective-permute-start | bytes 221192 | tf_op jit(solution)/shard_map/sum_pre/ppermute | solution.py:245
  89.7 1.9 %collective-permute-start.4 = (bf16[32,1152]{1,0:T(8,128)(2,1)}, bf16[32,1152]{1,0:T(8,128)(2,1)S(1)}, u32[]{:S(2)}, u32[]{:S(2)}) collective-permute-start(bf16[32,1152]{1,0:T(8,128)(2,1)} %get-tuple-element.37), channel_id=1, source_target_pairs={{0,24},{8,16},{16,8},{24,0},{1,25},{9,17},{17,9},{25,1},{2,26},{10... | collective-permute-start | bytes 221192 | tf_op jit(solution)/shard_map/sum_pre/ppermute | solution.py:245
  91.6 0.0 collective-permute-done.2
  91.6 0.5 collective-permute-done.3
  92.2 8.6 %collective-permute-done.4 = bf16[32,1152]{1,0:T(8,128)(2,1)S(1)} collective-permute-done((bf16[32,1152]{1,0:T(8,128)(2,1)}, bf16[32,1152]{1,0:T(8,128)(2,1)S(1)}, u32[]{:S(2)}, u32[]{:S(2)}) %collective-permute-start.4) | collective-permute-done | bytes 73760 | tf_op jit(solution)/shard_map/sum_pre/ppermute | solution.py:245
  100.7 0.9 add_convert_fusion.own_ref
  101.7 0.0 copy-start.6
  101.7 2.1 %collective-permute-start.7 = (bf16[32,1152]{1,0:T(8,128)(2,1)S(1)}, bf16[32,1152]{1,0:T(8,128)(2,1)S(1)}, u32[]{:S(2)}, u32[]{:S(2)}) collective-permute-start(bf16[32,1152]{1,0:T(8,128)(2,1)S(1)} %add_convert_fusion.own_ref), channel_id=1, source_target_pairs={{0,24},{8,16},{16,8},{24,0},{1,25},{9,17},{17,9},{25,1},{2,26},{10... | collective-permute-start | bytes 221192 | tf_op jit(solution)/shard_map/spread_pre/ppermute | solution.py:245
  103.8 3.5 %collective-permute-start.6 = (bf16[32,1152]{1,0:T(8,128)(2,1)S(1)}, bf16[32,1152]{1,0:T(8,128)(2,1)S(1)}, u32[]{:S(2)}, u32[]{:S(2)}) collective-permute-start(bf16[32,1152]{1,0:T(8,128)(2,1)S(1)} %add_convert_fusion.own_ref), channel_id=1, source_target_pairs={{0,16},{8,24},{16,0},{24,8},{1,17},{9,25},{17,1},{25,9},{2,18},{10... | collective-permute-start | bytes 221192 | tf_op jit(solution)/shard_map/spread_pre/ppermute | solution.py:245
  107.4 7.5 %collective-permute-start.5 = (bf16[32,1152]{1,0:T(8,128)(2,1)S(1)}, bf16[32,1152]{1,0:T(8,128)(2,1)S(1)}, u32[]{:S(2)}, u32[]{:S(2)}) collective-permute-start(bf16[32,1152]{1,0:T(8,128)(2,1)S(1)} %add_convert_fusion.own_ref), channel_id=1, source_target_pairs={{0,8},{8,0},{16,24},{24,16},{1,9},{9,1},{17,25},{25,17},{2,10},{10... | collective-permute-start | bytes 221192 | tf_op jit(solution)/shard_map/spread_pre/ppermute | solution.py:245
  114.9 0.0 collective-permute-done.7.pre3_ref
  114.9 0.0 copy-start.7
  114.9 0.0 collective-permute-done.6.pre2_ref
  114.9 0.0 copy-start.8
  114.9 2.0 %collective-permute-done.5.pre1_ref = bf16[32,1152]{1,0:T(8,128)(2,1)S(1)} collective-permute-done((bf16[32,1152]{1,0:T(8,128)(2,1)S(1)}, bf16[32,1152]{1,0:T(8,128)(2,1)S(1)}, u32[]{:S(2)}, u32[]{:S(2)}) %collective-permute-start.5) | collective-permute-done | bytes 73760 | tf_op jit(solution)/shard_map/spread_pre/ppermute | solution.py:245
  116.9 0.0 copy-done.6
  116.9 0.0 copy-done.7
  116.9 0.6 copy-done.9
  117.5 5.6 %shard_map.122 = (bf16[2,256,384]{2,1,0:T(8,128)(2,1)}, bf16[256,512]{1,0:T(8,128)(2,1)}, f32[256,128]{1,0:T(8,128)}, bf16[4,8,32,384]{3,2,1,0:T(8,128)(2,1)}) custom-call(s32[5]{0:T(128)} %stack.23.me_ref, bf16[32,1152]{1,0:T(8,128)(2,1)} %copy-done.6, bf16[32,1152]{1,0:T(8,128)(2,1)} %copy-done.9, bf16[32,1152]{1,0:T(8,128)(2,1)} %copy-done.8, ...), custom_call_target="tpu_custom_call" | custom-call | tf_op jit(solution)/shard_map/pallas_call | solution.py:226
  123.1 9.4 %collective-permute-start.8 = (bf16[4,8,32,384]{3,2,1,0:T(8,128)(2,1)}, bf16[4,8,32,384]{3,2,1,0:T(8,128)(2,1)S(1)}, u32[]{:S(2)}, u32[]{:S(2)}) collective-permute-start(bf16[4,8,32,384]{3,2,1,0:T(8,128)(2,1)} %get-tuple-element.41), channel_id=1, source_target_pairs={{0,32},{32,0},{1,33},{33,1},{2,34},{34,2},{3,35},{35,3},{4,36},{36... | collective-permute-start | bytes 2359304 | tf_op jit(solution)/shard_map/sum_dx/ppermute | solution.py:241
  132.5 2.1 %collective-permute-done.8.got_ref = bf16[4,8,32,384]{3,2,1,0:T(8,128)(2,1)S(1)} collective-permute-done((bf16[4,8,32,384]{3,2,1,0:T(8,128)(2,1)}, bf16[4,8,32,384]{3,2,1,0:T(8,128)(2,1)S(1)}, u32[]{:S(2)}, u32[]{:S(2)}) %collective-permute-start.8) | collective-permute-done | bytes 786464 | tf_op jit(solution)/shard_map/sum_dx/ppermute | solution.py:241
  134.6 0.9 copy-done.2
  135.5 3.5 %sum_dx.1 = bf16[4,8,32,384]{3,2,1,0:T(8,128)(2,1)} custom-call(bf16[4,8,32,384]{3,2,1,0:T(8,128)(2,1)} %copy-done.2, bf16[256,512]{1,0:T(8,128)(2,1)} %get-tuple-element.42.spread_ref, f32[256,128]{1,0:T(8,128)} %get-tuple-element.43.tail_ref, bf16[8,192,512]{2,1,0:T(8,128)(2,1)} %get-tuple-element.38.wx_ref), custom_call_target="tpu_custom_call" | custom-call | tf_op jit(solution)/shard_map/sum_dx/pallas_call | solution.py:226
  138.9 5.4 %all-to-all-start.2 = ((bf16[32,32,384]{2,1,0:T(8,128)(2,1)}), bf16[32,32,384]{2,1,0:T(8,128)(2,1)S(1)}, u32[]{:S(2)}, u32[]{:S(2)}) async-start(bf16[32,32,384]{2,1,0:T(8,128)(2,1)} %bitcast.44), calls=%async_computation.2 | async-start | bytes 1572864 | tf_op jit(solution)/shard_map/sum_dx/all_to_all | solution.py:237
  144.4 5.1 %shard_map.123 = bf16[8,2,3,40,384]{4,3,2,1,0:T(8,128)(2,1)} custom-call(bf16[8,2,256,192]{3,2,1,0:T(8,128)(2,1)} %get-tuple-element.32.xs_ref, bf16[8,2,256,192]{3,2,1,0:T(8,128)(2,1)} %get-tuple-element.33.ds_ref, bf16[2,256,384]{2,1,0:T(8,128)(2,1)} %get-tuple-element.46.d_ref), custom_call_target="tpu_custom_call" | custom-call | tf_op jit(solution)/shard_map/pallas_call | solution.py:226
  149.5 7.8 %all-to-all-done.2 = bf16[32,32,384]{2,1,0:T(8,128)(2,1)S(1)} async-done(((bf16[32,32,384]{2,1,0:T(8,128)(2,1)}), bf16[32,32,384]{2,1,0:T(8,128)(2,1)S(1)}, u32[]{:S(2)}, u32[]{:S(2)}) %all-to-all-start.2) | async-done | bytes 786464 | tf_op jit(solution)/shard_map/sum_dx/all_to_all | solution.py:237
  157.4 0.1 convert_reduce_fusion
  157.5 0.1 slice.27
  157.6 3.7 %all-to-all-start.3 = ((bf16[16,3,40,384]{3,2,1,0:T(8,128)(2,1)}), bf16[16,3,40,384]{3,2,1,0:T(8,128)(2,1)S(1)}, u32[]{:S(2)}, u32[]{:S(2)}) async-start(bf16[16,3,40,384]{3,2,1,0:T(8,128)(2,1)} %bitcast.43), calls=%async_computation.3 | async-start | bytes 2949120 | tf_op jit(solution)/shard_map/return_grads/all_to_all | solution.py:237
  161.2 0.6 slice.21.dx_ref
  161.8 9.7 %collective-permute-start.9 = (bf16[32,192]{1,0:T(8,128)(2,1)S(1)}, bf16[32,192]{1,0:T(8,128)(2,1)S(1)}, u32[]{:S(2)}, u32[]{:S(2)}) collective-permute-start(bf16[32,192]{1,0:T(8,128)(2,1)S(1)} %slice.27), channel_id=1, source_target_pairs={{0,64},{64,0},{1,65},{65,1},{2,66},{66,2},{3,67},{67,3},{4,68},{68... | collective-permute-start | bytes 36872 | tf_op jit(solution)/shard_map/ppermute | solution.py:241
  171.6 9.1 %all-to-all-done.3 = bf16[16,3,40,384]{3,2,1,0:T(8,128)(2,1)S(1)} async-done(((bf16[16,3,40,384]{3,2,1,0:T(8,128)(2,1)}), bf16[16,3,40,384]{3,2,1,0:T(8,128)(2,1)S(1)}, u32[]{:S(2)}, u32[]{:S(2)}) %all-to-all-start.3) | async-done | bytes 1474592 | tf_op jit(solution)/shard_map/return_grads/all_to_all | solution.py:237
  180.7 0.2 fusion
  180.9 0.8 copy.21
  181.7 0.8 copy.20
  182.5 0.8 copy.19
  183.4 1.4 collective-permute-done.9.got_ref
  184.8 0.6 copy-done.10
  185.4 1.5 shard_map.124
  (8 shorter events, 0.0 us)
Async XLA Ops:
  2.3 17.8 %collective-permute-start = (bf16[32,384]{1,0:T(8,128)(2,1)}, bf16[32,384]{1,0:T(8,128)(2,1)S(1)}, u32[]{:S(2)}, u32[]{:S(2)}) collective-permute-start(bf16[32,384]{1,0:T(8,128)(2,1)} %shard_map.119), channel_id=1, source_target_pairs={{0,64},{64,0},{1,65},{65,1},{2,66},{66,2},{3,67},{67,3},{4,68},{68... | collective-permute-start | bytes 73736 | tf_op jit(solution)/shard_map/gather_tokens/ppermute | solution.py:241
  22.3 7.6 %copy-start.3 = (bf16[16,15360]{1,0:T(8,128)(2,1)S(1)}, bf16[16,15360]{1,0:T(8,128)(2,1)}, u32[]{:S(2)}) copy-start(bf16[16,15360]{1,0:T(8,128)(2,1)} %param.13) | copy-start | bytes 1474564
  22.3 7.6 %copy-start.4 = (bf16[16,15360]{1,0:T(8,128)(2,1)S(1)}, bf16[16,15360]{1,0:T(8,128)(2,1)}, u32[]{:S(2)}) copy-start(bf16[16,15360]{1,0:T(8,128)(2,1)} %param.14) | copy-start | bytes 1474564
  22.3 27.4 %all-to-all-start = ((bf16[32,64,384]{2,1,0:T(8,128)(2,1)}), bf16[32,64,384]{2,1,0:T(8,128)(2,1)S(1)}, u32[]{:S(2)}, u32[]{:S(2)}) async-start(bf16[32,64,384]{2,1,0:T(8,128)(2,1)} %tile.2), calls=%async_computation | async-start | bytes 3145728 | tf_op jit(solution)/shard_map/gather_tokens/all_to_all | solution.py:237
  29.8 1.0 copy-start.5
  49.7 4.3 %copy-start = (bf16[32,64,384]{2,1,0:T(8,128)(2,1)}, bf16[32,64,384]{2,1,0:T(8,128)(2,1)S(1)}, u32[]{:S(2)}) copy-start(bf16[32,64,384]{2,1,0:T(8,128)(2,1)S(1)} %all-to-all-done) | copy-start | bytes 4718596
  49.7 21.1 %all-to-all-start.1 = ((bf16[16,3,40,384]{3,2,1,0:T(8,128)(2,1)}), bf16[16,3,40,384]{3,2,1,0:T(8,128)(2,1)S(1)}, u32[]{:S(2)}, u32[]{:S(2)}) async-start(bf16[16,3,40,384]{3,2,1,0:T(8,128)(2,1)} %pad_maximum_fusion), calls=%async_computation.1 | async-start | bytes 2949120 | tf_op jit(solution)/shard_map/move_weights/all_to_all | solution.py:237
  54.0 7.9 %collective-permute-start.1 = (bf16[4,8,64,384]{3,2,1,0:T(8,128)(2,1)S(1)}, bf16[4,8,64,384]{3,2,1,0:T(8,128)(2,1)}, u32[]{:S(2)}, u32[]{:S(2)}) collective-permute-start(bf16[4,8,64,384]{3,2,1,0:T(8,128)(2,1)S(1)} %bitcast.40), channel_id=1, source_target_pairs={{0,32},{32,0},{1,33},{33,1},{2,34},{34,2},{3,35},{35,3},{4,36},{36... | collective-permute-start | bytes 4718600 | tf_op jit(solution)/shard_map/gather_tokens/ppermute | solution.py:241
  70.8 1.1 copy-start.1
  77.5 14.1 %collective-permute-start.2 = (bf16[32,1152]{1,0:T(8,128)(2,1)}, bf16[32,1152]{1,0:T(8,128)(2,1)S(1)}, u32[]{:S(2)}, u32[]{:S(2)}) collective-permute-start(bf16[32,1152]{1,0:T(8,128)(2,1)} %get-tuple-element.35), channel_id=1, source_target_pairs={{0,8},{8,0},{16,24},{24,16},{1,9},{9,1},{17,25},{25,17},{2,10},{10... | collective-permute-start | bytes 221192 | tf_op jit(solution)/shard_map/sum_pre/ppermute | solution.py:245
  81.6 10.5 %collective-permute-start.3 = (bf16[32,1152]{1,0:T(8,128)(2,1)}, bf16[32,1152]{1,0:T(8,128)(2,1)S(1)}, u32[]{:S(2)}, u32[]{:S(2)}) collective-permute-start(bf16[32,1152]{1,0:T(8,128)(2,1)} %get-tuple-element.36), channel_id=1, source_target_pairs={{0,16},{8,24},{16,0},{24,8},{1,17},{9,25},{17,1},{25,9},{2,18},{10... | collective-permute-start | bytes 221192 | tf_op jit(solution)/shard_map/sum_pre/ppermute | solution.py:245
  89.7 11.0 %collective-permute-start.4 = (bf16[32,1152]{1,0:T(8,128)(2,1)}, bf16[32,1152]{1,0:T(8,128)(2,1)S(1)}, u32[]{:S(2)}, u32[]{:S(2)}) collective-permute-start(bf16[32,1152]{1,0:T(8,128)(2,1)} %get-tuple-element.37), channel_id=1, source_target_pairs={{0,24},{8,16},{16,8},{24,0},{1,25},{9,17},{17,9},{25,1},{2,26},{10... | collective-permute-start | bytes 221192 | tf_op jit(solution)/shard_map/sum_pre/ppermute | solution.py:245
  101.7 15.2 %copy-start.6 = (bf16[32,1152]{1,0:T(8,128)(2,1)}, bf16[32,1152]{1,0:T(8,128)(2,1)S(1)}, u32[]{:S(2)}) copy-start(bf16[32,1152]{1,0:T(8,128)(2,1)S(1)} %add_convert_fusion.own_ref) | copy-start | bytes 221188
  101.7 13.2 %collective-permute-start.7 = (bf16[32,1152]{1,0:T(8,128)(2,1)S(1)}, bf16[32,1152]{1,0:T(8,128)(2,1)S(1)}, u32[]{:S(2)}, u32[]{:S(2)}) collective-permute-start(bf16[32,1152]{1,0:T(8,128)(2,1)S(1)} %add_convert_fusion.own_ref), channel_id=1, source_target_pairs={{0,24},{8,16},{16,8},{24,0},{1,25},{9,17},{17,9},{25,1},{2,26},{10... | collective-permute-start | bytes 221192 | tf_op jit(solution)/shard_map/spread_pre/ppermute | solution.py:245
  103.8 11.1 %collective-permute-start.6 = (bf16[32,1152]{1,0:T(8,128)(2,1)S(1)}, bf16[32,1152]{1,0:T(8,128)(2,1)S(1)}, u32[]{:S(2)}, u32[]{:S(2)}) collective-permute-start(bf16[32,1152]{1,0:T(8,128)(2,1)S(1)} %add_convert_fusion.own_ref), channel_id=1, source_target_pairs={{0,16},{8,24},{16,0},{24,8},{1,17},{9,25},{17,1},{25,9},{2,18},{10... | collective-permute-start | bytes 221192 | tf_op jit(solution)/shard_map/spread_pre/ppermute | solution.py:245
  107.4 9.5 %collective-permute-start.5 = (bf16[32,1152]{1,0:T(8,128)(2,1)S(1)}, bf16[32,1152]{1,0:T(8,128)(2,1)S(1)}, u32[]{:S(2)}, u32[]{:S(2)}) collective-permute-start(bf16[32,1152]{1,0:T(8,128)(2,1)S(1)} %add_convert_fusion.own_ref), channel_id=1, source_target_pairs={{0,8},{8,0},{16,24},{24,16},{1,9},{9,1},{17,25},{25,17},{2,10},{10... | collective-permute-start | bytes 221192 | tf_op jit(solution)/shard_map/spread_pre/ppermute | solution.py:245
  114.9 2.0 %copy-start.7 = (bf16[32,1152]{1,0:T(8,128)(2,1)}, bf16[32,1152]{1,0:T(8,128)(2,1)S(1)}, u32[]{:S(2)}) copy-start(bf16[32,1152]{1,0:T(8,128)(2,1)S(1)} %collective-permute-done.7.pre3_ref) | copy-start | bytes 221188
  114.9 2.0 %copy-start.8 = (bf16[32,1152]{1,0:T(8,128)(2,1)}, bf16[32,1152]{1,0:T(8,128)(2,1)S(1)}, u32[]{:S(2)}) copy-start(bf16[32,1152]{1,0:T(8,128)(2,1)S(1)} %collective-permute-done.6.pre2_ref) | copy-start | bytes 221188
  116.9 0.6 copy-start.9
  123.1 11.5 %collective-permute-start.8 = (bf16[4,8,32,384]{3,2,1,0:T(8,128)(2,1)}, bf16[4,8,32,384]{3,2,1,0:T(8,128)(2,1)S(1)}, u32[]{:S(2)}, u32[]{:S(2)}) collective-permute-start(bf16[4,8,32,384]{3,2,1,0:T(8,128)(2,1)} %get-tuple-element.41), channel_id=1, source_target_pairs={{0,32},{32,0},{1,33},{33,1},{2,34},{34,2},{3,35},{35,3},{4,36},{36... | collective-permute-start | bytes 2359304 | tf_op jit(solution)/shard_map/sum_dx/ppermute | solution.py:241
  134.6 0.9 copy-start.2
  138.9 18.4 %all-to-all-start.2 = ((bf16[32,32,384]{2,1,0:T(8,128)(2,1)}), bf16[32,32,384]{2,1,0:T(8,128)(2,1)S(1)}, u32[]{:S(2)}, u32[]{:S(2)}) async-start(bf16[32,32,384]{2,1,0:T(8,128)(2,1)} %bitcast.44), calls=%async_computation.2 | async-start | bytes 1572864 | tf_op jit(solution)/shard_map/sum_dx/all_to_all | solution.py:237
  157.6 23.1 %all-to-all-start.3 = ((bf16[16,3,40,384]{3,2,1,0:T(8,128)(2,1)}), bf16[16,3,40,384]{3,2,1,0:T(8,128)(2,1)S(1)}, u32[]{:S(2)}, u32[]{:S(2)}) async-start(bf16[16,3,40,384]{3,2,1,0:T(8,128)(2,1)} %bitcast.43), calls=%async_computation.3 | async-start | bytes 2949120 | tf_op jit(solution)/shard_map/return_grads/all_to_all | solution.py:237
  161.8 22.9 %collective-permute-start.9 = (bf16[32,192]{1,0:T(8,128)(2,1)S(1)}, bf16[32,192]{1,0:T(8,128)(2,1)S(1)}, u32[]{:S(2)}, u32[]{:S(2)}) collective-permute-start(bf16[32,192]{1,0:T(8,128)(2,1)S(1)} %slice.27), channel_id=1, source_target_pairs={{0,64},{64,0},{1,65},{65,1},{2,66},{66,2},{3,67},{67,3},{4,68},{68... | collective-permute-start | bytes 36872 | tf_op jit(solution)/shard_map/ppermute | solution.py:241
  184.8 0.6 copy-start.10

commit v7 on v6

--- a/solution.py
+++ b/solution.py
@@ -34,7 +34,7 @@
 TRIO = 3 * FSH
 PACK = 2 * NE * TRIO
 PAIR = 2 * LANES
-VMEM = 56 * 1024 * 1024
+VMEM = 24 * 1024 * 1024
 BF16 = jnp.bfloat16
 F32 = jnp.float32
 
@@ -49,6 +49,13 @@
 
 def dot_dims(a, b, left, right):
     return lax.dot_general(a, b, (((left,), (right,)), ((), ())), preferred_element_type=F32)
+
+
+def fetch(sources, targets, sems):
+    copies = [pltpu.make_async_copy(a, b, sems.at[i]) for i, (a, b) in enumerate(zip(sources, targets))]
+    for copy in copies:
+        copy.start()
+    return copies
 
 
 def feature_of(column):
@@ -117,13 +124,17 @@
                 ds_ref[g, e, at, :] = dy[e * HSLOTS:(e + 1) * HSLOTS]
 
 
-def forward_kernel(me_ref, w_ref, xs_ref, ds_ref, keep_ref, give1_ref, give2_ref, give3_ref, wx_ref, wd_ref, pre_ref):
+def forward_kernel(me_ref, *refs):
+    (keep_ref, give1_ref, give2_ref, give3_ref, wx_ref, wd_ref, pre_ref, w_ref, xs_ref, ds_ref, sems) = refs[3:]
+    copies = fetch(refs[:3], (w_ref, xs_ref, ds_ref), sems)
+    copies[0].wait()
     low = jnp.zeros((STEP - Q, FSH), F32)
     side = jnp.zeros((STEP, LANES - FSH), F32)
     for g in range(NG):
+        every = w_ref[g].astype(F32)
         for e in range(NE):
             for i in range(3):
-                w = w_ref[g, e, i].astype(F32)
+                w = every[(3 * e + i) * Q:(3 * e + i + 1) * Q]
                 for s in range(4):
                     piece = jnp.concatenate([w[:, s * FSH:(s + 1) * FSH], low], axis=0)
                     piece = jnp.concatenate([piece, side], axis=1).astype(BF16)
@@ -131,6 +142,8 @@
                         wx_ref[g, s * STEP:(s + 1) * STEP, e * PAIR + i * LANES:e * PAIR + (i + 1) * LANES] = piece
                     else:
                         wd_ref[g, s * STEP:(s + 1) * STEP, e * LANES:(e + 1) * LANES] = piece
+    copies[1].wait()
+    copies[2].wait()
     for e in range(NE):
         ab = jnp.zeros((SLOTS, PAIR), F32)
         back = jnp.zeros((SLOTS, LANES), F32)
@@ -152,12 +165,17 @@
     return jnp.concatenate([dx[:, 0], dx[:, 1]], axis=2)
 
 
-def middle_kernel(me_ref, own_ref, pre1_ref, pre2_ref, pre3_ref, wx_ref, gate_ref, slot_ref,
-                  d_ref, spread_ref, tail_ref, give_ref, pre_ref, far_ref):
+def middle_kernel(me_ref, *refs):
+    (d_ref, spread_ref, tail_ref, give_ref, pre_ref, far_ref, *local_refs, sems) = refs[7:]
+    (gate_ref, slot_ref, wx_ref), parts = local_refs[4:], local_refs[:4]
+    copies = fetch(refs[:7], local_refs, sems)
     first = me_ref[0] * NE
-    for s, part_ref in enumerate((own_ref, pre1_ref, pre2_ref, pre3_ref)):
+    for s, part_ref in enumerate(parts):
         rows = pl.ds(pl.multiple_of(me_ref[1 + s] * PART, PART), PART)
+        copies[s].wait()
         pre_ref[rows, :] = part_ref[...].astype(F32)
+    copies[4].wait()
+    copies[5].wait()
     side = jnp.zeros((HSLOTS, LANES - FSH), F32)
     lane = iota((HSLOTS, LANES - FSH), 1)
     slots = iota((HALF, HSLOTS), 1).astype(F32)
@@ -188,11 +206,15 @@
         if h == 0:
             tail_ref[...] = tail
     tail = jnp.concatenate([tail, none], axis=1)
+    copies[6].wait()
     for g in range(NG):
         give_ref[:, g] = dx_of(far_ref[...], wx_ref[g], tail).astype(BF16)
 
 
-def input_kernel(got_ref, spread_ref, tail_ref, wx_ref, dx_ref):
+def input_kernel(*refs):
+    dx_ref, spread_ref, tail_ref, wx_ref, got_ref, sems = refs[4:]
+    for copy in fetch(refs[:4], (spread_ref, tail_ref, wx_ref, got_ref), sems):
+        copy.wait()
     none = jnp.zeros((HALF, WIDE - LANES), F32)
     tail = jnp.concatenate([tail_ref[...], none], axis=1)
     for g in range(NG):
@@ -210,7 +232,9 @@
                 out_ref[g, e, i] = jnp.concatenate(pieces, axis=1).astype(BF16)
 
 
-def finish_kernel(dx_ref, got_ref, in_ref, probs_ref):
+def finish_kernel(dx_any, got_any, in_ref, probs_ref, dx_ref, got_ref, sems):
+    for copy in fetch((dx_any, got_any), (dx_ref, got_ref), sems):
+        copy.wait()
     total = dx_ref[...] + got_ref[...].astype(F32)
     row, column = iota((WIDE, DSH), 0), iota((WIDE, DSH), 1)
     order = ones(feature_of(row) == column)
@@ -218,17 +242,22 @@
     probs_ref[...] = total[:, :LANES].T[IDS_AT:IDS_AT + TOP, :]
 
 
-def call(kernel, outs, args, scratch=(), scalar=False):
+def call(kernel, outs, args, scratch=(), scalar=False, by_hand=False):
     vmem = pl.BlockSpec(memory_space=pltpu.VMEM)
-    specs = [vmem] * len(args)
+    specs = [pl.BlockSpec(memory_space=pl.ANY) if by_hand else vmem] * len(args)
     if scalar:
         specs[0] = pl.BlockSpec(memory_space=pltpu.SMEM)
+    scratch_shapes = [pltpu.VMEM(shape, dtype) for shape, dtype in scratch]
+    if by_hand:
+        fetched = args[1:] if scalar else args
+        scratch_shapes += [pltpu.VMEM(v.shape, v.dtype) for v in fetched]
+        scratch_shapes.append(pltpu.SemaphoreType.DMA((len(fetched),)))
     return pl.pallas_call(
         kernel,
         out_shape=[jax.ShapeDtypeStruct(shape, dtype) for shape, dtype in outs],
         in_specs=specs,
         out_specs=[vmem] * len(outs),
-        scratch_shapes=[pltpu.VMEM(shape, dtype) for shape, dtype in scratch],
+        scratch_shapes=scratch_shapes,
         compiler_params=pltpu.CompilerParams(vmem_limit_bytes=VMEM),
     )(*args)
 
@@ -258,7 +287,7 @@
     with jax.named_scope("move_weights"):
         tiles = [w.reshape(EXPERTS, 1, Q, 4 * FSH) for w in (w_gate, w_up, w_down)]
         weights, x0 = lax.optimization_barrier((jnp.concatenate(tiles, axis=1), x0))
-        weights = exchange(weights, GROUP).reshape(NG, NE, 3, Q, 4 * FSH)
+        weights = exchange(weights, GROUP).reshape(NG, NE * 3 * Q, 4 * FSH)
     rows = ((NG, NE, SLOTS, WIDE), BF16)
     xs, ds, gate, slot = call(
         select_kernel,
@@ -272,7 +301,7 @@
         [((PART, PACK), F32), part, part, part, ((NG, WIDE, NE * PAIR), BF16)],
         (me, weights, xs, ds),
         [((NG, WIDE, NE * LANES), BF16), ((HSLOTS, PACK), F32)],
-        True)
+        True, True)
     with jax.named_scope("sum_pre"):
         got = [flip(give, "zq", 1 + i) for i, give in enumerate((give1, give2, give3))]
         pre = (keep + sum(v.astype(F32) for v in got)).astype(BF16)
@@ -282,11 +311,11 @@
     d, spread, tail, give = call(
         middle_kernel,
         [((NE, SLOTS, 3 * LANES), BF16), ((HALF, NE * PAIR), BF16), ((HALF, LANES), F32), (dx_shape, BF16)],
-        (me, *pre, wx, gate, slot),
+        (me, *pre, gate, slot, wx),
         [((HSLOTS, PACK), F32), ((HALF, NE * PAIR), BF16)],
-        True)
+        True, True)
     with jax.named_scope("sum_dx"):
-        (dx,) = call(input_kernel, [(dx_shape, BF16)], (swap(give, "core"), spread, tail, wx))
+        (dx,) = call(input_kernel, [(dx_shape, BF16)], (spread, tail, wx, swap(give, "core")), by_hand=True)
         dx, d = lax.optimization_barrier((dx, d))
         dx = exchange(dx.reshape(NX * NG, SHARD, COLS), ("x",) + GROUP)
         dx = jnp.sum(dx.astype(F32), axis=0)
@@ -298,7 +327,7 @@
         grads = exchange(grads.reshape(EXPERTS, 3, Q, 4 * FSH), GROUP)
         grads = [grads[:, i].reshape(w_gate.shape) for i in range(3)]
     keep, *grads = lax.optimization_barrier((keep, *grads))
-    grad_in, grad_probs = call(finish_kernel, [((SHARD, DSH), BF16), ((TOP, SHARD), F32)], (keep, got))
+    grad_in, grad_probs = call(finish_kernel, [((SHARD, DSH), BF16), ((TOP, SHARD), F32)], (keep, got), by_hand=True)
     return (grad_in, grad_probs.T, *grads)
 
 

time: 190 us -> 186 us (0.979)
  Pallas kernels: 29 us -> 17.3 us
  local copies, waits for them, and re-layouts: 9.67 us -> 15.9 us
    pallas_call x7, Pallas kernels: 29 us -> 17.3 us  [call(): pl.pallas_call(kernel, out_shape=[jax.ShapeDtypeStruct(shape, dtype) for...]
    unnamed x28 -> x34, local copies, waits for them, and re-layouts: 6.8 us -> 14.1 us
  transfers between devices with their start and end apart: 14 -> 14, of which waited for: 11 -> 11; matrix products, arithmetic and copies ran while one was open for 3% -> 2% of each run, Pallas kernels for 6% -> 3%
where the time goes in v7:
time: 186 us; the launch traced here: 183 us
  starting transfers between devices  89.9 us (48%)
  waiting for transfers between devices  56 us (30%)
  Pallas kernels  17.3 us (9%)
  local copies, waits for them, and re-layouts  15.9 us (9%)
  other arithmetic  2.64 us (1%)
    ppermute x4, starting transfers between devices, swap(): return lax.ppermute(value, axis, [(0, 1), (1, 0)])  40.2 us
    all_to_all x4, waiting for transfers between devices, exchange(): return lax.all_to_all(value, axis, split_axis=0, concat_axis=0, tiled=True)  37.4 us
    ppermute x6, starting transfers between devices, flip(): lax.ppermute(value, axis, [(i, i ^ bit) for i in range(lax.axis_size(axis...  27.5 us
    all_to_all x4, starting transfers between devices, exchange(): return lax.all_to_all(value, axis, split_axis=0, concat_axis=0, tiled=True)  22.2 us
    pallas_call x7, Pallas kernels, call(): pl.pallas_call(kernel, out_shape=[jax.ShapeDtypeStruct(shape, dtype) for...  17.3 us
    unnamed x34, local copies, waits for them, and re-layouts  14.1 us
    ppermute x6, waiting for transfers between devices, flip(): lax.ppermute(value, axis, [(i, i ^ bit) for i in range(lax.axis_size(axis...  11 us
    ppermute x4, waiting for transfers between devices, swap(): return lax.ppermute(value, axis, [(0, 1), (1, 0)])  7.6 us
  transfers between devices with their start and end apart: 14, of which 11 were waited for; matrix products, arithmetic and copies ran while one was open for 2% of the time, Pallas kernels for 3%

profile of v7, /device:TPU:1, one launch (start us, length us, event | category | flops | bytes accessed | tf_op | source)
XLA Modules:
  0.0 182.8 jit_solution(7849913453225218914)
XLA Ops:
  0.6 0.0 copy-start.6
  0.6 0.7 copy-done.6
  1.4 0.7 copy-done.7
  2.1 0.7 copy-done.8
  2.8 0.7 copy-done.9
  3.4 0.7 copy-done.10
  4.1 0.3 shard_map.119
  4.4 16.3 %collective-permute-start = (bf16[32,384]{1,0:T(8,128)(2,1)S(1)}, bf16[32,384]{1,0:T(8,128)(2,1)S(1)}, u32[]{:S(2)}, u32[]{:S(2)}) collective-permute-start(bf16[32,384]{1,0:T(8,128)(2,1)S(1)} %shard_map.119), channel_id=1, source_target_pairs={{0,64},{64,0},{1,65},{65,1},{2,66},{66,2},{3,67},{67,3},{4,68},{68... | collective-permute-start | bytes 73736 | tf_op jit(solution)/shard_map/gather_tokens/ppermute | solution.py:270
  20.7 1.3 collective-permute-done
  22.0 1.4 tile.2
  23.4 7.5 %all-to-all-start = ((bf16[32,64,384]{2,1,0:T(8,128)(2,1)}), bf16[32,64,384]{2,1,0:T(8,128)(2,1)S(1)}, u32[]{:S(2)}, u32[]{:S(2)}) async-start(bf16[32,64,384]{2,1,0:T(8,128)(2,1)} %tile.2), calls=%async_computation | async-start | bytes 3145728 | tf_op jit(solution)/shard_map/gather_tokens/all_to_all | solution.py:266
  31.0 0.0 copy-start.13
  31.0 0.0 copy-done.11
  31.0 0.1 copy.16
  31.1 0.0 copy-done.12
  31.1 0.1 copy.17
  31.2 0.9 copy-done.13
  32.0 0.1 copy.18
  32.1 1.3 pad_maximum_fusion
  33.4 17.4 %all-to-all-done = bf16[32,64,384]{2,1,0:T(8,128)(2,1)S(1)} async-done(((bf16[32,64,384]{2,1,0:T(8,128)(2,1)}), bf16[32,64,384]{2,1,0:T(8,128)(2,1)S(1)}, u32[]{:S(2)}, u32[]{:S(2)}) %all-to-all-start) | async-done | bytes 1572896 | tf_op jit(solution)/shard_map/gather_tokens/all_to_all | solution.py:266
  50.9 4.3 %all-to-all-start.1 = ((bf16[16,3,40,384]{3,2,1,0:T(8,128)(2,1)}), bf16[16,3,40,384]{3,2,1,0:T(8,128)(2,1)}, u32[]{:S(2)}, u32[]{:S(2)}) async-start(bf16[16,3,40,384]{3,2,1,0:T(8,128)(2,1)} %pad_maximum_fusion), calls=%async_computation.1 | async-start | bytes 2949120 | tf_op jit(solution)/shard_map/move_weights/all_to_all | solution.py:266
  55.2 0.0 copy-done.3
  55.2 5.0 %collective-permute-start.1 = (bf16[4,8,64,384]{3,2,1,0:T(8,128)(2,1)S(1)}, bf16[4,8,64,384]{3,2,1,0:T(8,128)(2,1)}, u32[]{:S(2)}, u32[]{:S(2)}) collective-permute-start(bf16[4,8,64,384]{3,2,1,0:T(8,128)(2,1)S(1)} %bitcast.40), channel_id=1, source_target_pairs={{0,32},{32,0},{1,33},{33,1},{2,34},{34,2},{3,35},{35,3},{4,36},{36... | collective-permute-start | bytes 4718600 | tf_op jit(solution)/shard_map/gather_tokens/ppermute | solution.py:270
  60.2 0.1 stack.23.me_ref
  60.3 3.1 %collective-permute-done.1.x1_ref = bf16[4,8,64,384]{3,2,1,0:T(8,128)(2,1)} collective-permute-done((bf16[4,8,64,384]{3,2,1,0:T(8,128)(2,1)S(1)}, bf16[4,8,64,384]{3,2,1,0:T(8,128)(2,1)}, u32[]{:S(2)}, u32[]{:S(2)}) %collective-permute-start.1) | collective-permute-done | bytes 1572896 | tf_op jit(solution)/shard_map/gather_tokens/ppermute | solution.py:270
  63.3 1.4 copy-done.4
  64.7 3.6 %shard_map.120 = (bf16[8,2,256,192]{3,2,1,0:T(8,128)(2,1)S(1)}, bf16[8,2,256,192]{3,2,1,0:T(8,128)(2,1)S(1)}, f32[2,256,128]{2,1,0:T(8,128)S(1)}, f32[512,128]{1,0:T(8,128)S(1)}) custom-call(s32[5]{0:T(128)S(1)} %stack.23.me_ref, bf16[4,8,64,384]{3,2,1,0:T(8,128)(2,1)S(1)} %bitcast.41, bf16[4,8,64,384]{3,2,1,0:T(8,128)(2,1)} %collective-permute-done.1.x1_ref), custom_call_target="tpu_custom_call" | custom-call | tf_op jit(solution)/shard_map/pallas_call | solution.py:255
  68.3 1.3 copy-done
  69.7 2.0 %all-to-all-done.1 = bf16[16,3,40,384]{3,2,1,0:T(8,128)(2,1)} async-done(((bf16[16,3,40,384]{3,2,1,0:T(8,128)(2,1)}), bf16[16,3,40,384]{3,2,1,0:T(8,128)(2,1)}, u32[]{:S(2)}, u32[]{:S(2)}) %all-to-all-start.1) | async-done | bytes 1474592 | tf_op jit(solution)/shard_map/move_weights/all_to_all | solution.py:266
  71.7 1.6 copy-done.1
  73.2 4.1 %shard_map.121 = (f32[32,1152]{1,0:T(8,128)S(1)}, bf16[32,1152]{1,0:T(8,128)(2,1)S(1)}, bf16[32,1152]{1,0:T(8,128)(2,1)S(1)}, bf16[32,1152]{1,0:T(8,128)(2,1)S(1)}, bf16[8,192,512]{2,1,0:T(8,128)(2,1)S(1)}) custom-call(s32[5]{0:T(128)S(1)} %stack.23.me_ref, bf16[8,240,384]{2,1,0:T(8,128)(2,1)} %bitcast.12.refs_0_, ...), custom_call_target="tpu_custom_call" | custom-call | tf_op jit(solution)/shard_map/pallas_call | solution.py:255
  77.4 4.6 %collective-permute-start.2 = (bf16[32,1152]{1,0:T(8,128)(2,1)S(1)}, bf16[32,1152]{1,0:T(8,128)(2,1)S(1)}, u32[]{:S(2)}, u32[]{:S(2)}) collective-permute-start(bf16[32,1152]{1,0:T(8,128)(2,1)S(1)} %get-tuple-element.35), channel_id=1, source_target_pairs={{0,8},{8,0},{16,24},{24,16},{1,9},{9,1},{17,25},{25,17},{2,10},{10... | collective-permute-start | bytes 221192 | tf_op jit(solution)/shard_map/sum_pre/ppermute | solution.py:274
  82.0 7.8 %collective-permute-start.3 = (bf16[32,1152]{1,0:T(8,128)(2,1)S(1)}, bf16[32,1152]{1,0:T(8,128)(2,1)S(1)}, u32[]{:S(2)}, u32[]{:S(2)}) collective-permute-start(bf16[32,1152]{1,0:T(8,128)(2,1)S(1)} %get-tuple-element.36), channel_id=1, source_target_pairs={{0,16},{8,24},{16,0},{24,8},{1,17},{9,25},{17,1},{25,9},{2,18},{10... | collective-permute-start | bytes 221192 | tf_op jit(solution)/shard_map/sum_pre/ppermute | solution.py:274
  89.8 1.9 %collective-permute-start.4 = (bf16[32,1152]{1,0:T(8,128)(2,1)S(1)}, bf16[32,1152]{1,0:T(8,128)(2,1)S(1)}, u32[]{:S(2)}, u32[]{:S(2)}) collective-permute-start(bf16[32,1152]{1,0:T(8,128)(2,1)S(1)} %get-tuple-element.37), channel_id=1, source_target_pairs={{0,24},{8,16},{16,8},{24,0},{1,25},{9,17},{17,9},{25,1},{2,26},{10... | collective-permute-start | bytes 221192 | tf_op jit(solution)/shard_map/sum_pre/ppermute | solution.py:274
  91.7 0.0 collective-permute-done.2
  91.7 0.3 collective-permute-done.3
  92.0 8.7 %collective-permute-done.4 = bf16[32,1152]{1,0:T(8,128)(2,1)S(1)} collective-permute-done((bf16[32,1152]{1,0:T(8,128)(2,1)S(1)}, bf16[32,1152]{1,0:T(8,128)(2,1)S(1)}, u32[]{:S(2)}, u32[]{:S(2)}) %collective-permute-start.4) | collective-permute-done | bytes 73760 | tf_op jit(solution)/shard_map/sum_pre/ppermute | solution.py:274
  100.8 2.0 %collective-permute-start.7 = (bf16[32,1152]{1,0:T(8,128)(2,1)S(1)}, bf16[32,1152]{1,0:T(8,128)(2,1)S(1)}, u32[]{:S(2)}, u32[]{:S(2)}) collective-permute-start(bf16[32,1152]{1,0:T(8,128)(2,1)S(1)} %add_convert_fusion.refs_0_), channel_id=1, source_target_pairs={{0,24},{8,16},{16,8},{24,0},{1,25},{9,17},{17,9},{25,1},{2,26},{10... | collective-permute-start | bytes 221192 | tf_op jit(solution)/shard_map/spread_pre/ppermute | solution.py:274
  102.8 3.8 %collective-permute-start.6 = (bf16[32,1152]{1,0:T(8,128)(2,1)S(1)}, bf16[32,1152]{1,0:T(8,128)(2,1)S(1)}, u32[]{:S(2)}, u32[]{:S(2)}) collective-permute-start(bf16[32,1152]{1,0:T(8,128)(2,1)S(1)} %add_convert_fusion.refs_0_), channel_id=1, source_target_pairs={{0,16},{8,24},{16,0},{24,8},{1,17},{9,25},{17,1},{25,9},{2,18},{10... | collective-permute-start | bytes 221192 | tf_op jit(solution)/shard_map/spread_pre/ppermute | solution.py:274
  106.5 7.4 %collective-permute-start.5 = (bf16[32,1152]{1,0:T(8,128)(2,1)S(1)}, bf16[32,1152]{1,0:T(8,128)(2,1)S(1)}, u32[]{:S(2)}, u32[]{:S(2)}) collective-permute-start(bf16[32,1152]{1,0:T(8,128)(2,1)S(1)} %add_convert_fusion.refs_0_), channel_id=1, source_target_pairs={{0,8},{8,0},{16,24},{24,16},{1,9},{9,1},{17,25},{25,17},{2,10},{10... | collective-permute-start | bytes 221192 | tf_op jit(solution)/shard_map/spread_pre/ppermute | solution.py:274
  114.0 0.0 collective-permute-done.7.refs_3_
  114.0 0.0 collective-permute-done.6.refs_2_
  114.0 2.0 %collective-permute-done.5.refs_1_ = bf16[32,1152]{1,0:T(8,128)(2,1)S(1)} collective-permute-done((bf16[32,1152]{1,0:T(8,128)(2,1)S(1)}, bf16[32,1152]{1,0:T(8,128)(2,1)S(1)}, u32[]{:S(2)}, u32[]{:S(2)}) %collective-permute-start.5) | collective-permute-done | bytes 73760 | tf_op jit(solution)/shard_map/spread_pre/ppermute | solution.py:274
  116.0 4.6 %shard_map.122 = (bf16[2,256,384]{2,1,0:T(8,128)(2,1)S(1)}, bf16[256,512]{1,0:T(8,128)(2,1)S(1)}, f32[256,128]{1,0:T(8,128)S(1)}, bf16[4,8,32,384]{3,2,1,0:T(8,128)(2,1)S(1)}) custom-call(s32[5]{0:T(128)S(1)} %stack.23.me_ref, bf16[32,1152]{1,0:T(8,128)(2,1)S(1)} %add_convert_fusion.refs_0_, bf16[32,1152]{1,0:T(8,128)(2,1)S(1)} %collective-permute-done.5.refs_1_, ...), custom_call_target="tpu_custom_call" | custom-call | tf_op jit(solution)/shard_map/pallas_call | solution.py:255
  120.6 9.2 %collective-permute-start.8 = (bf16[4,8,32,384]{3,2,1,0:T(8,128)(2,1)S(1)}, bf16[4,8,32,384]{3,2,1,0:T(8,128)(2,1)S(1)}, u32[]{:S(2)}, u32[]{:S(2)}) collective-permute-start(bf16[4,8,32,384]{3,2,1,0:T(8,128)(2,1)S(1)} %get-tuple-element.43), channel_id=1, source_target_pairs={{0,32},{32,0},{1,33},{33,1},{2,34},{34,2},{3,35},{35,3},{4,36},{36... | collective-permute-start | bytes 2359304 | tf_op jit(solution)/shard_map/sum_dx/ppermute | solution.py:270
  129.8 1.9 %collective-permute-done.8.refs_3_ = bf16[4,8,32,384]{3,2,1,0:T(8,128)(2,1)S(1)} collective-permute-done((bf16[4,8,32,384]{3,2,1,0:T(8,128)(2,1)S(1)}, bf16[4,8,32,384]{3,2,1,0:T(8,128)(2,1)S(1)}, u32[]{:S(2)}, u32[]{:S(2)}) %collective-permute-start.8) | collective-permute-done | bytes 786464 | tf_op jit(solution)/shard_map/sum_dx/ppermute | solution.py:270
  131.7 2.1 %sum_dx.1 = bf16[4,8,32,384]{3,2,1,0:T(8,128)(2,1)} custom-call(bf16[256,512]{1,0:T(8,128)(2,1)S(1)} %get-tuple-element.41.refs_0_, f32[256,128]{1,0:T(8,128)S(1)} %get-tuple-element.42.refs_1_, bf16[8,192,512]{2,1,0:T(8,128)(2,1)S(1)} %get-tuple-element.40.refs_6_.refs_2_, bf16[4,8,32,384]{3,2,1,0:T(8,128)(2,1)S(1)} %collective-permute-done.8.refs_3_), custom_call_target="tpu_custom_call" | custom-call | tf_op jit(solution)/shard_map/sum_dx/pallas_call | solution.py:255
  133.8 6.7 %all-to-all-start.2 = ((bf16[32,32,384]{2,1,0:T(8,128)(2,1)}), bf16[32,32,384]{2,1,0:T(8,128)(2,1)}, u32[]{:S(2)}, u32[]{:S(2)}) async-start(bf16[32,32,384]{2,1,0:T(8,128)(2,1)} %bitcast.13), calls=%async_computation.2 | async-start | bytes 1572864 | tf_op jit(solution)/shard_map/sum_dx/all_to_all | solution.py:266
  140.5 0.0 copy-start.2
  140.5 1.6 copy-done.2
  142.1 1.8 shard_map.123
  143.9 1.1 copy-done.5
  145.0 8.3 %all-to-all-done.2 = bf16[32,32,384]{2,1,0:T(8,128)(2,1)} async-done(((bf16[32,32,384]{2,1,0:T(8,128)(2,1)}), bf16[32,32,384]{2,1,0:T(8,128)(2,1)}, u32[]{:S(2)}, u32[]{:S(2)}) %all-to-all-start.2) | async-done | bytes 786464 | tf_op jit(solution)/shard_map/sum_dx/all_to_all | solution.py:266
  153.3 1.3 convert_reduce_fusion
  154.6 0.1 slice.27
  154.6 3.7 %all-to-all-start.3 = ((bf16[16,3,40,384]{3,2,1,0:T(8,128)(2,1)}), bf16[16,3,40,384]{3,2,1,0:T(8,128)(2,1)S(1)}, u32[]{:S(2)}, u32[]{:S(2)}) async-start(bf16[16,3,40,384]{3,2,1,0:T(8,128)(2,1)} %bitcast.42), calls=%async_computation.3 | async-start | bytes 2949120 | tf_op jit(solution)/shard_map/return_grads/all_to_all | solution.py:266
  158.3 9.7 %collective-permute-start.9 = (bf16[32,192]{1,0:T(8,128)(2,1)S(1)}, bf16[32,192]{1,0:T(8,128)(2,1)S(1)}, u32[]{:S(2)}, u32[]{:S(2)}) collective-permute-start(bf16[32,192]{1,0:T(8,128)(2,1)S(1)} %slice.27), channel_id=1, source_target_pairs={{0,64},{64,0},{1,65},{65,1},{2,66},{66,2},{3,67},{67,3},{4,68},{68... | collective-permute-start | bytes 36872 | tf_op jit(solution)/shard_map/ppermute | solution.py:270
  168.1 9.7 %all-to-all-done.3 = bf16[16,3,40,384]{3,2,1,0:T(8,128)(2,1)S(1)} async-done(((bf16[16,3,40,384]{3,2,1,0:T(8,128)(2,1)}), bf16[16,3,40,384]{3,2,1,0:T(8,128)(2,1)S(1)}, u32[]{:S(2)}, u32[]{:S(2)}) %all-to-all-start.3) | async-done | bytes 1474592 | tf_op jit(solution)/shard_map/return_grads/all_to_all | solution.py:266
  177.8 0.1 fusion
  177.9 0.8 copy.21
  178.8 0.8 copy.20
  179.6 0.8 copy.19
  180.4 1.4 collective-permute-done.9.got_any
  181.8 0.8 shard_map.124
  (14 shorter events, 0.1 us)
Async XLA Ops:
  0.6 0.7 copy-start.6
  1.4 0.7 copy-start.7
  2.1 0.7 copy-start.8
  2.8 0.7 copy-start.9
  3.4 0.7 copy-start.10
  4.4 17.6 %collective-permute-start = (bf16[32,384]{1,0:T(8,128)(2,1)S(1)}, bf16[32,384]{1,0:T(8,128)(2,1)S(1)}, u32[]{:S(2)}, u32[]{:S(2)}) collective-permute-start(bf16[32,384]{1,0:T(8,128)(2,1)S(1)} %shard_map.119), channel_id=1, source_target_pairs={{0,64},{64,0},{1,65},{65,1},{2,66},{66,2},{3,67},{67,3},{4,68},{68... | collective-permute-start | bytes 73736 | tf_op jit(solution)/shard_map/gather_tokens/ppermute | solution.py:270
  23.4 7.6 %copy-start.11 = (bf16[16,15360]{1,0:T(8,128)(2,1)S(1)}, bf16[16,15360]{1,0:T(8,128)(2,1)}, u32[]{:S(2)}) copy-start(bf16[16,15360]{1,0:T(8,128)(2,1)} %param.13) | copy-start | bytes 1474564
  23.4 7.6 %copy-start.12 = (bf16[16,15360]{1,0:T(8,128)(2,1)S(1)}, bf16[16,15360]{1,0:T(8,128)(2,1)}, u32[]{:S(2)}) copy-start(bf16[16,15360]{1,0:T(8,128)(2,1)} %param.14) | copy-start | bytes 1474564
  23.4 27.4 %all-to-all-start = ((bf16[32,64,384]{2,1,0:T(8,128)(2,1)}), bf16[32,64,384]{2,1,0:T(8,128)(2,1)S(1)}, u32[]{:S(2)}, u32[]{:S(2)}) async-start(bf16[32,64,384]{2,1,0:T(8,128)(2,1)} %tile.2), calls=%async_computation | async-start | bytes 3145728 | tf_op jit(solution)/shard_map/gather_tokens/all_to_all | solution.py:266
  31.0 1.0 copy-start.13
  50.9 4.3 %copy-start.3 = (bf16[32,64,384]{2,1,0:T(8,128)(2,1)}, bf16[32,64,384]{2,1,0:T(8,128)(2,1)S(1)}, u32[]{:S(2)}) copy-start(bf16[32,64,384]{2,1,0:T(8,128)(2,1)S(1)} %all-to-all-done) | copy-start | bytes 4718596
  50.9 20.8 %all-to-all-start.1 = ((bf16[16,3,40,384]{3,2,1,0:T(8,128)(2,1)}), bf16[16,3,40,384]{3,2,1,0:T(8,128)(2,1)}, u32[]{:S(2)}, u32[]{:S(2)}) async-start(bf16[16,3,40,384]{3,2,1,0:T(8,128)(2,1)} %pad_maximum_fusion), calls=%async_computation.1 | async-start | bytes 2949120 | tf_op jit(solution)/shard_map/move_weights/all_to_all | solution.py:266
  55.2 8.1 %collective-permute-start.1 = (bf16[4,8,64,384]{3,2,1,0:T(8,128)(2,1)S(1)}, bf16[4,8,64,384]{3,2,1,0:T(8,128)(2,1)}, u32[]{:S(2)}, u32[]{:S(2)}) collective-permute-start(bf16[4,8,64,384]{3,2,1,0:T(8,128)(2,1)S(1)} %bitcast.40), channel_id=1, source_target_pairs={{0,32},{32,0},{1,33},{33,1},{2,34},{34,2},{3,35},{35,3},{4,36},{36... | collective-permute-start | bytes 4718600 | tf_op jit(solution)/shard_map/gather_tokens/ppermute | solution.py:270
  63.3 1.4 copy-start.4
  68.3 1.4 copy-start
  71.7 1.6 copy-start.1
  77.4 14.3 %collective-permute-start.2 = (bf16[32,1152]{1,0:T(8,128)(2,1)S(1)}, bf16[32,1152]{1,0:T(8,128)(2,1)S(1)}, u32[]{:S(2)}, u32[]{:S(2)}) collective-permute-start(bf16[32,1152]{1,0:T(8,128)(2,1)S(1)} %get-tuple-element.35), channel_id=1, source_target_pairs={{0,8},{8,0},{16,24},{24,16},{1,9},{9,1},{17,25},{25,17},{2,10},{10... | collective-permute-start | bytes 221192 | tf_op jit(solution)/shard_map/sum_pre/ppermute | solution.py:274
  82.0 10.0 %collective-permute-start.3 = (bf16[32,1152]{1,0:T(8,128)(2,1)S(1)}, bf16[32,1152]{1,0:T(8,128)(2,1)S(1)}, u32[]{:S(2)}, u32[]{:S(2)}) collective-permute-start(bf16[32,1152]{1,0:T(8,128)(2,1)S(1)} %get-tuple-element.36), channel_id=1, source_target_pairs={{0,16},{8,24},{16,0},{24,8},{1,17},{9,25},{17,1},{25,9},{2,18},{10... | collective-permute-start | bytes 221192 | tf_op jit(solution)/shard_map/sum_pre/ppermute | solution.py:274
  89.8 10.9 %collective-permute-start.4 = (bf16[32,1152]{1,0:T(8,128)(2,1)S(1)}, bf16[32,1152]{1,0:T(8,128)(2,1)S(1)}, u32[]{:S(2)}, u32[]{:S(2)}) collective-permute-start(bf16[32,1152]{1,0:T(8,128)(2,1)S(1)} %get-tuple-element.37), channel_id=1, source_target_pairs={{0,24},{8,16},{16,8},{24,0},{1,25},{9,17},{17,9},{25,1},{2,26},{10... | collective-permute-start | bytes 221192 | tf_op jit(solution)/shard_map/sum_pre/ppermute | solution.py:274
  100.8 13.2 %collective-permute-start.7 = (bf16[32,1152]{1,0:T(8,128)(2,1)S(1)}, bf16[32,1152]{1,0:T(8,128)(2,1)S(1)}, u32[]{:S(2)}, u32[]{:S(2)}) collective-permute-start(bf16[32,1152]{1,0:T(8,128)(2,1)S(1)} %add_convert_fusion.refs_0_), channel_id=1, source_target_pairs={{0,24},{8,16},{16,8},{24,0},{1,25},{9,17},{17,9},{25,1},{2,26},{10... | collective-permute-start | bytes 221192 | tf_op jit(solution)/shard_map/spread_pre/ppermute | solution.py:274
  102.8 11.2 %collective-permute-start.6 = (bf16[32,1152]{1,0:T(8,128)(2,1)S(1)}, bf16[32,1152]{1,0:T(8,128)(2,1)S(1)}, u32[]{:S(2)}, u32[]{:S(2)}) collective-permute-start(bf16[32,1152]{1,0:T(8,128)(2,1)S(1)} %add_convert_fusion.refs_0_), channel_id=1, source_target_pairs={{0,16},{8,24},{16,0},{24,8},{1,17},{9,25},{17,1},{25,9},{2,18},{10... | collective-permute-start | bytes 221192 | tf_op jit(solution)/shard_map/spread_pre/ppermute | solution.py:274
  106.5 9.4 %collective-permute-start.5 = (bf16[32,1152]{1,0:T(8,128)(2,1)S(1)}, bf16[32,1152]{1,0:T(8,128)(2,1)S(1)}, u32[]{:S(2)}, u32[]{:S(2)}) collective-permute-start(bf16[32,1152]{1,0:T(8,128)(2,1)S(1)} %add_convert_fusion.refs_0_), channel_id=1, source_target_pairs={{0,8},{8,0},{16,24},{24,16},{1,9},{9,1},{17,25},{25,17},{2,10},{10... | collective-permute-start | bytes 221192 | tf_op jit(solution)/shard_map/spread_pre/ppermute | solution.py:274
  120.6 11.1 %collective-permute-start.8 = (bf16[4,8,32,384]{3,2,1,0:T(8,128)(2,1)S(1)}, bf16[4,8,32,384]{3,2,1,0:T(8,128)(2,1)S(1)}, u32[]{:S(2)}, u32[]{:S(2)}) collective-permute-start(bf16[4,8,32,384]{3,2,1,0:T(8,128)(2,1)S(1)} %get-tuple-element.43), channel_id=1, source_target_pairs={{0,32},{32,0},{1,33},{33,1},{2,34},{34,2},{3,35},{35,3},{4,36},{36... | collective-permute-start | bytes 2359304 | tf_op jit(solution)/shard_map/sum_dx/ppermute | solution.py:270
  133.8 19.5 %all-to-all-start.2 = ((bf16[32,32,384]{2,1,0:T(8,128)(2,1)}), bf16[32,32,384]{2,1,0:T(8,128)(2,1)}, u32[]{:S(2)}, u32[]{:S(2)}) async-start(bf16[32,32,384]{2,1,0:T(8,128)(2,1)} %bitcast.13), calls=%async_computation.2 | async-start | bytes 1572864 | tf_op jit(solution)/shard_map/sum_dx/all_to_all | solution.py:266
  140.5 1.6 copy-start.2
  143.9 1.1 copy-start.5
  154.6 23.1 %all-to-all-start.3 = ((bf16[16,3,40,384]{3,2,1,0:T(8,128)(2,1)}), bf16[16,3,40,384]{3,2,1,0:T(8,128)(2,1)S(1)}, u32[]{:S(2)}, u32[]{:S(2)}) async-start(bf16[16,3,40,384]{3,2,1,0:T(8,128)(2,1)} %bitcast.42), calls=%async_computation.3 | async-start | bytes 2949120 | tf_op jit(solution)/shard_map/return_grads/all_to_all | solution.py:266
  158.3 23.5 %collective-permute-start.9 = (bf16[32,192]{1,0:T(8,128)(2,1)S(1)}, bf16[32,192]{1,0:T(8,128)(2,1)S(1)}, u32[]{:S(2)}, u32[]{:S(2)}) collective-permute-start(bf16[32,192]{1,0:T(8,128)(2,1)S(1)} %slice.27), channel_id=1, source_target_pairs={{0,64},{64,0},{1,65},{65,1},{2,66},{66,2},{3,67},{67,3},{4,68},{68... | collective-permute-start | bytes 36872 | tf_op jit(solution)/shard_map/ppermute | solution.py:270

commit v8 on v7

--- a/solution.py
+++ b/solution.py
@@ -35,6 +35,7 @@
 PACK = 2 * NE * TRIO
 PAIR = 2 * LANES
 VMEM = 24 * 1024 * 1024
+MOST = 56 * 1024 * 1024
 BF16 = jnp.bfloat16
 F32 = jnp.float32
 
@@ -242,7 +243,7 @@
     probs_ref[...] = total[:, :LANES].T[IDS_AT:IDS_AT + TOP, :]
 
 
-def call(kernel, outs, args, scratch=(), scalar=False, by_hand=False):
+def call(kernel, outs, args, scratch=(), scalar=False, by_hand=False, grant=VMEM):
     vmem = pl.BlockSpec(memory_space=pltpu.VMEM)
     specs = [pl.BlockSpec(memory_space=pl.ANY) if by_hand else vmem] * len(args)
     if scalar:
@@ -258,7 +259,7 @@
         in_specs=specs,
         out_specs=[vmem] * len(outs),
         scratch_shapes=scratch_shapes,
-        compiler_params=pltpu.CompilerParams(vmem_limit_bytes=VMEM),
+        compiler_params=pltpu.CompilerParams(vmem_limit_bytes=grant),
     )(*args)
 
 
@@ -279,7 +280,8 @@
     zq = lax.axis_index("zq").astype(jnp.int32)
     me = jnp.stack([group] + [zq ^ s for s in range(4)])
     small = [v.T for v in (scale_exp, route_ids, route_probs)]
-    (xin,) = call(prepare_kernel, [((SHARD, COLS), BF16)], (stash, small[0], grad_out, small[1], small[2]))
+    (xin,) = call(prepare_kernel, [((SHARD, COLS), BF16)], (stash, small[0], grad_out, small[1], small[2]),
+                  grant=MOST)
     with jax.named_scope("gather_tokens"):
         xin = jnp.concatenate([xin, swap(xin, "zh")])
         x0 = exchange(jnp.tile(xin, (NX * NG, 1)), ("x",) + GROUP).reshape(NX, NG, 2 * SHARD, COLS)

time: 186 us -> 184 us (0.989)
  local copies, waits for them, and re-layouts: 15.9 us -> 12.4 us
    unnamed x34 -> x24, local copies, waits for them, and re-layouts: 14.1 us -> 10.6 us
where the time goes in v8:
time: 184 us; the launch traced here: 181 us
  starting transfers between devices  89.6 us (49%)
  waiting for transfers between devices  56.5 us (31%)
  Pallas kernels  18.7 us (10%)
  local copies, waits for them, and re-layouts  12.4 us (7%)
  other arithmetic  3.37 us (2%)
    ppermute x4, starting transfers between devices, swap(): return lax.ppermute(value, axis, [(0, 1), (1, 0)])  40.2 us
    all_to_all x4, waiting for transfers between devices, exchange(): return lax.all_to_all(value, axis, split_axis=0, concat_axis=0, tiled=True)  37.7 us
    ppermute x6, starting transfers between devices, flip(): lax.ppermute(value, axis, [(i, i ^ bit) for i in range(lax.axis_size(axis...  27.3 us
    all_to_all x4, starting transfers between devices, exchange(): return lax.all_to_all(value, axis, split_axis=0, concat_axis=0, tiled=True)  22.1 us
    pallas_call x7, Pallas kernels, call(): pl.pallas_call(kernel, out_shape=[jax.ShapeDtypeStruct(shape, dtype) for...  18.7 us
    ppermute x6, waiting for transfers between devices, flip(): lax.ppermute(value, axis, [(i, i ^ bit) for i in range(lax.axis_size(axis...  11 us
    unnamed x24, local copies, waits for them, and re-layouts  10.6 us
    ppermute x4, waiting for transfers between devices, swap(): return lax.ppermute(value, axis, [(0, 1), (1, 0)])  7.85 us
  transfers between devices with their start and end apart: 14, of which 11 were waited for; matrix products, arithmetic and copies ran while one was open for 2% of the time, Pallas kernels for 3%

profile of v8, /device:TPU:1, one launch (start us, length us, event | category | flops | bytes accessed | tf_op | source)
XLA Modules:
  0.0 181.5 jit_solution(13989548684364223795)
XLA Ops:
  0.6 1.7 shard_map.119
  2.3 16.3 %collective-permute-start = (bf16[32,384]{1,0:T(8,128)(2,1)}, bf16[32,384]{1,0:T(8,128)(2,1)S(1)}, u32[]{:S(2)}, u32[]{:S(2)}) collective-permute-start(bf16[32,384]{1,0:T(8,128)(2,1)} %shard_map.119), channel_id=1, source_target_pairs={{0,64},{64,0},{1,65},{65,1},{2,66},{66,2},{3,67},{67,3},{4,68},{68... | collective-permute-start | bytes 73736 | tf_op jit(solution)/shard_map/gather_tokens/ppermute | solution.py:271
  18.6 1.5 collective-permute-done
  20.1 0.7 pad_maximum_fusion.1
  20.8 1.4 tile.2
  22.3 0.0 copy-start.6
  22.3 0.0 copy-start.7
  22.3 7.5 %all-to-all-start = ((bf16[32,64,384]{2,1,0:T(8,128)(2,1)}), bf16[32,64,384]{2,1,0:T(8,128)(2,1)S(1)}, u32[]{:S(2)}, u32[]{:S(2)}) async-start(bf16[32,64,384]{2,1,0:T(8,128)(2,1)} %tile.2), calls=%async_computation | async-start | bytes 3145728 | tf_op jit(solution)/shard_map/gather_tokens/all_to_all | solution.py:267
  29.8 0.0 copy-start.8
  29.8 0.0 copy-done.6
  29.8 0.1 copy.16
  29.9 0.0 copy-done.7
  29.9 0.1 copy.17
  30.0 0.9 copy-done.8
  30.8 0.1 copy.18
  30.9 1.3 pad_maximum_fusion
  32.2 17.5 %all-to-all-done = bf16[32,64,384]{2,1,0:T(8,128)(2,1)S(1)} async-done(((bf16[32,64,384]{2,1,0:T(8,128)(2,1)}), bf16[32,64,384]{2,1,0:T(8,128)(2,1)S(1)}, u32[]{:S(2)}, u32[]{:S(2)}) %all-to-all-start) | async-done | bytes 1572896 | tf_op jit(solution)/shard_map/gather_tokens/all_to_all | solution.py:267
  49.7 0.0 copy-start.3
  49.7 4.3 %all-to-all-start.1 = ((bf16[16,3,40,384]{3,2,1,0:T(8,128)(2,1)}), bf16[16,3,40,384]{3,2,1,0:T(8,128)(2,1)}, u32[]{:S(2)}, u32[]{:S(2)}) async-start(bf16[16,3,40,384]{3,2,1,0:T(8,128)(2,1)} %pad_maximum_fusion), calls=%async_computation.1 | async-start | bytes 2949120 | tf_op jit(solution)/shard_map/move_weights/all_to_all | solution.py:267
  54.0 0.0 copy-done.3
  54.0 4.9 %collective-permute-start.1 = (bf16[4,8,64,384]{3,2,1,0:T(8,128)(2,1)S(1)}, bf16[4,8,64,384]{3,2,1,0:T(8,128)(2,1)}, u32[]{:S(2)}, u32[]{:S(2)}) collective-permute-start(bf16[4,8,64,384]{3,2,1,0:T(8,128)(2,1)S(1)} %bitcast.40), channel_id=1, source_target_pairs={{0,32},{32,0},{1,33},{33,1},{2,34},{34,2},{3,35},{35,3},{4,36},{36... | collective-permute-start | bytes 4718600 | tf_op jit(solution)/shard_map/gather_tokens/ppermute | solution.py:271
  59.0 0.1 stack.23.me_ref
  59.1 3.1 %collective-permute-done.1.x1_ref = bf16[4,8,64,384]{3,2,1,0:T(8,128)(2,1)} collective-permute-done((bf16[4,8,64,384]{3,2,1,0:T(8,128)(2,1)S(1)}, bf16[4,8,64,384]{3,2,1,0:T(8,128)(2,1)}, u32[]{:S(2)}, u32[]{:S(2)}) %collective-permute-start.1) | collective-permute-done | bytes 1572896 | tf_op jit(solution)/shard_map/gather_tokens/ppermute | solution.py:271
  62.1 1.4 copy-done.4
  63.5 3.6 %shard_map.120 = (bf16[8,2,256,192]{3,2,1,0:T(8,128)(2,1)S(1)}, bf16[8,2,256,192]{3,2,1,0:T(8,128)(2,1)S(1)}, f32[2,256,128]{2,1,0:T(8,128)S(1)}, f32[512,128]{1,0:T(8,128)S(1)}) custom-call(s32[5]{0:T(128)S(1)} %stack.23.me_ref, bf16[4,8,64,384]{3,2,1,0:T(8,128)(2,1)S(1)} %bitcast.41, bf16[4,8,64,384]{3,2,1,0:T(8,128)(2,1)} %collective-permute-done.1.x1_ref), custom_call_target="tpu_custom_call" | custom-call | tf_op jit(solution)/shard_map/pallas_call | solution.py:256
  67.1 0.0 copy-start
  67.1 1.3 copy-done
  68.5 2.1 %all-to-all-done.1 = bf16[16,3,40,384]{3,2,1,0:T(8,128)(2,1)} async-done(((bf16[16,3,40,384]{3,2,1,0:T(8,128)(2,1)}), bf16[16,3,40,384]{3,2,1,0:T(8,128)(2,1)}, u32[]{:S(2)}, u32[]{:S(2)}) %all-to-all-start.1) | async-done | bytes 1474592 | tf_op jit(solution)/shard_map/move_weights/all_to_all | solution.py:267
  70.6 1.6 copy-done.1
  72.1 4.1 %shard_map.121 = (f32[32,1152]{1,0:T(8,128)S(1)}, bf16[32,1152]{1,0:T(8,128)(2,1)S(1)}, bf16[32,1152]{1,0:T(8,128)(2,1)S(1)}, bf16[32,1152]{1,0:T(8,128)(2,1)S(1)}, bf16[8,192,512]{2,1,0:T(8,128)(2,1)S(1)}) custom-call(s32[5]{0:T(128)S(1)} %stack.23.me_ref, bf16[8,240,384]{2,1,0:T(8,128)(2,1)} %bitcast.12.refs_0_, ...), custom_call_target="tpu_custom_call" | custom-call | tf_op jit(solution)/shard_map/pallas_call | solution.py:256
  76.3 4.5 %collective-permute-start.2 = (bf16[32,1152]{1,0:T(8,128)(2,1)S(1)}, bf16[32,1152]{1,0:T(8,128)(2,1)S(1)}, u32[]{:S(2)}, u32[]{:S(2)}) collective-permute-start(bf16[32,1152]{1,0:T(8,128)(2,1)S(1)} %get-tuple-element.35), channel_id=1, source_target_pairs={{0,8},{8,0},{16,24},{24,16},{1,9},{9,1},{17,25},{25,17},{2,10},{10... | collective-permute-start | bytes 221192 | tf_op jit(solution)/shard_map/sum_pre/ppermute | solution.py:275
  80.8 7.7 %collective-permute-start.3 = (bf16[32,1152]{1,0:T(8,128)(2,1)S(1)}, bf16[32,1152]{1,0:T(8,128)(2,1)S(1)}, u32[]{:S(2)}, u32[]{:S(2)}) collective-permute-start(bf16[32,1152]{1,0:T(8,128)(2,1)S(1)} %get-tuple-element.36), channel_id=1, source_target_pairs={{0,16},{8,24},{16,0},{24,8},{1,17},{9,25},{17,1},{25,9},{2,18},{10... | collective-permute-start | bytes 221192 | tf_op jit(solution)/shard_map/sum_pre/ppermute | solution.py:275
  88.6 1.9 %collective-permute-start.4 = (bf16[32,1152]{1,0:T(8,128)(2,1)S(1)}, bf16[32,1152]{1,0:T(8,128)(2,1)S(1)}, u32[]{:S(2)}, u32[]{:S(2)}) collective-permute-start(bf16[32,1152]{1,0:T(8,128)(2,1)S(1)} %get-tuple-element.37), channel_id=1, source_target_pairs={{0,24},{8,16},{16,8},{24,0},{1,25},{9,17},{17,9},{25,1},{2,26},{10... | collective-permute-start | bytes 221192 | tf_op jit(solution)/shard_map/sum_pre/ppermute | solution.py:275
  90.5 0.0 collective-permute-done.2
  90.5 0.3 collective-permute-done.3
  90.8 8.7 %collective-permute-done.4 = bf16[32,1152]{1,0:T(8,128)(2,1)S(1)} collective-permute-done((bf16[32,1152]{1,0:T(8,128)(2,1)S(1)}, bf16[32,1152]{1,0:T(8,128)(2,1)S(1)}, u32[]{:S(2)}, u32[]{:S(2)}) %collective-permute-start.4) | collective-permute-done | bytes 73760 | tf_op jit(solution)/shard_map/sum_pre/ppermute | solution.py:275
  99.6 2.0 %collective-permute-start.7 = (bf16[32,1152]{1,0:T(8,128)(2,1)S(1)}, bf16[32,1152]{1,0:T(8,128)(2,1)S(1)}, u32[]{:S(2)}, u32[]{:S(2)}) collective-permute-start(bf16[32,1152]{1,0:T(8,128)(2,1)S(1)} %add_convert_fusion.refs_0_), channel_id=1, source_target_pairs={{0,24},{8,16},{16,8},{24,0},{1,25},{9,17},{17,9},{25,1},{2,26},{10... | collective-permute-start | bytes 221192 | tf_op jit(solution)/shard_map/spread_pre/ppermute | solution.py:275
  101.6 3.8 %collective-permute-start.6 = (bf16[32,1152]{1,0:T(8,128)(2,1)S(1)}, bf16[32,1152]{1,0:T(8,128)(2,1)S(1)}, u32[]{:S(2)}, u32[]{:S(2)}) collective-permute-start(bf16[32,1152]{1,0:T(8,128)(2,1)S(1)} %add_convert_fusion.refs_0_), channel_id=1, source_target_pairs={{0,16},{8,24},{16,0},{24,8},{1,17},{9,25},{17,1},{25,9},{2,18},{10... | collective-permute-start | bytes 221192 | tf_op jit(solution)/shard_map/spread_pre/ppermute | solution.py:275
  105.4 7.4 %collective-permute-start.5 = (bf16[32,1152]{1,0:T(8,128)(2,1)S(1)}, bf16[32,1152]{1,0:T(8,128)(2,1)S(1)}, u32[]{:S(2)}, u32[]{:S(2)}) collective-permute-start(bf16[32,1152]{1,0:T(8,128)(2,1)S(1)} %add_convert_fusion.refs_0_), channel_id=1, source_target_pairs={{0,8},{8,0},{16,24},{24,16},{1,9},{9,1},{17,25},{25,17},{2,10},{10... | collective-permute-start | bytes 221192 | tf_op jit(solution)/shard_map/spread_pre/ppermute | solution.py:275
  112.8 0.0 collective-permute-done.7.refs_3_
  112.8 0.0 collective-permute-done.6.refs_2_
  112.8 2.0 %collective-permute-done.5.refs_1_ = bf16[32,1152]{1,0:T(8,128)(2,1)S(1)} collective-permute-done((bf16[32,1152]{1,0:T(8,128)(2,1)S(1)}, bf16[32,1152]{1,0:T(8,128)(2,1)S(1)}, u32[]{:S(2)}, u32[]{:S(2)}) %collective-permute-start.5) | collective-permute-done | bytes 73760 | tf_op jit(solution)/shard_map/spread_pre/ppermute | solution.py:275
  114.8 4.6 %shard_map.122 = (bf16[2,256,384]{2,1,0:T(8,128)(2,1)S(1)}, bf16[256,512]{1,0:T(8,128)(2,1)S(1)}, f32[256,128]{1,0:T(8,128)S(1)}, bf16[4,8,32,384]{3,2,1,0:T(8,128)(2,1)S(1)}) custom-call(s32[5]{0:T(128)S(1)} %stack.23.me_ref, bf16[32,1152]{1,0:T(8,128)(2,1)S(1)} %add_convert_fusion.refs_0_, bf16[32,1152]{1,0:T(8,128)(2,1)S(1)} %collective-permute-done.5.refs_1_, ...), custom_call_target="tpu_custom_call" | custom-call | tf_op jit(solution)/shard_map/pallas_call | solution.py:256
  119.4 9.2 %collective-permute-start.8 = (bf16[4,8,32,384]{3,2,1,0:T(8,128)(2,1)S(1)}, bf16[4,8,32,384]{3,2,1,0:T(8,128)(2,1)S(1)}, u32[]{:S(2)}, u32[]{:S(2)}) collective-permute-start(bf16[4,8,32,384]{3,2,1,0:T(8,128)(2,1)S(1)} %get-tuple-element.43), channel_id=1, source_target_pairs={{0,32},{32,0},{1,33},{33,1},{2,34},{34,2},{3,35},{35,3},{4,36},{36... | collective-permute-start | bytes 2359304 | tf_op jit(solution)/shard_map/sum_dx/ppermute | solution.py:271
  128.6 1.9 %collective-permute-done.8.refs_3_ = bf16[4,8,32,384]{3,2,1,0:T(8,128)(2,1)S(1)} collective-permute-done((bf16[4,8,32,384]{3,2,1,0:T(8,128)(2,1)S(1)}, bf16[4,8,32,384]{3,2,1,0:T(8,128)(2,1)S(1)}, u32[]{:S(2)}, u32[]{:S(2)}) %collective-permute-start.8) | collective-permute-done | bytes 786464 | tf_op jit(solution)/shard_map/sum_dx/ppermute | solution.py:271
  130.5 2.1 %sum_dx.1 = bf16[4,8,32,384]{3,2,1,0:T(8,128)(2,1)} custom-call(bf16[256,512]{1,0:T(8,128)(2,1)S(1)} %get-tuple-element.41.refs_0_, f32[256,128]{1,0:T(8,128)S(1)} %get-tuple-element.42.refs_1_, bf16[8,192,512]{2,1,0:T(8,128)(2,1)S(1)} %get-tuple-element.40.refs_6_.refs_2_, bf16[4,8,32,384]{3,2,1,0:T(8,128)(2,1)S(1)} %collective-permute-done.8.refs_3_), custom_call_target="tpu_custom_call" | custom-call | tf_op jit(solution)/shard_map/sum_dx/pallas_call | solution.py:256
  132.6 6.5 %all-to-all-start.2 = ((bf16[32,32,384]{2,1,0:T(8,128)(2,1)}), bf16[32,32,384]{2,1,0:T(8,128)(2,1)}, u32[]{:S(2)}, u32[]{:S(2)}) async-start(bf16[32,32,384]{2,1,0:T(8,128)(2,1)} %bitcast.13), calls=%async_computation.2 | async-start | bytes 1572864 | tf_op jit(solution)/shard_map/sum_dx/all_to_all | solution.py:267
  139.2 0.0 copy-start.2
  139.2 1.6 copy-done.2
  140.7 1.8 shard_map.123
  142.5 0.0 copy-start.5
  142.5 1.1 copy-done.5
  143.6 8.5 %all-to-all-done.2 = bf16[32,32,384]{2,1,0:T(8,128)(2,1)} async-done(((bf16[32,32,384]{2,1,0:T(8,128)(2,1)}), bf16[32,32,384]{2,1,0:T(8,128)(2,1)}, u32[]{:S(2)}, u32[]{:S(2)}) %all-to-all-start.2) | async-done | bytes 786464 | tf_op jit(solution)/shard_map/sum_dx/all_to_all | solution.py:267
  152.1 1.3 convert_reduce_fusion
  153.4 0.1 slice.27
  153.4 3.7 %all-to-all-start.3 = ((bf16[16,3,40,384]{3,2,1,0:T(8,128)(2,1)}), bf16[16,3,40,384]{3,2,1,0:T(8,128)(2,1)S(1)}, u32[]{:S(2)}, u32[]{:S(2)}) async-start(bf16[16,3,40,384]{3,2,1,0:T(8,128)(2,1)} %bitcast.42), calls=%async_computation.3 | async-start | bytes 2949120 | tf_op jit(solution)/shard_map/return_grads/all_to_all | solution.py:267
  157.1 9.8 %collective-permute-start.9 = (bf16[32,192]{1,0:T(8,128)(2,1)S(1)}, bf16[32,192]{1,0:T(8,128)(2,1)S(1)}, u32[]{:S(2)}, u32[]{:S(2)}) collective-permute-start(bf16[32,192]{1,0:T(8,128)(2,1)S(1)} %slice.27), channel_id=1, source_target_pairs={{0,64},{64,0},{1,65},{65,1},{2,66},{66,2},{3,67},{67,3},{4,68},{68... | collective-permute-start | bytes 36872 | tf_op jit(solution)/shard_map/ppermute | solution.py:271
  166.9 9.7 %all-to-all-done.3 = bf16[16,3,40,384]{3,2,1,0:T(8,128)(2,1)S(1)} async-done(((bf16[16,3,40,384]{3,2,1,0:T(8,128)(2,1)}), bf16[16,3,40,384]{3,2,1,0:T(8,128)(2,1)S(1)}, u32[]{:S(2)}, u32[]{:S(2)}) %all-to-all-start.3) | async-done | bytes 1474592 | tf_op jit(solution)/shard_map/return_grads/all_to_all | solution.py:267
  176.6 0.1 fusion
  176.7 0.8 copy.21
  177.6 0.8 copy.20
  178.4 0.8 copy.19
  179.3 1.4 collective-permute-done.9.got_any
  180.7 0.8 shard_map.124
  (4 shorter events, 0.1 us)
Async XLA Ops:
  2.3 17.8 %collective-permute-start = (bf16[32,384]{1,0:T(8,128)(2,1)}, bf16[32,384]{1,0:T(8,128)(2,1)S(1)}, u32[]{:S(2)}, u32[]{:S(2)}) collective-permute-start(bf16[32,384]{1,0:T(8,128)(2,1)} %shard_map.119), channel_id=1, source_target_pairs={{0,64},{64,0},{1,65},{65,1},{2,66},{66,2},{3,67},{67,3},{4,68},{68... | collective-permute-start | bytes 73736 | tf_op jit(solution)/shard_map/gather_tokens/ppermute | solution.py:271
  22.3 7.6 %copy-start.6 = (bf16[16,15360]{1,0:T(8,128)(2,1)S(1)}, bf16[16,15360]{1,0:T(8,128)(2,1)}, u32[]{:S(2)}) copy-start(bf16[16,15360]{1,0:T(8,128)(2,1)} %param.13) | copy-start | bytes 1474564
  22.3 7.6 %copy-start.7 = (bf16[16,15360]{1,0:T(8,128)(2,1)S(1)}, bf16[16,15360]{1,0:T(8,128)(2,1)}, u32[]{:S(2)}) copy-start(bf16[16,15360]{1,0:T(8,128)(2,1)} %param.14) | copy-start | bytes 1474564
  22.3 27.4 %all-to-all-start = ((bf16[32,64,384]{2,1,0:T(8,128)(2,1)}), bf16[32,64,384]{2,1,0:T(8,128)(2,1)S(1)}, u32[]{:S(2)}, u32[]{:S(2)}) async-start(bf16[32,64,384]{2,1,0:T(8,128)(2,1)} %tile.2), calls=%async_computation | async-start | bytes 3145728 | tf_op jit(solution)/shard_map/gather_tokens/all_to_all | solution.py:267
  29.8 1.0 copy-start.8
  49.7 4.3 %copy-start.3 = (bf16[32,64,384]{2,1,0:T(8,128)(2,1)}, bf16[32,64,384]{2,1,0:T(8,128)(2,1)S(1)}, u32[]{:S(2)}) copy-start(bf16[32,64,384]{2,1,0:T(8,128)(2,1)S(1)} %all-to-all-done) | copy-start | bytes 4718596
  49.7 20.9 %all-to-all-start.1 = ((bf16[16,3,40,384]{3,2,1,0:T(8,128)(2,1)}), bf16[16,3,40,384]{3,2,1,0:T(8,128)(2,1)}, u32[]{:S(2)}, u32[]{:S(2)}) async-start(bf16[16,3,40,384]{3,2,1,0:T(8,128)(2,1)} %pad_maximum_fusion), calls=%async_computation.1 | async-start | bytes 2949120 | tf_op jit(solution)/shard_map/move_weights/all_to_all | solution.py:267
  54.0 8.1 %collective-permute-start.1 = (bf16[4,8,64,384]{3,2,1,0:T(8,128)(2,1)S(1)}, bf16[4,8,64,384]{3,2,1,0:T(8,128)(2,1)}, u32[]{:S(2)}, u32[]{:S(2)}) collective-permute-start(bf16[4,8,64,384]{3,2,1,0:T(8,128)(2,1)S(1)} %bitcast.40), channel_id=1, source_target_pairs={{0,32},{32,0},{1,33},{33,1},{2,34},{34,2},{3,35},{35,3},{4,36},{36... | collective-permute-start | bytes 4718600 | tf_op jit(solution)/shard_map/gather_tokens/ppermute | solution.py:271
  62.1 1.4 copy-start.4
  67.1 1.3 copy-start
  70.6 1.6 copy-start.1
  76.3 14.2 %collective-permute-start.2 = (bf16[32,1152]{1,0:T(8,128)(2,1)S(1)}, bf16[32,1152]{1,0:T(8,128)(2,1)S(1)}, u32[]{:S(2)}, u32[]{:S(2)}) collective-permute-start(bf16[32,1152]{1,0:T(8,128)(2,1)S(1)} %get-tuple-element.35), channel_id=1, source_target_pairs={{0,8},{8,0},{16,24},{24,16},{1,9},{9,1},{17,25},{25,17},{2,10},{10... | collective-permute-start | bytes 221192 | tf_op jit(solution)/shard_map/sum_pre/ppermute | solution.py:275
  80.8 10.0 %collective-permute-start.3 = (bf16[32,1152]{1,0:T(8,128)(2,1)S(1)}, bf16[32,1152]{1,0:T(8,128)(2,1)S(1)}, u32[]{:S(2)}, u32[]{:S(2)}) collective-permute-start(bf16[32,1152]{1,0:T(8,128)(2,1)S(1)} %get-tuple-element.36), channel_id=1, source_target_pairs={{0,16},{8,24},{16,0},{24,8},{1,17},{9,25},{17,1},{25,9},{2,18},{10... | collective-permute-start | bytes 221192 | tf_op jit(solution)/shard_map/sum_pre/ppermute | solution.py:275
  88.6 11.0 %collective-permute-start.4 = (bf16[32,1152]{1,0:T(8,128)(2,1)S(1)}, bf16[32,1152]{1,0:T(8,128)(2,1)S(1)}, u32[]{:S(2)}, u32[]{:S(2)}) collective-permute-start(bf16[32,1152]{1,0:T(8,128)(2,1)S(1)} %get-tuple-element.37), channel_id=1, source_target_pairs={{0,24},{8,16},{16,8},{24,0},{1,25},{9,17},{17,9},{25,1},{2,26},{10... | collective-permute-start | bytes 221192 | tf_op jit(solution)/shard_map/sum_pre/ppermute | solution.py:275
  99.6 13.2 %collective-permute-start.7 = (bf16[32,1152]{1,0:T(8,128)(2,1)S(1)}, bf16[32,1152]{1,0:T(8,128)(2,1)S(1)}, u32[]{:S(2)}, u32[]{:S(2)}) collective-permute-start(bf16[32,1152]{1,0:T(8,128)(2,1)S(1)} %add_convert_fusion.refs_0_), channel_id=1, source_target_pairs={{0,24},{8,16},{16,8},{24,0},{1,25},{9,17},{17,9},{25,1},{2,26},{10... | collective-permute-start | bytes 221192 | tf_op jit(solution)/shard_map/spread_pre/ppermute | solution.py:275
  101.6 11.2 %collective-permute-start.6 = (bf16[32,1152]{1,0:T(8,128)(2,1)S(1)}, bf16[32,1152]{1,0:T(8,128)(2,1)S(1)}, u32[]{:S(2)}, u32[]{:S(2)}) collective-permute-start(bf16[32,1152]{1,0:T(8,128)(2,1)S(1)} %add_convert_fusion.refs_0_), channel_id=1, source_target_pairs={{0,16},{8,24},{16,0},{24,8},{1,17},{9,25},{17,1},{25,9},{2,18},{10... | collective-permute-start | bytes 221192 | tf_op jit(solution)/shard_map/spread_pre/ppermute | solution.py:275
  105.4 9.4 %collective-permute-start.5 = (bf16[32,1152]{1,0:T(8,128)(2,1)S(1)}, bf16[32,1152]{1,0:T(8,128)(2,1)S(1)}, u32[]{:S(2)}, u32[]{:S(2)}) collective-permute-start(bf16[32,1152]{1,0:T(8,128)(2,1)S(1)} %add_convert_fusion.refs_0_), channel_id=1, source_target_pairs={{0,8},{8,0},{16,24},{24,16},{1,9},{9,1},{17,25},{25,17},{2,10},{10... | collective-permute-start | bytes 221192 | tf_op jit(solution)/shard_map/spread_pre/ppermute | solution.py:275
  119.4 11.1 %collective-permute-start.8 = (bf16[4,8,32,384]{3,2,1,0:T(8,128)(2,1)S(1)}, bf16[4,8,32,384]{3,2,1,0:T(8,128)(2,1)S(1)}, u32[]{:S(2)}, u32[]{:S(2)}) collective-permute-start(bf16[4,8,32,384]{3,2,1,0:T(8,128)(2,1)S(1)} %get-tuple-element.43), channel_id=1, source_target_pairs={{0,32},{32,0},{1,33},{33,1},{2,34},{34,2},{3,35},{35,3},{4,36},{36... | collective-permute-start | bytes 2359304 | tf_op jit(solution)/shard_map/sum_dx/ppermute | solution.py:271
  132.6 19.5 %all-to-all-start.2 = ((bf16[32,32,384]{2,1,0:T(8,128)(2,1)}), bf16[32,32,384]{2,1,0:T(8,128)(2,1)}, u32[]{:S(2)}, u32[]{:S(2)}) async-start(bf16[32,32,384]{2,1,0:T(8,128)(2,1)} %bitcast.13), calls=%async_computation.2 | async-start | bytes 1572864 | tf_op jit(solution)/shard_map/sum_dx/all_to_all | solution.py:267
  139.2 1.6 copy-start.2
  142.5 1.1 copy-start.5
  153.4 23.1 %all-to-all-start.3 = ((bf16[16,3,40,384]{3,2,1,0:T(8,128)(2,1)}), bf16[16,3,40,384]{3,2,1,0:T(8,128)(2,1)S(1)}, u32[]{:S(2)}, u32[]{:S(2)}) async-start(bf16[16,3,40,384]{3,2,1,0:T(8,128)(2,1)} %bitcast.42), calls=%async_computation.3 | async-start | bytes 2949120 | tf_op jit(solution)/shard_map/return_grads/all_to_all | solution.py:267
  157.1 23.5 %collective-permute-start.9 = (bf16[32,192]{1,0:T(8,128)(2,1)S(1)}, bf16[32,192]{1,0:T(8,128)(2,1)S(1)}, u32[]{:S(2)}, u32[]{:S(2)}) collective-permute-start(bf16[32,192]{1,0:T(8,128)(2,1)S(1)} %slice.27), channel_id=1, source_target_pairs={{0,64},{64,0},{1,65},{65,1},{2,66},{66,2},{3,67},{67,3},{4,68},{68... | collective-permute-start | bytes 36872 | tf_op jit(solution)/shard_map/ppermute | solution.py:271

commit v9 on v8

--- a/solution.py
+++ b/solution.py
@@ -84,6 +84,12 @@
     out = out + dot_dims(ids_ref[...].astype(F32).astype(BF16), ones(row == column - IDS_AT), 0, 0)
     out = out + dot_dims(probs_ref[...], ones(row == column - PROBS_AT), 0, 0)
     out_ref[...] = out.astype(BF16)
+
+
+def repeat_kernel(own_ref, other_ref, out_ref):
+    for i in range(NX * NG):
+        out_ref[i, :SHARD] = own_ref[...]
+        out_ref[i, SHARD:] = other_ref[...]
 
 
 def select_kernel(me_ref, x0_ref, x1_ref, xs_ref, ds_ref, gate_ref, slot_ref, pick_ref):
@@ -283,8 +289,8 @@
     (xin,) = call(prepare_kernel, [((SHARD, COLS), BF16)], (stash, small[0], grad_out, small[1], small[2]),
                   grant=MOST)
     with jax.named_scope("gather_tokens"):
-        xin = jnp.concatenate([xin, swap(xin, "zh")])
-        x0 = exchange(jnp.tile(xin, (NX * NG, 1)), ("x",) + GROUP).reshape(NX, NG, 2 * SHARD, COLS)
+        (xin,) = call(repeat_kernel, [((NX * NG, 2 * SHARD, COLS), BF16)], (xin, swap(xin, "zh")), grant=MOST)
+        x0 = exchange(xin, ("x",) + GROUP).reshape(NX, NG, 2 * SHARD, COLS)
         x1 = swap(x0, "core")
     with jax.named_scope("move_weights"):
         tiles = [w.reshape(EXPERTS, 1, Q, 4 * FSH) for w in (w_gate, w_up, w_down)]

time: 184 us -> 185 us (level)
  Pallas kernels: 18.7 us -> 20.8 us
    pallas_call x7 -> x8, Pallas kernels: 18.7 us -> 20.8 us  [call(): pl.pallas_call(kernel, out_shape=[jax.ShapeDtypeStruct(shape, dtype) for...]
    unnamed x24 -> x26, local copies, waits for them, and re-layouts: 10.6 us -> 11.2 us
where the time goes in v9:
time: 185 us; the launch traced here: 182 us
  starting transfers between devices  89.6 us (48%)
  waiting for transfers between devices  56.5 us (31%)
  Pallas kernels  20.8 us (11%)
  local copies, waits for them, and re-layouts  11.5 us (6%)
  other arithmetic  2.62 us (1%)
    ppermute x4, starting transfers between devices, swap(): return lax.ppermute(value, axis, [(0, 1), (1, 0)])  40.1 us
    all_to_all x4, waiting for transfers between devices, exchange(): return lax.all_to_all(value, axis, split_axis=0, concat_axis=0, tiled=True)  37.7 us
    ppermute x6, starting transfers between devices, flip(): lax.ppermute(value, axis, [(i, i ^ bit) for i in range(lax.axis_size(axis...  27.3 us
    all_to_all x4, starting transfers between devices, exchange(): return lax.all_to_all(value, axis, split_axis=0, concat_axis=0, tiled=True)  22.1 us
    pallas_call x8, Pallas kernels, call(): pl.pallas_call(kernel, out_shape=[jax.ShapeDtypeStruct(shape, dtype) for...  20.8 us
    unnamed x26, local copies, waits for them, and re-layouts  11.2 us
    ppermute x6, waiting for transfers between devices, flip(): lax.ppermute(value, axis, [(i, i ^ bit) for i in range(lax.axis_size(axis...  11.1 us
    ppermute x4, waiting for transfers between devices, swap(): return lax.ppermute(value, axis, [(0, 1), (1, 0)])  7.78 us
  transfers between devices with their start and end apart: 14, of which 11 were waited for; matrix products, arithmetic and copies ran while one was open for 2% of the time, Pallas kernels for 3%

profile of v9, /device:TPU:1, one launch (start us, length us, event | category | flops | bytes accessed | tf_op | source)
XLA Modules:
  0.0 181.9 jit_solution(6776158494961521352)
XLA Ops:
  0.6 1.7 shard_map.119.own_ref
  2.3 16.3 %collective-permute-start = (bf16[32,384]{1,0:T(8,128)(2,1)}, bf16[32,384]{1,0:T(8,128)(2,1)S(1)}, u32[]{:S(2)}, u32[]{:S(2)}) collective-permute-start(bf16[32,384]{1,0:T(8,128)(2,1)} %shard_map.119.own_ref), channel_id=1, source_target_pairs={{0,64},{64,0},{1,65},{65,1},{2,66},{66,2},{3,67},{67,3},{4,68},{68... | collective-permute-start | bytes 73736 | tf_op jit(solution)/shard_map/gather_tokens/ppermute | solution.py:277
  18.6 1.5 collective-permute-done.other_ref
  20.1 0.0 copy-start.9
  20.1 0.6 copy-done.9
  20.7 2.1 %gather_tokens.1 = bf16[32,64,384]{2,1,0:T(8,128)(2,1)} custom-call(bf16[32,384]{1,0:T(8,128)(2,1)} %shard_map.119.own_ref, bf16[32,384]{1,0:T(8,128)(2,1)} %copy-done.9), custom_call_target="tpu_custom_call" | custom-call | tf_op jit(solution)/shard_map/gather_tokens/pallas_call | solution.py:262
  22.8 0.0 copy-start.6
  22.8 0.0 copy-start.7
  22.8 7.5 %all-to-all-start = ((bf16[32,64,384]{2,1,0:T(8,128)(2,1)}), bf16[32,64,384]{2,1,0:T(8,128)(2,1)S(1)}, u32[]{:S(2)}, u32[]{:S(2)}) async-start(bf16[32,64,384]{2,1,0:T(8,128)(2,1)} %gather_tokens.1), calls=%async_computation | async-start | bytes 3145728 | tf_op jit(solution)/shard_map/gather_tokens/all_to_all | solution.py:273
  30.3 0.0 copy-start.8
  30.4 0.0 copy-done.6
  30.4 0.1 copy.16
  30.4 0.0 copy-done.7
  30.4 0.1 copy.17
  30.5 0.9 copy-done.8
  31.4 0.1 copy.18
  31.4 1.3 pad_maximum_fusion
  32.8 17.5 %all-to-all-done = bf16[32,64,384]{2,1,0:T(8,128)(2,1)S(1)} async-done(((bf16[32,64,384]{2,1,0:T(8,128)(2,1)}), bf16[32,64,384]{2,1,0:T(8,128)(2,1)S(1)}, u32[]{:S(2)}, u32[]{:S(2)}) %all-to-all-start) | async-done | bytes 1572896 | tf_op jit(solution)/shard_map/gather_tokens/all_to_all | solution.py:273
  50.2 4.3 %all-to-all-start.1 = ((bf16[16,3,40,384]{3,2,1,0:T(8,128)(2,1)}), bf16[16,3,40,384]{3,2,1,0:T(8,128)(2,1)}, u32[]{:S(2)}, u32[]{:S(2)}) async-start(bf16[16,3,40,384]{3,2,1,0:T(8,128)(2,1)} %pad_maximum_fusion), calls=%async_computation.1 | async-start | bytes 2949120 | tf_op jit(solution)/shard_map/move_weights/all_to_all | solution.py:273
  54.6 0.0 copy-done.3
  54.6 4.9 %collective-permute-start.1 = (bf16[4,8,64,384]{3,2,1,0:T(8,128)(2,1)S(1)}, bf16[4,8,64,384]{3,2,1,0:T(8,128)(2,1)}, u32[]{:S(2)}, u32[]{:S(2)}) collective-permute-start(bf16[4,8,64,384]{3,2,1,0:T(8,128)(2,1)S(1)} %bitcast.40), channel_id=1, source_target_pairs={{0,32},{32,0},{1,33},{33,1},{2,34},{34,2},{3,35},{35,3},{4,36},{36... | collective-permute-start | bytes 4718600 | tf_op jit(solution)/shard_map/gather_tokens/ppermute | solution.py:277
  59.5 0.1 stack.23.me_ref
  59.6 3.1 %collective-permute-done.1.x1_ref = bf16[4,8,64,384]{3,2,1,0:T(8,128)(2,1)} collective-permute-done((bf16[4,8,64,384]{3,2,1,0:T(8,128)(2,1)S(1)}, bf16[4,8,64,384]{3,2,1,0:T(8,128)(2,1)}, u32[]{:S(2)}, u32[]{:S(2)}) %collective-permute-start.1) | collective-permute-done | bytes 1572896 | tf_op jit(solution)/shard_map/gather_tokens/ppermute | solution.py:277
  62.7 1.4 copy-done.4
  64.1 3.6 %shard_map.120 = (bf16[8,2,256,192]{3,2,1,0:T(8,128)(2,1)S(1)}, bf16[8,2,256,192]{3,2,1,0:T(8,128)(2,1)S(1)}, f32[2,256,128]{2,1,0:T(8,128)S(1)}, f32[512,128]{1,0:T(8,128)S(1)}) custom-call(s32[5]{0:T(128)S(1)} %stack.23.me_ref, bf16[4,8,64,384]{3,2,1,0:T(8,128)(2,1)S(1)} %bitcast.41, bf16[4,8,64,384]{3,2,1,0:T(8,128)(2,1)} %collective-permute-done.1.x1_ref), custom_call_target="tpu_custom_call" | custom-call | tf_op jit(solution)/shard_map/pallas_call | solution.py:262
  67.7 0.0 copy-start
  67.7 1.3 copy-done
  69.1 2.0 %all-to-all-done.1 = bf16[16,3,40,384]{3,2,1,0:T(8,128)(2,1)} async-done(((bf16[16,3,40,384]{3,2,1,0:T(8,128)(2,1)}), bf16[16,3,40,384]{3,2,1,0:T(8,128)(2,1)}, u32[]{:S(2)}, u32[]{:S(2)}) %all-to-all-start.1) | async-done | bytes 1474592 | tf_op jit(solution)/shard_map/move_weights/all_to_all | solution.py:273
  71.1 1.6 copy-done.1
  72.7 4.1 %shard_map.121 = (f32[32,1152]{1,0:T(8,128)S(1)}, bf16[32,1152]{1,0:T(8,128)(2,1)S(1)}, bf16[32,1152]{1,0:T(8,128)(2,1)S(1)}, bf16[32,1152]{1,0:T(8,128)(2,1)S(1)}, bf16[8,192,512]{2,1,0:T(8,128)(2,1)S(1)}) custom-call(s32[5]{0:T(128)S(1)} %stack.23.me_ref, bf16[8,240,384]{2,1,0:T(8,128)(2,1)} %bitcast.12.refs_0_, ...), custom_call_target="tpu_custom_call" | custom-call | tf_op jit(solution)/shard_map/pallas_call | solution.py:262
  76.8 4.6 %collective-permute-start.2 = (bf16[32,1152]{1,0:T(8,128)(2,1)S(1)}, bf16[32,1152]{1,0:T(8,128)(2,1)S(1)}, u32[]{:S(2)}, u32[]{:S(2)}) collective-permute-start(bf16[32,1152]{1,0:T(8,128)(2,1)S(1)} %get-tuple-element.35), channel_id=1, source_target_pairs={{0,8},{8,0},{16,24},{24,16},{1,9},{9,1},{17,25},{25,17},{2,10},{10... | collective-permute-start | bytes 221192 | tf_op jit(solution)/shard_map/sum_pre/ppermute | solution.py:281
  81.4 7.6 %collective-permute-start.3 = (bf16[32,1152]{1,0:T(8,128)(2,1)S(1)}, bf16[32,1152]{1,0:T(8,128)(2,1)S(1)}, u32[]{:S(2)}, u32[]{:S(2)}) collective-permute-start(bf16[32,1152]{1,0:T(8,128)(2,1)S(1)} %get-tuple-element.36), channel_id=1, source_target_pairs={{0,16},{8,24},{16,0},{24,8},{1,17},{9,25},{17,1},{25,9},{2,18},{10... | collective-permute-start | bytes 221192 | tf_op jit(solution)/shard_map/sum_pre/ppermute | solution.py:281
  89.0 1.9 %collective-permute-start.4 = (bf16[32,1152]{1,0:T(8,128)(2,1)S(1)}, bf16[32,1152]{1,0:T(8,128)(2,1)S(1)}, u32[]{:S(2)}, u32[]{:S(2)}) collective-permute-start(bf16[32,1152]{1,0:T(8,128)(2,1)S(1)} %get-tuple-element.37), channel_id=1, source_target_pairs={{0,24},{8,16},{16,8},{24,0},{1,25},{9,17},{17,9},{25,1},{2,26},{10... | collective-permute-start | bytes 221192 | tf_op jit(solution)/shard_map/sum_pre/ppermute | solution.py:281
  91.0 0.0 collective-permute-done.2
  91.0 0.3 collective-permute-done.3
  91.3 8.8 %collective-permute-done.4 = bf16[32,1152]{1,0:T(8,128)(2,1)S(1)} collective-permute-done((bf16[32,1152]{1,0:T(8,128)(2,1)S(1)}, bf16[32,1152]{1,0:T(8,128)(2,1)S(1)}, u32[]{:S(2)}, u32[]{:S(2)}) %collective-permute-start.4) | collective-permute-done | bytes 73760 | tf_op jit(solution)/shard_map/sum_pre/ppermute | solution.py:281
  100.1 1.9 %collective-permute-start.7 = (bf16[32,1152]{1,0:T(8,128)(2,1)S(1)}, bf16[32,1152]{1,0:T(8,128)(2,1)S(1)}, u32[]{:S(2)}, u32[]{:S(2)}) collective-permute-start(bf16[32,1152]{1,0:T(8,128)(2,1)S(1)} %add_convert_fusion.refs_0_), channel_id=1, source_target_pairs={{0,24},{8,16},{16,8},{24,0},{1,25},{9,17},{17,9},{25,1},{2,26},{10... | collective-permute-start | bytes 221192 | tf_op jit(solution)/shard_map/spread_pre/ppermute | solution.py:281
  102.0 3.9 %collective-permute-start.6 = (bf16[32,1152]{1,0:T(8,128)(2,1)S(1)}, bf16[32,1152]{1,0:T(8,128)(2,1)S(1)}, u32[]{:S(2)}, u32[]{:S(2)}) collective-permute-start(bf16[32,1152]{1,0:T(8,128)(2,1)S(1)} %add_convert_fusion.refs_0_), channel_id=1, source_target_pairs={{0,16},{8,24},{16,0},{24,8},{1,17},{9,25},{17,1},{25,9},{2,18},{10... | collective-permute-start | bytes 221192 | tf_op jit(solution)/shard_map/spread_pre/ppermute | solution.py:281
  105.9 7.4 %collective-permute-start.5 = (bf16[32,1152]{1,0:T(8,128)(2,1)S(1)}, bf16[32,1152]{1,0:T(8,128)(2,1)S(1)}, u32[]{:S(2)}, u32[]{:S(2)}) collective-permute-start(bf16[32,1152]{1,0:T(8,128)(2,1)S(1)} %add_convert_fusion.refs_0_), channel_id=1, source_target_pairs={{0,8},{8,0},{16,24},{24,16},{1,9},{9,1},{17,25},{25,17},{2,10},{10... | collective-permute-start | bytes 221192 | tf_op jit(solution)/shard_map/spread_pre/ppermute | solution.py:281
  113.3 0.0 collective-permute-done.7.refs_3_
  113.3 0.0 collective-permute-done.6.refs_2_
  113.3 2.0 %collective-permute-done.5.refs_1_ = bf16[32,1152]{1,0:T(8,128)(2,1)S(1)} collective-permute-done((bf16[32,1152]{1,0:T(8,128)(2,1)S(1)}, bf16[32,1152]{1,0:T(8,128)(2,1)S(1)}, u32[]{:S(2)}, u32[]{:S(2)}) %collective-permute-start.5) | collective-permute-done | bytes 73760 | tf_op jit(solution)/shard_map/spread_pre/ppermute | solution.py:281
  115.3 4.6 %shard_map.122 = (bf16[2,256,384]{2,1,0:T(8,128)(2,1)S(1)}, bf16[256,512]{1,0:T(8,128)(2,1)S(1)}, f32[256,128]{1,0:T(8,128)S(1)}, bf16[4,8,32,384]{3,2,1,0:T(8,128)(2,1)S(1)}) custom-call(s32[5]{0:T(128)S(1)} %stack.23.me_ref, bf16[32,1152]{1,0:T(8,128)(2,1)S(1)} %add_convert_fusion.refs_0_, bf16[32,1152]{1,0:T(8,128)(2,1)S(1)} %collective-permute-done.5.refs_1_, ...), custom_call_target="tpu_custom_call" | custom-call | tf_op jit(solution)/shard_map/pallas_call | solution.py:262
  119.9 9.2 %collective-permute-start.8 = (bf16[4,8,32,384]{3,2,1,0:T(8,128)(2,1)S(1)}, bf16[4,8,32,384]{3,2,1,0:T(8,128)(2,1)S(1)}, u32[]{:S(2)}, u32[]{:S(2)}) collective-permute-start(bf16[4,8,32,384]{3,2,1,0:T(8,128)(2,1)S(1)} %get-tuple-element.43), channel_id=1, source_target_pairs={{0,32},{32,0},{1,33},{33,1},{2,34},{34,2},{3,35},{35,3},{4,36},{36... | collective-permute-start | bytes 2359304 | tf_op jit(solution)/shard_map/sum_dx/ppermute | solution.py:277
  129.1 1.9 %collective-permute-done.8.refs_3_ = bf16[4,8,32,384]{3,2,1,0:T(8,128)(2,1)S(1)} collective-permute-done((bf16[4,8,32,384]{3,2,1,0:T(8,128)(2,1)S(1)}, bf16[4,8,32,384]{3,2,1,0:T(8,128)(2,1)S(1)}, u32[]{:S(2)}, u32[]{:S(2)}) %collective-permute-start.8) | collective-permute-done | bytes 786464 | tf_op jit(solution)/shard_map/sum_dx/ppermute | solution.py:277
  131.0 2.1 %sum_dx.1 = bf16[4,8,32,384]{3,2,1,0:T(8,128)(2,1)} custom-call(bf16[256,512]{1,0:T(8,128)(2,1)S(1)} %get-tuple-element.41.refs_0_, f32[256,128]{1,0:T(8,128)S(1)} %get-tuple-element.42.refs_1_, bf16[8,192,512]{2,1,0:T(8,128)(2,1)S(1)} %get-tuple-element.40.refs_6_.refs_2_, bf16[4,8,32,384]{3,2,1,0:T(8,128)(2,1)S(1)} %collective-permute-done.8.refs_3_), custom_call_target="tpu_custom_call" | custom-call | tf_op jit(solution)/shard_map/sum_dx/pallas_call | solution.py:262
  133.1 6.6 %all-to-all-start.2 = ((bf16[32,32,384]{2,1,0:T(8,128)(2,1)}), bf16[32,32,384]{2,1,0:T(8,128)(2,1)}, u32[]{:S(2)}, u32[]{:S(2)}) async-start(bf16[32,32,384]{2,1,0:T(8,128)(2,1)} %bitcast.13), calls=%async_computation.2 | async-start | bytes 1572864 | tf_op jit(solution)/shard_map/sum_dx/all_to_all | solution.py:273
  139.7 0.0 copy-start.2
  139.7 1.6 copy-done.2
  141.3 1.7 shard_map.123
  143.0 0.0 copy-start.5
  143.0 1.1 copy-done.5
  144.2 8.5 %all-to-all-done.2 = bf16[32,32,384]{2,1,0:T(8,128)(2,1)} async-done(((bf16[32,32,384]{2,1,0:T(8,128)(2,1)}), bf16[32,32,384]{2,1,0:T(8,128)(2,1)}, u32[]{:S(2)}, u32[]{:S(2)}) %all-to-all-start.2) | async-done | bytes 786464 | tf_op jit(solution)/shard_map/sum_dx/all_to_all | solution.py:273
  152.6 1.3 convert_reduce_fusion
  153.9 0.1 slice.27
  154.0 3.7 %all-to-all-start.3 = ((bf16[16,3,40,384]{3,2,1,0:T(8,128)(2,1)}), bf16[16,3,40,384]{3,2,1,0:T(8,128)(2,1)S(1)}, u32[]{:S(2)}, u32[]{:S(2)}) async-start(bf16[16,3,40,384]{3,2,1,0:T(8,128)(2,1)} %bitcast.42), calls=%async_computation.3 | async-start | bytes 2949120 | tf_op jit(solution)/shard_map/return_grads/all_to_all | solution.py:273
  157.7 9.7 %collective-permute-start.9 = (bf16[32,192]{1,0:T(8,128)(2,1)S(1)}, bf16[32,192]{1,0:T(8,128)(2,1)S(1)}, u32[]{:S(2)}, u32[]{:S(2)}) collective-permute-start(bf16[32,192]{1,0:T(8,128)(2,1)S(1)} %slice.27), channel_id=1, source_target_pairs={{0,64},{64,0},{1,65},{65,1},{2,66},{66,2},{3,67},{67,3},{4,68},{68... | collective-permute-start | bytes 36872 | tf_op jit(solution)/shard_map/ppermute | solution.py:277
  167.4 9.7 %all-to-all-done.3 = bf16[16,3,40,384]{3,2,1,0:T(8,128)(2,1)S(1)} async-done(((bf16[16,3,40,384]{3,2,1,0:T(8,128)(2,1)}), bf16[16,3,40,384]{3,2,1,0:T(8,128)(2,1)S(1)}, u32[]{:S(2)}, u32[]{:S(2)}) %all-to-all-start.3) | async-done | bytes 1474592 | tf_op jit(solution)/shard_map/return_grads/all_to_all | solution.py:273
  177.1 0.2 fusion
  177.3 0.8 copy.21
  178.1 0.8 copy.20
  179.0 0.8 copy.19
  179.8 1.3 collective-permute-done.9.got_any
  181.1 0.8 shard_map.124
  (5 shorter events, 0.1 us)
Async XLA Ops:
  2.3 17.8 %collective-permute-start = (bf16[32,384]{1,0:T(8,128)(2,1)}, bf16[32,384]{1,0:T(8,128)(2,1)S(1)}, u32[]{:S(2)}, u32[]{:S(2)}) collective-permute-start(bf16[32,384]{1,0:T(8,128)(2,1)} %shard_map.119.own_ref), channel_id=1, source_target_pairs={{0,64},{64,0},{1,65},{65,1},{2,66},{66,2},{3,67},{67,3},{4,68},{68... | collective-permute-start | bytes 73736 | tf_op jit(solution)/shard_map/gather_tokens/ppermute | solution.py:277
  20.1 0.6 copy-start.9
  22.8 7.6 %copy-start.6 = (bf16[16,15360]{1,0:T(8,128)(2,1)S(1)}, bf16[16,15360]{1,0:T(8,128)(2,1)}, u32[]{:S(2)}) copy-start(bf16[16,15360]{1,0:T(8,128)(2,1)} %param.13) | copy-start | bytes 1474564
  22.8 7.6 %copy-start.7 = (bf16[16,15360]{1,0:T(8,128)(2,1)S(1)}, bf16[16,15360]{1,0:T(8,128)(2,1)}, u32[]{:S(2)}) copy-start(bf16[16,15360]{1,0:T(8,128)(2,1)} %param.14) | copy-start | bytes 1474564
  22.8 27.4 %all-to-all-start = ((bf16[32,64,384]{2,1,0:T(8,128)(2,1)}), bf16[32,64,384]{2,1,0:T(8,128)(2,1)S(1)}, u32[]{:S(2)}, u32[]{:S(2)}) async-start(bf16[32,64,384]{2,1,0:T(8,128)(2,1)} %gather_tokens.1), calls=%async_computation | async-start | bytes 3145728 | tf_op jit(solution)/shard_map/gather_tokens/all_to_all | solution.py:273
  30.3 1.0 copy-start.8
  50.2 4.3 %copy-start.3 = (bf16[32,64,384]{2,1,0:T(8,128)(2,1)}, bf16[32,64,384]{2,1,0:T(8,128)(2,1)S(1)}, u32[]{:S(2)}) copy-start(bf16[32,64,384]{2,1,0:T(8,128)(2,1)S(1)} %all-to-all-done) | copy-start | bytes 4718596
  50.2 20.9 %all-to-all-start.1 = ((bf16[16,3,40,384]{3,2,1,0:T(8,128)(2,1)}), bf16[16,3,40,384]{3,2,1,0:T(8,128)(2,1)}, u32[]{:S(2)}, u32[]{:S(2)}) async-start(bf16[16,3,40,384]{3,2,1,0:T(8,128)(2,1)} %pad_maximum_fusion), calls=%async_computation.1 | async-start | bytes 2949120 | tf_op jit(solution)/shard_map/move_weights/all_to_all | solution.py:273
  54.6 8.1 %collective-permute-start.1 = (bf16[4,8,64,384]{3,2,1,0:T(8,128)(2,1)S(1)}, bf16[4,8,64,384]{3,2,1,0:T(8,128)(2,1)}, u32[]{:S(2)}, u32[]{:S(2)}) collective-permute-start(bf16[4,8,64,384]{3,2,1,0:T(8,128)(2,1)S(1)} %bitcast.40), channel_id=1, source_target_pairs={{0,32},{32,0},{1,33},{33,1},{2,34},{34,2},{3,35},{35,3},{4,36},{36... | collective-permute-start | bytes 4718600 | tf_op jit(solution)/shard_map/gather_tokens/ppermute | solution.py:277
  62.7 1.4 copy-start.4
  67.7 1.4 copy-start
  71.1 1.6 copy-start.1
  76.8 14.2 %collective-permute-start.2 = (bf16[32,1152]{1,0:T(8,128)(2,1)S(1)}, bf16[32,1152]{1,0:T(8,128)(2,1)S(1)}, u32[]{:S(2)}, u32[]{:S(2)}) collective-permute-start(bf16[32,1152]{1,0:T(8,128)(2,1)S(1)} %get-tuple-element.35), channel_id=1, source_target_pairs={{0,8},{8,0},{16,24},{24,16},{1,9},{9,1},{17,25},{25,17},{2,10},{10... | collective-permute-start | bytes 221192 | tf_op jit(solution)/shard_map/sum_pre/ppermute | solution.py:281
  81.4 9.9 %collective-permute-start.3 = (bf16[32,1152]{1,0:T(8,128)(2,1)S(1)}, bf16[32,1152]{1,0:T(8,128)(2,1)S(1)}, u32[]{:S(2)}, u32[]{:S(2)}) collective-permute-start(bf16[32,1152]{1,0:T(8,128)(2,1)S(1)} %get-tuple-element.36), channel_id=1, source_target_pairs={{0,16},{8,24},{16,0},{24,8},{1,17},{9,25},{17,1},{25,9},{2,18},{10... | collective-permute-start | bytes 221192 | tf_op jit(solution)/shard_map/sum_pre/ppermute | solution.py:281
  89.0 11.0 %collective-permute-start.4 = (bf16[32,1152]{1,0:T(8,128)(2,1)S(1)}, bf16[32,1152]{1,0:T(8,128)(2,1)S(1)}, u32[]{:S(2)}, u32[]{:S(2)}) collective-permute-start(bf16[32,1152]{1,0:T(8,128)(2,1)S(1)} %get-tuple-element.37), channel_id=1, source_target_pairs={{0,24},{8,16},{16,8},{24,0},{1,25},{9,17},{17,9},{25,1},{2,26},{10... | collective-permute-start | bytes 221192 | tf_op jit(solution)/shard_map/sum_pre/ppermute | solution.py:281
  100.1 13.2 %collective-permute-start.7 = (bf16[32,1152]{1,0:T(8,128)(2,1)S(1)}, bf16[32,1152]{1,0:T(8,128)(2,1)S(1)}, u32[]{:S(2)}, u32[]{:S(2)}) collective-permute-start(bf16[32,1152]{1,0:T(8,128)(2,1)S(1)} %add_convert_fusion.refs_0_), channel_id=1, source_target_pairs={{0,24},{8,16},{16,8},{24,0},{1,25},{9,17},{17,9},{25,1},{2,26},{10... | collective-permute-start | bytes 221192 | tf_op jit(solution)/shard_map/spread_pre/ppermute | solution.py:281
  102.0 11.3 %collective-permute-start.6 = (bf16[32,1152]{1,0:T(8,128)(2,1)S(1)}, bf16[32,1152]{1,0:T(8,128)(2,1)S(1)}, u32[]{:S(2)}, u32[]{:S(2)}) collective-permute-start(bf16[32,1152]{1,0:T(8,128)(2,1)S(1)} %add_convert_fusion.refs_0_), channel_id=1, source_target_pairs={{0,16},{8,24},{16,0},{24,8},{1,17},{9,25},{17,1},{25,9},{2,18},{10... | collective-permute-start | bytes 221192 | tf_op jit(solution)/shard_map/spread_pre/ppermute | solution.py:281
  105.9 9.4 %collective-permute-start.5 = (bf16[32,1152]{1,0:T(8,128)(2,1)S(1)}, bf16[32,1152]{1,0:T(8,128)(2,1)S(1)}, u32[]{:S(2)}, u32[]{:S(2)}) collective-permute-start(bf16[32,1152]{1,0:T(8,128)(2,1)S(1)} %add_convert_fusion.refs_0_), channel_id=1, source_target_pairs={{0,8},{8,0},{16,24},{24,16},{1,9},{9,1},{17,25},{25,17},{2,10},{10... | collective-permute-start | bytes 221192 | tf_op jit(solution)/shard_map/spread_pre/ppermute | solution.py:281
  119.9 11.1 %collective-permute-start.8 = (bf16[4,8,32,384]{3,2,1,0:T(8,128)(2,1)S(1)}, bf16[4,8,32,384]{3,2,1,0:T(8,128)(2,1)S(1)}, u32[]{:S(2)}, u32[]{:S(2)}) collective-permute-start(bf16[4,8,32,384]{3,2,1,0:T(8,128)(2,1)S(1)} %get-tuple-element.43), channel_id=1, source_target_pairs={{0,32},{32,0},{1,33},{33,1},{2,34},{34,2},{3,35},{35,3},{4,36},{36... | collective-permute-start | bytes 2359304 | tf_op jit(solution)/shard_map/sum_dx/ppermute | solution.py:277
  133.1 19.5 %all-to-all-start.2 = ((bf16[32,32,384]{2,1,0:T(8,128)(2,1)}), bf16[32,32,384]{2,1,0:T(8,128)(2,1)}, u32[]{:S(2)}, u32[]{:S(2)}) async-start(bf16[32,32,384]{2,1,0:T(8,128)(2,1)} %bitcast.13), calls=%async_computation.2 | async-start | bytes 1572864 | tf_op jit(solution)/shard_map/sum_dx/all_to_all | solution.py:273
  139.7 1.6 copy-start.2
  143.0 1.1 copy-start.5
  154.0 23.1 %all-to-all-start.3 = ((bf16[16,3,40,384]{3,2,1,0:T(8,128)(2,1)}), bf16[16,3,40,384]{3,2,1,0:T(8,128)(2,1)S(1)}, u32[]{:S(2)}, u32[]{:S(2)}) async-start(bf16[16,3,40,384]{3,2,1,0:T(8,128)(2,1)} %bitcast.42), calls=%async_computation.3 | async-start | bytes 2949120 | tf_op jit(solution)/shard_map/return_grads/all_to_all | solution.py:273
  157.7 23.5 %collective-permute-start.9 = (bf16[32,192]{1,0:T(8,128)(2,1)S(1)}, bf16[32,192]{1,0:T(8,128)(2,1)S(1)}, u32[]{:S(2)}, u32[]{:S(2)}) collective-permute-start(bf16[32,192]{1,0:T(8,128)(2,1)S(1)} %slice.27), channel_id=1, source_target_pairs={{0,64},{64,0},{1,65},{65,1},{2,66},{66,2},{3,67},{67,3},{4,68},{68... | collective-permute-start | bytes 36872 | tf_op jit(solution)/shard_map/ppermute | solution.py:277
